TPU v7x, 256 devices: a whole 4x4x8 slice. The times are simulated.
256 devices in a mesh: box: 32 (over y, z), depth: 8 (over x, core).
Axes of the slice: x: 4, y: 4, z: 8, core: 2. Of those that a mesh axis runs over, the one named last changes fastest.
Arguments:
- state: float32 [5, 64, 256, 384], P(None, 'depth', 'box')
- velocity: float32 [3, 64, 256, 384], P(None, 'depth', 'box'), may hold values from -6 to 6
- bins: int32 [64, 256, 384], P('depth', 'box'), may hold values from 0 to 4095, as said below
Outputs:
- new_state: float32 [5, 64, 256, 384], P(None, 'depth', 'box')
- potential: float32 [64, 256, 384], P('depth', 'box')
- base_profile: float32 [5, 4096], replicated
Inputs may be any that keep to these rules, and one draw needn't show every extreme that they name: `bins`: bins grow with the squared distance of a cell from a centre cell inside the grid, which has bin 0.
All inputs are finite; a program needn't handle non-finite values. Where the computation divides by a largest or mean magnitude, that divisor is 1e-20 or more.
Results may differ from a plain program's by a relative error of at most 0.0003.
Values sent between devices are 32-bit elements; how exact they have to be, the bound alone decides.
No kernel may reach another device: no remote copies, remote signals or barrier semaphores. Data moves between devices by JAX's collectives and lax.ppermute only.
A program may use at most 64 MiB of HBM per device.

v0:
```python
import math

import jax
import jax.numpy as jnp
from jax import lax
from jax.sharding import PartitionSpec as P

NBINS = 4096
ITERS = 4


COURANT = 0.8
OMEGA_RELAX = 0.8
KAPPA_SHIFT = 0.1
RHS_WEIGHTS = (1.0, 0.5, -0.5, 0.25, 0.75)


def extended_2(cells, sides, width):
    for axis, dim in sides:
        count = lax.axis_size(axis)
        ends = count - 1
        head = lax.slice_in_dim(cells, 0, width, axis=dim)
        tail = lax.slice_in_dim(cells, cells.shape[dim] - width, cells.shape[dim], axis=dim)
        cells = jnp.concatenate(
            [
                lax.ppermute(tail, axis, [(i, (i + 1) % count) for i in range(ends)]),
                cells,
                lax.ppermute(head, axis, [((i + 1) % count, i) for i in range(ends)]),
            ],
            axis=dim,
        )
    return cells


def upwind(padded, velocity, time_step):
    center = padded[:, 1:-1, 1:-1, 1:-1]
    lowers = (padded[:, :-2, 1:-1, 1:-1], padded[:, 1:-1, :-2, 1:-1], padded[:, 1:-1, 1:-1, :-2])
    uppers = (padded[:, 2:, 1:-1, 1:-1], padded[:, 1:-1, 2:, 1:-1], padded[:, 1:-1, 1:-1, 2:])
    change = jnp.zeros_like(center)
    for axis_index in range(3):
        comp_speed = velocity[axis_index][None]
        change = (
            change
            + jnp.maximum(comp_speed, 0.0) * (center - lowers[axis_index])
            + jnp.minimum(comp_speed, 0.0) * (uppers[axis_index] - center)
        )
    return center - time_step * change


def relax(padded, source):
    center = padded[1:-1, 1:-1, 1:-1]
    beside = padded[2:, 1:-1, 1:-1] + padded[:-2, 1:-1, 1:-1]
    beside = beside + padded[1:-1, 2:, 1:-1] + padded[1:-1, :-2, 1:-1]
    beside = beside + padded[1:-1, 1:-1, 2:] + padded[1:-1, 1:-1, :-2]
    diagonal = 6.0 + KAPPA_SHIFT
    return center + OMEGA_RELAX * (source - (diagonal * center - beside)) / diagonal


def pad_depth(field):
    return jnp.pad(field, ((0, 0), (0, 0), (1, 1)))


def split_three(values):
    upper = lax.optimization_barrier(values.astype(jnp.bfloat16))
    rest = values - upper.astype(jnp.float32)
    middle = lax.optimization_barrier(rest.astype(jnp.bfloat16))
    lower = (rest - middle.astype(jnp.float32)).astype(jnp.bfloat16)
    return jnp.concatenate([upper, middle, lower], axis=0)


def block_size(total):
    return math.gcd(total, 2048)


def one_hot(bin_block):
    return (bin_block[:, None] == jnp.arange(NBINS, dtype=jnp.int32)[None, :]).astype(jnp.bfloat16)


def bin_sums(fields, flat_bins):
    count_fields = fields.shape[0]
    total = flat_bins.shape[0]
    blk = block_size(total)
    blocks = total // blk
    pieces = split_three(fields)
    rows = jnp.concatenate([pieces, jnp.ones((1, total), jnp.bfloat16)], axis=0)
    rows = rows.reshape(rows.shape[0], blocks, blk)
    bin_blocks = flat_bins.reshape(blocks, blk)

    def add_block(carry, index):
        block_rows = lax.dynamic_index_in_dim(rows, index, 1, keepdims=False)
        table = one_hot(lax.dynamic_index_in_dim(bin_blocks, index, 0, keepdims=False))
        return (carry + jnp.dot(block_rows, table, preferred_element_type=jnp.float32), None)

    start = jnp.zeros((rows.shape[0], NBINS), jnp.float32)
    totals, unused = lax.scan(add_block, start, jnp.arange(blocks, dtype=jnp.int32))
    sums = (
        totals[:count_fields]
        + totals[count_fields : 2 * count_fields]
        + totals[2 * count_fields : 3 * count_fields]
    )
    return (sums, totals[3 * count_fields])


def lift(table, bin_field):
    count_fields = table.shape[0]
    flat_bins = bin_field.reshape(-1)
    total = flat_bins.shape[0]
    blk = block_size(total)
    blocks = total // blk
    pieces = split_three(table)
    bin_blocks = flat_bins.reshape(blocks, blk)

    def pick_block(bin_block):
        chosen = lax.dot_general(
            pieces, one_hot(bin_block), (((1,), (1,)), ((), ())), preferred_element_type=jnp.float32
        )
        return (
            chosen[:count_fields]
            + chosen[count_fields : 2 * count_fields]
            + chosen[2 * count_fields :]
        )

    picked = lax.map(pick_block, bin_blocks)
    picked = jnp.moveaxis(picked, 1, 0).reshape(count_fields, total)
    return picked.reshape((count_fields,) + bin_field.shape)


def profile(fields, flat_bins):
    sums, counts = bin_sums(fields.reshape(fields.shape[0], -1), flat_bins)
    total_sums, total_counts = lax.psum((sums, counts), ("box", "depth"))
    return total_sums / jnp.maximum(total_counts, 1.0)


def per_device(state, velocity, bins):
    flat_bins = bins.reshape(-1)
    local_speed = jnp.max(jnp.sum(jnp.abs(velocity), axis=0))
    top_speed = lax.pmax(local_speed, ("box", "depth"))
    time_step = COURANT / (top_speed + 1.0)
    first = profile(state, flat_bins)
    first_lift = lift(first, bins)
    perturb = state - first_lift
    extended = extended_2(perturb, (("box", 2), ("depth", 1)), 1)
    padded = jnp.pad(extended, ((0, 0), (0, 0), (0, 0), (1, 1)))
    new_state = first_lift + upwind(padded, velocity, time_step)
    second = profile(new_state, flat_bins)
    lifted = lift(second, bins)
    source = jnp.zeros_like(new_state[0])
    for field_index in range(len(RHS_WEIGHTS)):
        source = source + RHS_WEIGHTS[field_index] * (new_state[field_index] - lifted[field_index])
    potential = jnp.zeros_like(source)
    for sweep_index in range(ITERS):
        rimmed = extended_2(potential, (("box", 1), ("depth", 0)), 1)
        potential = relax(pad_depth(rimmed), source)
    return (new_state, potential, second)


def solution(mesh):
    return jax.shard_map(
        per_device,
        mesh=mesh,
        in_specs=(
            P(None, "depth", "box", None),
            P(None, "depth", "box", None),
            P("depth", "box", None),
        ),
        out_specs=(P(None, "depth", "box", None), P("depth", "box", None), P()),
        check_vma=False,
    )
```

profile of v0, /device:TPU:1, one launch (start us, length us, event | category | flops | bytes accessed | tf_op | source)
XLA Modules:
  0.0 952.0 jit_solution(8284085759273161880)
XLA Ops:
  16.1 105.2 %while.44 = (s32[]{:T(128)}, f32[16,4096]{1,0:T(8,128)S(1)}, s32[12]{0:T(128)S(1)}, bf16[16,12,2048]{2,0,1:T(8,128)(2,1)S(1)}, s32[12,2048]{1,0:T(8,128)S(1)}, /*index=5*/s32[]{:T(128)}, s32[]{:T(128)}, s32[]{:T(128)}) while((s32[]{:T(128)}, f32[16,4096]{1,0:T(8,128)S(1)}, s32[12]{0:T(128)S(1)}, ...), condition=%wide.region_1.0_spmd.clone, body=%wide.region_0.0_spmd.clone.sunk | while | flops 276955136 | bytes 614549 | solution.py:95
  122.3 81.7 %psum.29 = f32[4096]{0:T(1024)S(1)} all-reduce(f32[4096]{0:T(1024)S(1)} %bitcast.152), channel_id=1, replica_groups=mesh['box'=32,'depth'=8] {'box','depth'}, use_global_device_ids=true, to_apply=%region_3.4 | all-reduce | flops 4096 | bytes 32768 | tf_op jit(solution)/shard_map/psum | solution.py:130
  204.6 73.8 %pmax.7 = f32[]{:T(128)} all-reduce(f32[]{:T(128)} %reduce_max.9), channel_id=1, replica_groups=mesh['box'=32,'depth'=8] {'box','depth'}, use_global_device_ids=true, to_apply=%region_8.9 | all-reduce | flops 1 | bytes 8 | tf_op jit(solution)/shard_map/pmax | solution.py:137
  279.0 89.2 %all-reduce.10.cloned.1.call-done = f32[5,4096]{1,0:T(8,128)} async-done(((f32[5,4096]{1,0:T(8,128)}), f32[5,4096]{1,0:T(8,128)}) %all-reduce.10.cloned.1.call-update) | async-done | bytes 81936 | tf_op jit(solution)/shard_map/psum | solution.py:130
  371.2 75.4 %while.42 = (s32[]{:T(128)}, f32[12,5,2048]{2,1,0:T(8,128)S(1)}, s32[12,2048]{1,0:T(8,128)S(1)}, bf16[15,4096]{1,0:T(8,128)(2,1)S(1)}, s32[]{:T(128)}) while((s32[]{:T(128)}, f32[12,5,2048]{2,1,0:T(8,128)S(1)}, s32[12,2048]{1,0:T(8,128)S(1)}, bf16[15,4096]{1,0:T(8,128)(2,1)S(1)}, s32[]{:T(128)}) %tuple.112), condition=%wide.region_5.6_spmd, body=%wide.region_4.5_spmd.sunk | while | flops 260067328 | bytes 532549 | solution.py:123
  371.2 6.2 fusion.108
  383.8 6.2 fusion.108
  396.3 6.2 fusion.108
  408.9 6.2 fusion.108
  415.2 6.2 fusion.108
  421.5 6.2 fusion.108
  427.8 6.2 fusion.108
  434.1 6.2 fusion.108
  440.3 6.2 fusion.108
  470.1 105.2 %while.45 = (s32[]{:T(128)}, f32[16,4096]{1,0:T(8,128)S(1)}, s32[12]{0:T(128)S(1)}, bf16[16,12,2048]{2,0,1:T(8,128)(2,1)S(1)}, s32[12,2048]{1,0:T(8,128)S(1)}, /*index=5*/s32[]{:T(128)}, s32[]{:T(128)}, s32[]{:T(128)}) while((s32[]{:T(128)}, f32[16,4096]{1,0:T(8,128)S(1)}, s32[12]{0:T(128)S(1)}, ...), condition=%wide.region_10.11_spmd.clone, body=%wide.region_9.10_spmd.clone.sunk | while | flops 276955136 | bytes 614549 | solution.py:95
  576.1 78.5 %psum.31 = f32[4096]{0:T(1024)S(1)} all-reduce(f32[4096]{0:T(1024)S(1)} %bitcast.153), channel_id=1, replica_groups=mesh['box'=32,'depth'=8] {'box','depth'}, use_global_device_ids=true, to_apply=%region_12.13 | all-reduce | flops 4096 | bytes 32768 | tf_op jit(solution)/shard_map/psum | solution.py:130
  654.6 162.1 %all-reduce.12.cloned.1.call-done = f32[5,4096]{1,0:T(8,128)} async-done(((f32[5,4096]{1,0:T(8,128)}), f32[5,4096]{1,0:T(8,128)}) %all-reduce.12.cloned.1.call-update) | async-done | bytes 81936 | tf_op jit(solution)/shard_map/psum | solution.py:130
  818.3 75.4 %while.43 = (s32[]{:T(128)}, f32[12,5,2048]{2,1,0:T(8,128)S(1)}, s32[12,2048]{1,0:T(8,128)S(1)}, bf16[15,4096]{1,0:T(8,128)(2,1)S(1)}, s32[]{:T(128)}) while((s32[]{:T(128)}, f32[12,5,2048]{2,1,0:T(8,128)S(1)}, s32[12,2048]{1,0:T(8,128)S(1)}, bf16[15,4096]{1,0:T(8,128)(2,1)S(1)}, s32[]{:T(128)}) %tuple.114), condition=%wide.region_14.15_spmd, body=%wide.region_13.14_spmd.sunk | while | flops 260067328 | bytes 532549 | solution.py:123
  818.3 6.2 fusion.111
  830.8 6.2 fusion.111
  843.4 6.2 fusion.111
  856.0 6.2 fusion.111
  868.6 6.2 fusion.111
  881.1 6.2 fusion.111
  (250 shorter events, 310.4 us)
Async XLA Ops:
  7.2 361.0 %all-reduce.10.cloned.1.call-start = ((), (), s32[]{:S(2)}) async-start(), calls=%async_computation | async-start | bytes 262144 | tf_op jit(solution)/shard_map/psum | solution.py:130
  7.8 444.8 %collective-permute-start.4 = (f32[8,1,384]{2,1,0:T(1,128)}, f32[8,1,384]{2,1,0:T(1,128)S(1)}, u32[]{:S(2)}, u32[]{:S(2)}) collective-permute-start(f32[8,1,384]{2,1,0:T(1,128)} %broadcast.58), channel_id=1, source_target_pairs={{0,8},{8,16},{16,24},{24,32},{32,40},{40,48},{48,56},{56,64},{64,7... | collective-permute-start | bytes 36872 | tf_op jit(solution)/shard_map/ppermute | solution.py:26
  12.2 440.5 %collective-permute-start.5 = (f32[8,1,384]{2,1,0:T(1,128)}, f32[8,1,384]{2,1,0:T(1,128)}, u32[]{:S(2)}, u32[]{:S(2)}) collective-permute-start(f32[8,1,384]{2,1,0:T(1,128)} %broadcast.58), channel_id=1, source_target_pairs={{8,0},{16,8},{24,16},{32,24},{40,32},{48,40},{56,48},{64,56},{72,6... | collective-permute-start | bytes 36872 | tf_op jit(solution)/shard_map/ppermute | solution.py:28
  16.1 106.0 %copy-start.2 = (f32[3,8,8,384]{3,2,1,0:T(8,128)S(1)}, f32[3,8,8,384]{3,2,1,0:T(8,128)}, u32[]{:S(2)}) copy-start(f32[3,8,8,384]{3,2,1,0:T(8,128)} %param.12) | copy-start | bytes 884740
  122.1 694.6 %all-reduce.12.cloned.1.call-start = ((), (), s32[]{:S(2)}) async-start(), calls=%async_computation.1 | async-start | bytes 262144 | tf_op jit(solution)/shard_map/psum | solution.py:130
  447.8 11.2 %collective-permute-start = (f32[5,8,1,384]{3,2,1,0:T(1,128)S(1)}, f32[5,8,1,384]{3,2,1,0:T(1,128)S(1)}, u32[]{:S(2)}, u32[]{:S(2)}) collective-permute-start(f32[5,8,1,384]{3,2,1,0:T(1,128)S(1)} %get-tuple-element.209), channel_id=1, source_target_pairs={{0,8},{8,16},{16,24},{24,32},{32,40},{40,48},{48,56},{56,64},{64,7... | collective-permute-start | bytes 184328 | tf_op jit(solution)/shard_map/ppermute | solution.py:26
  451.3 7.6 collective-permute-start.1
  453.4 10.0 %collective-permute-start.6 = (f32[1,10,384]{2,1,0:T(8,128)S(1)}, f32[1,10,384]{2,1,0:T(8,128)S(1)}, u32[]{:S(2)}, u32[]{:S(2)}) collective-permute-start(f32[1,10,384]{2,1,0:T(8,128)S(1)} %get-tuple-element.224), channel_id=1, source_target_pairs={{1,0},{2,1},{3,2},{4,3},{5,4},{6,5},{7,6},{9,8},{10,9},{11,10},{12... | collective-permute-start | bytes 46088 | tf_op jit(solution)/shard_map/ppermute | solution.py:28
  455.5 7.9 collective-permute-start.7
  459.0 5.3 collective-permute-start.2
  461.0 6.2 collective-permute-start.3
  469.0 426.2 %copy-start = (f32[5,8,8,384]{3,2,1,0:T(8,128)}, f32[5,8,8,384]{3,2,1,0:T(8,128)S(1)}, u32[]{:S(2)}) copy-start(f32[5,8,8,384]{3,2,1,0:T(8,128)S(1)} %fusion.29) | copy-start | bytes 1474564
  896.0 4.9 collective-permute-start.8
  899.6 4.4 collective-permute-start.9
  904.1 6.3 collective-permute-start.10
  907.3 3.9 collective-permute-start.11
  911.7 3.9 collective-permute-start.12
  914.3 4.8 collective-permute-start.13
  919.1 7.2 collective-permute-start.14
  921.5 5.8 collective-permute-start.15
  927.6 4.9 collective-permute-start.16
  931.2 4.7 collective-permute-start.17
  936.0 7.3 collective-permute-start.18
  937.9 6.3 collective-permute-start.19
  (3 other events, 2.6 us)
Sparse Core Ops, SparseCore 0:
  122.2 245.9 all-reduce.9
  576.2 240.4 all-reduce.11
where the time goes:
time: 955 us; the launch traced here: 952 us
  matrix products  298 us (31%)
  waiting for transfers between devices  267 us (28%)
  blocking collectives  234 us (25%)
  starting transfers between devices  54.9 us (6%)
  loops' own time  47.7 us (5%)
  local copies, waits for them, and re-layouts  20.8 us (2%)
  between operations  15.4 us (2%)
  other arithmetic  13.8 us (1%)
    psum x2, waiting for transfers between devices, profile(): total_sums, total_counts = lax.psum((sums, counts), ('box', 'depth'))  251 us
    psum x2, blocking collectives, profile(): total_sums, total_counts = lax.psum((sums, counts), ('box', 'depth'))  160 us
    dot_general x24, matrix products, pick_block(): lax.dot_general(pieces, one_hot(bin_block), (((1,), (1,)), ((), ())), pre...  149 us
    dot_general x24, matrix products, add_block(): jnp.dot(block_rows, table, preferred_element_type=jnp.float32)  149 us
    pmax x1, blocking collectives, per_device(): top_speed = lax.pmax(local_speed, ('box', 'depth'))  73.8 us
    another operation x2, loops' own time, bin_sums(): lax.scan(add_block, start, jnp.arange(blocks, dtype=jnp.int32))  47 us
    ppermute x10, starting transfers between devices, extended_2(): lax.ppermute(tail, axis, [(i, (i + 1) % count) for i in range(ends)])  36.4 us
  transfers between devices with their start and end apart: 22, of which 9 were waited for; matrix products, arithmetic and copies ran while one was open for 17% of the time, Pallas kernels for 0%

commit v1 on v0

v1 whole, which is shorter than its diff:
```python
import jax
import jax.numpy as jnp
from jax import lax
from jax.experimental import pallas as pl
from jax.experimental.pallas import tpu as pltpu
from jax.sharding import PartitionSpec as P

NBINS = 4096
COURANT = 0.8
OMEGA_RELAX = 0.8
DIAGONAL = 6.1
WEIGHTS = (1.0, 0.5, -0.5, 0.25, 0.75)
NF = 5
X, Y, Z = 8, 8, 384
TILES = NBINS // 128
REACH = 3
F32, BF16 = jnp.float32, jnp.bfloat16
VMEM_BYTES = 48 * 1024 * 1024


def pieces_of(values):
    upper = values.astype(BF16).astype(F32)
    rest = values - upper
    middle = rest.astype(BF16).astype(F32)
    return upper, middle, rest - middle


def lo_table(lo_row):
    wide = jnp.broadcast_to(lo_row, (16, Z)).astype(BF16)
    row = lax.broadcasted_iota(jnp.int32, (16, Z), 0).astype(F32).astype(BF16)
    one, zero = jnp.ones((16, Z), BF16), jnp.zeros((16, Z), BF16)
    return jnp.concatenate([jnp.where(wide == row + jnp.asarray(16 * k, BF16), one, zero) for k in range(16)], axis=0)


def hi_rows(hi_row, rows16):
    wide = jnp.broadcast_to(hi_row, (16, Z)).astype(BF16)
    zero = jnp.zeros((16, Z), BF16)
    return jnp.concatenate([jnp.where(wide == jnp.asarray(k, BF16), rows16, zero) for k in range(16)], axis=0)


def put_rows(rows, p, values):
    for j in range(3):
        rows[j, pl.ds(p, Y, stride=16), :] = values[:, j * 128 : (j + 1) * 128]


def get_rows(rows, y):
    return jnp.concatenate([rows[j, pl.ds(16 * y, 16), :].astype(BF16) for j in range(3)], axis=1)


def get_field(lifted, x, f):
    return jnp.concatenate([lifted[x, j, pl.ds(f, Y, stride=8), :] for j in range(3)], axis=1)


def add_bins(acc, rows, hi, lo, x):
    left, right = [], []
    for y in range(Y):
        left.append(hi_rows(hi[x, pl.ds(y, 1), :], get_rows(rows, y)))
        right.append(lo_table(lo[x, pl.ds(y, 1), :]))
    acc[...] += lax.dot_general(
        jnp.concatenate(left, 1), jnp.concatenate(right, 1), (((1,), (1,)), ((), ())), preferred_element_type=F32
    )


def put_sums(out, acc, extra):
    for k in range(16):
        s = acc[pl.ds(16 * k, 16), :]
        tile = jnp.concatenate([s[0:5] + s[5:10] + s[10:15], s[15:16], extra], axis=0)
        out[2 * k] = tile[:, :128]
        out[2 * k + 1] = tile[:, 128:]


def split_bins(bins, hi, lo):
    b = bins[...]
    hi[...] = lax.shift_right_logical(b, 8).astype(F32)
    lo[...] = (b & 255).astype(F32)


def sums_kernel(state, velocity, bins, out, hi, lo, rows, acc):
    split_bins(bins, hi, lo)
    acc[...] = jnp.zeros_like(acc)
    put_rows(rows, 15, jnp.ones((Y, Z), F32))

    def step(x, carry):
        for f in range(NF):
            for i, piece in enumerate(pieces_of(state[f, x])):
                put_rows(rows, NF * i + f, piece)
        add_bins(acc, rows, hi, lo, x)
        return carry

    lax.fori_loop(0, X, step, 0)
    top = jnp.max(jnp.abs(velocity[0]) + jnp.abs(velocity[1]) + jnp.abs(velocity[2]))
    put_sums(out, acc, jnp.full((2, 256), top, F32))


def digits(b):
    h = jnp.floor(b * (1.0 / 256.0))
    return h, b - 256.0 * h


def lift_row(table, hi_row, lo_row):
    found = lax.dot_general(table, lo_table(lo_row), (((1,), (0,)), ((), ())), preferred_element_type=F32)
    wide = jnp.broadcast_to(hi_row, (16, Z))
    acc = jnp.zeros((16, Z), F32)
    for k in range(16):
        acc = jnp.where(wide == float(k), found[16 * k : 16 * k + 16], acc)
    total = acc[0:5] + acc[5:10] + acc[10:15]
    return jnp.concatenate([total, jnp.zeros((3, Z), F32)], axis=0)


def step_kernel(
    first, state, velocity, bins, ylo, yhi, xlo, xhi, new_state, q_out, out, hi, lo, face_hi, face_lo, table, lifted, p, rows, acc
):
    for k in range(16):
        pair = jnp.concatenate([first[2 * k], first[2 * k + 1]], axis=1)
        u, m, l = pieces_of(pair)
        block = jnp.concatenate([u[0:5], m[0:5], l[0:5], jnp.zeros((1, 256), F32)], axis=0)
        table[pl.ds(16 * k, 16), :] = block.astype(BF16)
    tab = table[...]
    time_step = COURANT / (1.0 + jnp.max(first[0, 6:7, :]))
    split_bins(bins, hi, lo)
    for s, (ref, near) in enumerate(((xlo, 7), (xhi, 5))):
        face_hi[s], face_lo[s] = digits(ref[near] - 1.0)

    def lift_x(x, carry):
        for y in range(Y):
            eight = lift_row(tab, hi[x, pl.ds(y, 1), :], lo[x, pl.ds(y, 1), :])
            for j in range(3):
                lifted[x, j, pl.ds(8 * y, 8), :] = eight[:, 128 * j : 128 * j + 128]
        for f in range(NF):
            p[f, x + 1, pl.ds(8, 8), :] = state[f, x] - get_field(lifted, x, f)
        for ref, at, near in ((ylo, 7, 7), (yhi, 16, 5)):
            h, l = digits(ref[x, near : near + 1, :] - 1.0)
            eight = ref[x] - lift_row(tab, h, l)
            for f in range(NF):
                p[f, x + 1, at : at + 1, :] = eight[f : f + 1]
        return carry

    lax.fori_loop(0, X, lift_x, 0)
    for s, (ref, at) in enumerate(((xlo, 0), (xhi, X + 1))):
        for y in range(Y):
            eight = lift_row(tab, face_hi[s, y : y + 1, :], face_lo[s, y : y + 1, :])
            for j in range(3):
                lifted[X, j, pl.ds(8 * y, 8), :] = eight[:, 128 * j : 128 * j + 128]
        for f in range(NF):
            p[f, at, pl.ds(8, 8), :] = ref[f] - get_field(lifted, X, f)

    acc[...] = jnp.zeros_like(acc)
    lane = lax.broadcasted_iota(jnp.int32, (Y, Z), 1)
    put_rows(rows, 15, jnp.zeros((Y, Z), F32))

    def advect(x, carry):
        v = [velocity[d, x] for d in range(3)]
        up = [jnp.maximum(c, 0.0) for c in v]
        down = [jnp.minimum(c, 0.0) for c in v]
        q = jnp.zeros((Y, Z), F32)
        for f in range(NF):
            c = p[f, x + 1, pl.ds(8, 8), :]
            before = jnp.where(lane == 0, 0.0, pltpu.roll(c, 1, 1))
            after = jnp.where(lane == Z - 1, 0.0, pltpu.roll(c, Z - 1, 1))
            change = up[0] * (c - p[f, x, pl.ds(8, 8), :]) + down[0] * (p[f, x + 2, pl.ds(8, 8), :] - c)
            change += up[1] * (c - p[f, x + 1, pl.ds(7, 8), :]) + down[1] * (p[f, x + 1, pl.ds(9, 8), :] - c)
            change += up[2] * (c - before) + down[2] * (after - c)
            moved = c - time_step * change
            new_state[f, x] = get_field(lifted, x, f) + moved
            q += WEIGHTS[f] * moved
            for i, piece in enumerate(pieces_of(moved)):
                put_rows(rows, NF * i + f, piece)
        q_out[x] = q
        add_bins(acc, rows, hi, lo, x)
        return carry

    lax.fori_loop(0, X, advect, 0)
    put_sums(out, acc, jnp.zeros((2, 256), F32))


def relax_kernel(
    second, first, q, qylo, qyhi, qxlo, qxhi, bins, ylo, yhi, xlo, xhi, potential, profile, table, digit, src, pot
):
    total = jnp.zeros((TILES, 128), F32)
    for t in range(TILES):
        profile[:, 128 * t : 128 * t + 128] = (first[t] + second[t])[0:NF]
    for f in range(NF):
        total += WEIGHTS[f] * second[:, f, :]
    cols = jnp.concatenate([total[:, 0:64], total[:, 64:128]], axis=0)
    upper = cols.astype(BF16).astype(F32)
    table[...] = jnp.concatenate([upper, cols - upper], axis=1).astype(BF16)
    tab = table[...]
    src[...] = jnp.zeros_like(src)
    digit[...] = jnp.full(digit.shape, -1.0, F32)
    src[pl.ds(3, 8), 8:16, :] = q[...]
    src[pl.ds(3, 8), 5:8, :] = qylo[...]
    src[pl.ds(3, 8), 16:19, :] = qyhi[...]
    digit[pl.ds(3, 8), 8:16, :] = bins[...].astype(F32)
    digit[pl.ds(3, 8), 5:8, :] = ylo[:, 5:8, :] - 1.0
    digit[pl.ds(3, 8), 16:19, :] = yhi[:, 5:8, :] - 1.0
    for at, qref, bref in ((0, qxlo, xlo), (11, qxhi, xhi)):
        for dst, ref, base, less in ((src, qref, 0, 0.0), (digit, bref, NF, 1.0)):
            dst[pl.ds(at, 3), 8:16, :] = ref[pl.ds(base, 3)] - less
            dst[pl.ds(at, 3), 5:8, :] = ref[pl.ds(base + 3, 3), 0:3, :] - less
            dst[pl.ds(at, 3), 16:19, :] = ref[pl.ds(base + 3, 3), 3:6, :] - less
    row = lax.broadcasted_iota(jnp.int32, (64, Z), 0).astype(F32)
    row16 = lax.broadcasted_iota(jnp.int32, (16, Z), 0).astype(F32).astype(BF16)
    one, zero = jnp.ones((16, Z), BF16), jnp.zeros((16, Z), BF16)

    def lift_x(x, carry):
        for y in range(5, 19):
            b = digit[x, y : y + 1, :]
            h = jnp.floor(b * (1.0 / 64.0))
            l = jnp.broadcast_to(b - 64.0 * h, (16, Z)).astype(BF16)
            g = jnp.floor(h * 0.5)
            h = jnp.where(b < 0.0, -1.0, g + 32.0 * (h - 2.0 * g))
            t = jnp.concatenate([jnp.where(l == row16 + jnp.asarray(16 * k, BF16), one, zero) for k in range(4)], axis=0)
            o = lax.dot_general(tab, jnp.concatenate([t, t], axis=0), (((1,), (0,)), ((), ())), preferred_element_type=F32)
            o = jnp.where(jnp.broadcast_to(h, (64, Z)) == row, o, 0.0)
            src[x, y : y + 1, :] = src[x, y : y + 1, :] - jnp.sum(o, axis=0, keepdims=True)
        return carry

    lax.fori_loop(0, 14, lift_x, 0)
    lane = lax.broadcasted_iota(jnp.int32, (24, Z), 1)

    def start(x, carry):
        pot[0, x] = src[x] * (OMEGA_RELAX / DIAGONAL)
        return carry

    lax.fori_loop(0, 14, start, 0)
    for s in range(1, 4):
        now, later = (s + 1) % 2, s % 2

        def sweep(x, carry):
            c = pot[now, x]
            near = pot[now, x - 1] + pot[now, x + 1]
            near += pltpu.roll(c, 1, 0) + pltpu.roll(c, 23, 0)
            near += jnp.where(lane == 0, 0.0, pltpu.roll(c, 1, 1)) + jnp.where(lane == Z - 1, 0.0, pltpu.roll(c, Z - 1, 1))
            new = c + OMEGA_RELAX * (src[x] - (DIAGONAL * c - near)) / DIAGONAL
            if s < 3:
                pot[later, x] = jnp.where(digit[x] < 0.0, 0.0, new)
            else:
                potential[x - 3] = new[8:16]
            return carry

        lax.fori_loop(s, 14 - s, sweep, 0)


def call(kernel, out_shape, scratch, *args):
    return pl.pallas_call(
        kernel,
        out_shape=out_shape,
        scratch_shapes=[pltpu.VMEM(shape, dtype) for shape, dtype in scratch],
        compiler_params=pltpu.CompilerParams(vmem_limit_bytes=VMEM_BYTES),
    )(*args)


def f32_like(*shape):
    return jax.ShapeDtypeStruct(shape, F32)


def from_below(face, axis):
    count = lax.axis_size(axis)
    return lax.ppermute(face, axis, [(i, i + 1) for i in range(count - 1)])


def from_above(face, axis):
    count = lax.axis_size(axis)
    return lax.ppermute(face, axis, [(i + 1, i) for i in range(count - 1)])


def beside(below, above, part):
    gap = jnp.zeros((REACH, 2, Z), F32)
    return jnp.concatenate([below[part], above[part], gap], axis=1)


def merge(tiles):
    total = jnp.sum(tiles, axis=0)
    top = jnp.max(tiles, axis=0)
    row = lax.broadcasted_iota(jnp.int32, total.shape, 1)
    return jnp.where(row == 6, top, total)


def own_share(tiles):
    depth, box = lax.axis_size("depth"), lax.axis_size("box")
    share = tiles.reshape(depth, TILES // depth, 8, 128)
    share = merge(lax.all_to_all(share, "depth", 0, 0, tiled=True))
    copies = jnp.broadcast_to(share[None], (box,) + share.shape)
    return merge(lax.all_to_all(copies, "box", 0, 0, tiled=True))


def spread(share):
    depth = lax.axis_size("depth")
    copies = jnp.broadcast_to(share[None], (depth,) + share.shape)
    return lax.all_to_all(copies, "depth", 0, 0, tiled=True).reshape(TILES, 8, 128)


def per_device(state, velocity, bins):
    shifted = bins.astype(F32) + 1.0
    ylo = from_below(jnp.concatenate([jnp.swapaxes(state[:, :, Y - 1], 0, 1), shifted[:, Y - REACH :]], axis=1), "box")
    yhi = from_above(jnp.concatenate([jnp.swapaxes(state[:, :, 0], 0, 1), shifted[:, :REACH]], axis=1), "box")
    low, high = slice(0, REACH), slice(X - REACH, X)
    xfaces = []
    for part, edge in ((high, X - 1), (low, 0)):
        corners = beside(ylo[:, NF:], yhi[:, NF:], part)
        xfaces.append(jnp.concatenate([state[:, edge], shifted[part], corners], axis=0))
    xlo = from_below(xfaces[0], "depth")
    xhi = from_above(xfaces[1], "depth")
    tiles = call(
        sums_kernel,
        f32_like(TILES, 8, 128),
        [((X, Y, Z), F32), ((X, Y, Z), F32), ((3, Y * 16, 128), F32), ((256, 256), F32)],
        state, velocity, bins,
    )
    share = own_share(tiles)
    counts = jnp.maximum(share[:, 5:6], 1.0)
    row = lax.broadcasted_iota(jnp.int32, share.shape, 1)
    first = spread(jnp.where(row < NF, share / counts, share))
    new_state, q, tiles = call(
        step_kernel,
        (f32_like(NF, X, Y, Z), f32_like(X, Y, Z), f32_like(TILES, 8, 128)),
        [
            ((X, Y, Z), F32), ((X, Y, Z), F32), ((2, Y, Z), F32), ((2, Y, Z), F32), ((256, 256), BF16),
            ((X + 1, 3, 64, 128), F32), ((NF, X + 2, 24, Z), F32), ((3, Y * 16, 128), F32), ((256, 256), F32),
        ],
        first, state, velocity, bins, ylo, yhi, xlo, xhi,
    )
    qylo = from_below(q[:, Y - REACH :], "box")
    qyhi = from_above(q[:, :REACH], "box")
    qxlo = from_below(jnp.concatenate([q[high], beside(qylo, qyhi, high)], axis=0), "depth")
    qxhi = from_above(jnp.concatenate([q[low], beside(qylo, qyhi, low)], axis=0), "depth")
    second = spread(own_share(tiles) / counts)
    potential, profile = call(
        relax_kernel,
        (f32_like(X, Y, Z), f32_like(NF, NBINS)),
        [((64, 128), BF16), ((14, 24, Z), F32), ((14, 24, Z), F32), ((2, 14, 24, Z), F32)],
        second, first, q, qylo, qyhi, qxlo, qxhi, bins, ylo, yhi, xlo, xhi,
    )
    return (new_state, potential, profile)


def solution(mesh):
    return jax.shard_map(
        per_device,
        mesh=mesh,
        in_specs=(
            P(None, "depth", "box", None),
            P(None, "depth", "box", None),
            P("depth", "box", None),
        ),
        out_specs=(P(None, "depth", "box", None), P("depth", "box", None), P()),
        check_vma=False,
    )
```

time: 955 us -> 134 us (0.14)
  matrix products: 298 us -> 0 us
  waiting for transfers between devices: 267 us -> 26.5 us
  blocking collectives: 234 us -> 8.51 us
  loops' own time: 47.7 us -> 0 us
  Pallas kernels: 0 us -> 29.4 us
  local copies, waits for them, and re-layouts: 20.8 us -> 6.19 us
  between operations: 15.4 us -> 0.92 us
  other arithmetic: 13.8 us -> 0.64 us
    dot_general x48 -> x0, matrix products: 298 us -> none  [the longest x24 149 us: pick_block(): lax.dot_general(pieces, one_hot(bin_block), (((1,), (1,)), ((), ())), pre...]
    psum x2 -> x0, waiting for transfers between devices: 251 us -> none  [profile(): total_sums, total_counts = lax.psum((sums, counts), ('box', 'depth'))]
    psum x2 -> x0, blocking collectives: 160 us -> none  [profile(): total_sums, total_counts = lax.psum((sums, counts), ('box', 'depth'))]
    pmax x1 -> x0, blocking collectives: 73.8 us -> none  [per_device(): top_speed = lax.pmax(local_speed, ('box', 'depth'))]
    another operation x4 -> x0, loops' own time: 47.7 us -> none  [the longest x2 47 us: bin_sums(): lax.scan(add_block, start, jnp.arange(blocks, dtype=jnp.int32))]
    all_to_all x0 -> x5, starting transfers between devices: none -> 40 us  [the longest x2 17 us: own_share(): return merge(lax.all_to_all(copies, 'box', 0, 0, tiled=True))]
    ppermute x20 -> x8, starting transfers between devices: 54.8 us -> 21.2 us  [the longest x4 14.7 us: from_below(): return lax.ppermute(face, axis, [(i, i + 1) for i in range(count - 1)])]
    pallas_call x0 -> x3, Pallas kernels: none -> 29.4 us  [call(): pl.pallas_call(kernel, out_shape=out_shape, scratch_shapes=[pltpu.VMEM(sh...]
  transfers between devices with their start and end apart: 22 -> 13, of which waited for: 9 -> 6; matrix products, arithmetic and copies ran while one was open for 17% -> 2% of each run, Pallas kernels for 0% -> 0%
where the time goes in v1:
time: 134 us; the launch traced here: 133 us
  starting transfers between devices  61.2 us (46%)
  Pallas kernels  29.4 us (22%)
  waiting for transfers between devices  26.5 us (20%)
  blocking collectives  8.51 us (6%)
  local copies, waits for them, and re-layouts  6.19 us (5%)
    pallas_call x3, Pallas kernels, call(): pl.pallas_call(kernel, out_shape=out_shape, scratch_shapes=[pltpu.VMEM(sh...  29.4 us
    all_to_all x2, starting transfers between devices, own_share(): return merge(lax.all_to_all(copies, 'box', 0, 0, tiled=True))  17 us
    all_to_all x2, starting transfers between devices, spread(): lax.all_to_all(copies, 'depth', 0, 0, tiled=True).reshape(TILES, 8, 128)  16.4 us
    ppermute x4, starting transfers between devices, from_below(): return lax.ppermute(face, axis, [(i, i + 1) for i in range(count - 1)])  14.7 us
    ppermute x4, waiting for transfers between devices, from_above(): return lax.ppermute(face, axis, [(i + 1, i) for i in range(count - 1)])  11.4 us
    all_to_all x2, waiting for transfers between devices, own_share(): return merge(lax.all_to_all(copies, 'box', 0, 0, tiled=True))  8.9 us
    all_to_all x1, blocking collectives, own_share(): share = merge(lax.all_to_all(share, 'depth', 0, 0, tiled=True))  8.51 us
    all_to_all x1, starting transfers between devices, own_share(): share = merge(lax.all_to_all(share, 'depth', 0, 0, tiled=True))  6.64 us
  transfers between devices with their start and end apart: 13, of which 6 were waited for; matrix products, arithmetic and copies ran while one was open for 2% of the time, Pallas kernels for 0%

profile of v1, /device:TPU:1, one launch (start us, length us, event | category | flops | bytes accessed | tf_op | source)
XLA Modules:
  0.0 133.4 jit_solution(5253222156343060362)
XLA Ops:
  0.6 1.0 copy-done
  2.6 1.0 copy-done.4
  3.5 5.8 %shard_map.58 = f32[32,8,128]{2,1,0:T(8,128)} custom-call(f32[5,8,8,384]{3,2,1,0:T(8,128)S(1)} %copy-done, f32[3,8,8,384]{3,2,1,0:T(8,128)S(1)} %copy-done.4, s32[8,8,384]{2,1,0:T(8,128)S(1)} %copy-done.2), custom_call_target="tpu_custom_call" | custom-call | tf_op jit(solution)/shard_map/pallas_call | solution.py:245
  9.3 6.6 %all-to-all-start = ((f32[8,4,8,128]{3,2,1,0:T(8,128)}), f32[8,4,8,128]{3,2,1,0:T(8,128)S(1)}, u32[]{:S(2)}, u32[]{:S(2)}) async-start(f32[8,4,8,128]{3,2,1,0:T(8,128)} %bitcast), calls=%async_computation | async-start | bytes 262144 | tf_op jit(solution)/shard_map/all_to_all | solution.py:282
  16.2 2.8 %collective-permute-start = (f32[8,8,384]{2,1,0:T(8,128)S(1)}, f32[8,8,384]{2,1,0:T(8,128)S(1)}, u32[]{:S(2)}, u32[]{:S(2)}) collective-permute-start(f32[8,8,384]{2,1,0:T(8,128)S(1)} %pad_maximum_fusion.4), channel_id=1, source_target_pairs={{0,8},{8,16},{16,24},{24,32},{32,40},{40,48},{48,56},{56,64},{64,7... | collective-permute-start | bytes 294920 | tf_op jit(solution)/shard_map/ppermute | solution.py:259
  19.1 1.3 collective-permute-start.1
  22.2 12.0 %all-to-all-start.1 = ((f32[32,4,8,128]{3,2,1,0:T(8,128)}), f32[32,4,8,128]{3,2,1,0:T(8,128)S(1)}, u32[]{:S(2)}, u32[]{:S(2)}) async-start(f32[32,4,8,128]{3,2,1,0:T(8,128)} %broadcast_in_dim.8), calls=%async_computation.1 | async-start | bytes 1048576 | tf_op jit(solution)/shard_map/all_to_all | solution.py:284
  34.4 4.4 %collective-permute-start.2 = (f32[11,8,384]{2,1,0:T(8,128)S(1)}, f32[11,8,384]{2,1,0:T(8,128)S(1)}, u32[]{:S(2)}, u32[]{:S(2)}) collective-permute-start(f32[11,8,384]{2,1,0:T(8,128)S(1)} %get-tuple-element.44), channel_id=1, source_target_pairs={{0,1},{1,2},{2,3},{3,4},{4,5},{5,6},{6,7},{8,9},{9,10},{10,11},{11... | collective-permute-start | bytes 405512 | tf_op jit(solution)/shard_map/ppermute | solution.py:259
  38.8 1.9 %collective-permute-start.3 = (f32[11,8,384]{2,1,0:T(8,128)S(1)}, f32[11,8,384]{2,1,0:T(8,128)S(1)}, u32[]{:S(2)}, u32[]{:S(2)}) collective-permute-start(f32[11,8,384]{2,1,0:T(8,128)S(1)} %get-tuple-element.43), channel_id=1, source_target_pairs={{1,0},{2,1},{3,2},{4,3},{5,4},{6,5},{7,6},{9,8},{10,9},{11,10},{12... | collective-permute-start | bytes 405512 | tf_op jit(solution)/shard_map/ppermute | solution.py:264
  40.7 7.9 %all-to-all-done.1 = f32[32,4,8,128]{3,2,1,0:T(8,128)S(1)} async-done(((f32[32,4,8,128]{3,2,1,0:T(8,128)}), f32[32,4,8,128]{3,2,1,0:T(8,128)S(1)}, u32[]{:S(2)}, u32[]{:S(2)}) %all-to-all-start.1) | async-done | bytes 524320 | tf_op jit(solution)/shard_map/all_to_all | solution.py:284
  49.5 8.2 %all-to-all-start.2 = ((f32[8,4,8,128]{3,2,1,0:T(8,128)}), f32[8,4,8,128]{3,2,1,0:T(8,128)S(1)}, u32[]{:S(2)}, u32[]{:S(2)}) async-start(f32[8,4,8,128]{3,2,1,0:T(8,128)} %broadcast_in_dim.9), calls=%async_computation.2 | async-start | bytes 262144 | tf_op jit(solution)/shard_map/all_to_all | solution.py:290
  57.7 5.3 %all-to-all-done.2 = f32[8,4,8,128]{3,2,1,0:T(8,128)S(1)} async-done(((f32[8,4,8,128]{3,2,1,0:T(8,128)}), f32[8,4,8,128]{3,2,1,0:T(8,128)S(1)}, u32[]{:S(2)}, u32[]{:S(2)}) %all-to-all-start.2) | async-done | bytes 131104 | tf_op jit(solution)/shard_map/all_to_all | solution.py:290
  63.0 14.2 %shard_map.59 = (f32[5,8,8,384]{3,2,1,0:T(8,128)}, f32[8,8,384]{2,1,0:T(8,128)S(1)}, f32[32,8,128]{2,1,0:T(8,128)S(1)}) custom-call(f32[32,8,128]{2,1,0:T(8,128)S(1)} %bitcast.23, f32[5,8,8,384]{3,2,1,0:T(8,128)S(1)} %copy-done.1, f32[3,8,8,384]{3,2,1,0:T(8,128)S(1)} %copy-done.5, s32[8,8,384]{2,1,0:T(8,128)S(1)} %copy-done.3, ...), custom_call_target="tpu_custom_call" | custom-call | tf_op jit(solution)/shard_map/pallas_call | solution.py:245
  77.2 8.5 %all_to_all.30 = f32[8,4,8,128]{3,2,1,0:T(8,128)S(1)} all-to-all(f32[8,4,8,128]{3,2,1,0:T(8,128)S(1)} %bitcast.26), channel_id=1, replica_groups=mesh['box'=32,'depth'=8] {'depth'}, dimensions={0} | all-to-all | bytes 262144 | tf_op jit(solution)/shard_map/all_to_all | solution.py:282
  86.6 5.0 %all-to-all-start.4 = ((f32[32,4,8,128]{3,2,1,0:T(8,128)}), f32[32,4,8,128]{3,2,1,0:T(8,128)S(1)}, u32[]{:S(2)}, u32[]{:S(2)}) async-start(f32[32,4,8,128]{3,2,1,0:T(8,128)} %broadcast_in_dim.10), calls=%async_computation.4 | async-start | bytes 1048576 | tf_op jit(solution)/shard_map/all_to_all | solution.py:284
  91.7 1.3 collective-permute-start.5
  93.0 4.0 %collective-permute-start.4 = (f32[8,3,384]{2,1,0:T(4,128)S(1)}, f32[8,3,384]{2,1,0:T(4,128)S(1)}, u32[]{:S(2)}, u32[]{:S(2)}) collective-permute-start(f32[8,3,384]{2,1,0:T(4,128)S(1)} %get-tuple-element.28), channel_id=1, source_target_pairs={{0,8},{8,16},{16,24},{24,32},{32,40},{40,48},{48,56},{56,64},{64,7... | collective-permute-start | bytes 110600 | tf_op jit(solution)/shard_map/ppermute | solution.py:259
  97.0 7.7 %collective-permute-done.5.qyhi = f32[8,3,384]{2,1,0:T(4,128)S(1)} collective-permute-done((f32[8,3,384]{2,1,0:T(4,128)S(1)}, f32[8,3,384]{2,1,0:T(4,128)S(1)}, u32[]{:S(2)}, u32[]{:S(2)}) %collective-permute-start.5) | collective-permute-done | bytes 36896 | tf_op jit(solution)/shard_map/ppermute | solution.py:264
  104.7 1.0 all-to-all-done.4
  106.5 8.2 %all-to-all-start.5 = ((f32[8,4,8,128]{3,2,1,0:T(8,128)}), f32[8,4,8,128]{3,2,1,0:T(8,128)S(1)}, u32[]{:S(2)}, u32[]{:S(2)}) async-start(f32[8,4,8,128]{3,2,1,0:T(8,128)} %broadcast_in_dim.11), calls=%async_computation.5 | async-start | bytes 262144 | tf_op jit(solution)/shard_map/all_to_all | solution.py:290
  114.7 3.5 %collective-permute-start.6 = (f32[6,8,384]{2,1,0:T(8,128)S(1)}, f32[6,8,384]{2,1,0:T(8,128)S(1)}, u32[]{:S(2)}, u32[]{:S(2)}) collective-permute-start(f32[6,8,384]{2,1,0:T(8,128)S(1)} %get-tuple-element.42), channel_id=1, source_target_pairs={{0,1},{1,2},{2,3},{3,4},{4,5},{5,6},{6,7},{8,9},{9,10},{10,11},{11... | collective-permute-start | bytes 221192 | tf_op jit(solution)/shard_map/ppermute | solution.py:259
  118.2 1.9 %collective-permute-start.7 = (f32[6,8,384]{2,1,0:T(8,128)S(1)}, f32[6,8,384]{2,1,0:T(8,128)S(1)}, u32[]{:S(2)}, u32[]{:S(2)}) collective-permute-start(f32[6,8,384]{2,1,0:T(8,128)S(1)} %get-tuple-element.41), channel_id=1, source_target_pairs={{1,0},{2,1},{3,2},{4,3},{5,4},{6,5},{7,6},{9,8},{10,9},{11,10},{12... | collective-permute-start | bytes 221192 | tf_op jit(solution)/shard_map/ppermute | solution.py:264
  120.2 3.7 %collective-permute-done.7.qxhi = f32[6,8,384]{2,1,0:T(8,128)S(1)} collective-permute-done((f32[6,8,384]{2,1,0:T(8,128)S(1)}, f32[6,8,384]{2,1,0:T(8,128)S(1)}, u32[]{:S(2)}, u32[]{:S(2)}) %collective-permute-start.7) | collective-permute-done | bytes 73760 | tf_op jit(solution)/shard_map/ppermute | solution.py:264
  123.9 9.5 %shard_map.60 = (f32[8,8,384]{2,1,0:T(8,128)}, f32[5,4096]{1,0:T(8,128)}) custom-call(f32[32,8,128]{2,1,0:T(8,128)S(1)} %bitcast.25, f32[32,8,128]{2,1,0:T(8,128)S(1)} %bitcast.24, f32[8,8,384]{2,1,0:T(8,128)S(1)} %get-tuple-element.10.q, f32[8,3,384]{2,1,0:T(4,128)S(1)} %collective-permute-done.4.qylo, f32[8,3,384]{2,1,0:T(4,128)S(1)} %collective-permute-done.5.qyhi, ...), custom_call_target="tpu_custom_call" | custom-call | tf_op jit(solution)/shard_map/pallas_call | solution.py:245
  (52 shorter events, 5.8 us)
Async XLA Ops:
  0.6 1.0 copy-start
  1.7 0.9 copy-start.2
  2.6 1.0 copy-start.4
  3.5 12.5 %copy-start.1 = (f32[5,8,8,384]{3,2,1,0:T(8,128)S(1)}, f32[5,8,8,384]{3,2,1,0:T(8,128)}, u32[]{:S(2)}) copy-start(f32[5,8,8,384]{3,2,1,0:T(8,128)} %state.3) | copy-start | bytes 1474564
  9.3 6.6 %copy-start.3 = (s32[8,8,384]{2,1,0:T(8,128)S(1)}, s32[8,8,384]{2,1,0:T(8,128)}, u32[]{:S(2)}) copy-start(s32[8,8,384]{2,1,0:T(8,128)} %bins.5) | copy-start | bytes 294916
  9.3 11.9 %all-to-all-start = ((f32[8,4,8,128]{3,2,1,0:T(8,128)}), f32[8,4,8,128]{3,2,1,0:T(8,128)S(1)}, u32[]{:S(2)}, u32[]{:S(2)}) async-start(f32[8,4,8,128]{3,2,1,0:T(8,128)} %bitcast), calls=%async_computation | async-start | bytes 262144 | tf_op jit(solution)/shard_map/all_to_all | solution.py:282
  16.2 18.1 %collective-permute-start = (f32[8,8,384]{2,1,0:T(8,128)S(1)}, f32[8,8,384]{2,1,0:T(8,128)S(1)}, u32[]{:S(2)}, u32[]{:S(2)}) collective-permute-start(f32[8,8,384]{2,1,0:T(8,128)S(1)} %pad_maximum_fusion.4), channel_id=1, source_target_pairs={{0,8},{8,16},{16,24},{24,32},{32,40},{40,48},{48,56},{56,64},{64,7... | collective-permute-start | bytes 294920 | tf_op jit(solution)/shard_map/ppermute | solution.py:259
  19.1 15.2 %collective-permute-start.1 = (f32[8,8,384]{2,1,0:T(8,128)S(1)}, f32[8,8,384]{2,1,0:T(8,128)S(1)}, u32[]{:S(2)}, u32[]{:S(2)}) collective-permute-start(f32[8,8,384]{2,1,0:T(8,128)S(1)} %pad_maximum_fusion.5), channel_id=1, source_target_pairs={{8,0},{16,8},{24,16},{32,24},{40,32},{48,40},{56,48},{64,56},{72,6... | collective-permute-start | bytes 294920 | tf_op jit(solution)/shard_map/ppermute | solution.py:264
  22.2 26.4 %all-to-all-start.1 = ((f32[32,4,8,128]{3,2,1,0:T(8,128)}), f32[32,4,8,128]{3,2,1,0:T(8,128)S(1)}, u32[]{:S(2)}, u32[]{:S(2)}) async-start(f32[32,4,8,128]{3,2,1,0:T(8,128)} %broadcast_in_dim.8), calls=%async_computation.1 | async-start | bytes 1048576 | tf_op jit(solution)/shard_map/all_to_all | solution.py:284
  34.4 23.3 %collective-permute-start.2 = (f32[11,8,384]{2,1,0:T(8,128)S(1)}, f32[11,8,384]{2,1,0:T(8,128)S(1)}, u32[]{:S(2)}, u32[]{:S(2)}) collective-permute-start(f32[11,8,384]{2,1,0:T(8,128)S(1)} %get-tuple-element.44), channel_id=1, source_target_pairs={{0,1},{1,2},{2,3},{3,4},{4,5},{5,6},{6,7},{8,9},{9,10},{10,11},{11... | collective-permute-start | bytes 405512 | tf_op jit(solution)/shard_map/ppermute | solution.py:259
  38.8 18.9 %collective-permute-start.3 = (f32[11,8,384]{2,1,0:T(8,128)S(1)}, f32[11,8,384]{2,1,0:T(8,128)S(1)}, u32[]{:S(2)}, u32[]{:S(2)}) collective-permute-start(f32[11,8,384]{2,1,0:T(8,128)S(1)} %get-tuple-element.43), channel_id=1, source_target_pairs={{1,0},{2,1},{3,2},{4,3},{5,4},{6,5},{7,6},{9,8},{10,9},{11,10},{12... | collective-permute-start | bytes 405512 | tf_op jit(solution)/shard_map/ppermute | solution.py:264
  48.7 14.3 %copy-start.5 = (f32[3,8,8,384]{3,2,1,0:T(8,128)S(1)}, f32[3,8,8,384]{3,2,1,0:T(8,128)}, u32[]{:S(2)}) copy-start(f32[3,8,8,384]{3,2,1,0:T(8,128)} %velocity.3) | copy-start | bytes 884740
  49.5 13.4 %all-to-all-start.2 = ((f32[8,4,8,128]{3,2,1,0:T(8,128)}), f32[8,4,8,128]{3,2,1,0:T(8,128)S(1)}, u32[]{:S(2)}, u32[]{:S(2)}) async-start(f32[8,4,8,128]{3,2,1,0:T(8,128)} %broadcast_in_dim.9), calls=%async_computation.2 | async-start | bytes 262144 | tf_op jit(solution)/shard_map/all_to_all | solution.py:290
  86.6 19.0 %all-to-all-start.4 = ((f32[32,4,8,128]{3,2,1,0:T(8,128)}), f32[32,4,8,128]{3,2,1,0:T(8,128)S(1)}, u32[]{:S(2)}, u32[]{:S(2)}) async-start(f32[32,4,8,128]{3,2,1,0:T(8,128)} %broadcast_in_dim.10), calls=%async_computation.4 | async-start | bytes 1048576 | tf_op jit(solution)/shard_map/all_to_all | solution.py:284
  91.7 13.0 %collective-permute-start.5 = (f32[8,3,384]{2,1,0:T(4,128)S(1)}, f32[8,3,384]{2,1,0:T(4,128)S(1)}, u32[]{:S(2)}, u32[]{:S(2)}) collective-permute-start(f32[8,3,384]{2,1,0:T(4,128)S(1)} %get-tuple-element.27), channel_id=1, source_target_pairs={{8,0},{16,8},{24,16},{32,24},{40,32},{48,40},{56,48},{64,56},{72,6... | collective-permute-start | bytes 110600 | tf_op jit(solution)/shard_map/ppermute | solution.py:264
  93.0 11.7 %collective-permute-start.4 = (f32[8,3,384]{2,1,0:T(4,128)S(1)}, f32[8,3,384]{2,1,0:T(4,128)S(1)}, u32[]{:S(2)}, u32[]{:S(2)}) collective-permute-start(f32[8,3,384]{2,1,0:T(4,128)S(1)} %get-tuple-element.28), channel_id=1, source_target_pairs={{0,8},{8,16},{16,24},{24,32},{32,40},{40,48},{48,56},{56,64},{64,7... | collective-permute-start | bytes 110600 | tf_op jit(solution)/shard_map/ppermute | solution.py:259
  106.5 17.4 %all-to-all-start.5 = ((f32[8,4,8,128]{3,2,1,0:T(8,128)}), f32[8,4,8,128]{3,2,1,0:T(8,128)S(1)}, u32[]{:S(2)}, u32[]{:S(2)}) async-start(f32[8,4,8,128]{3,2,1,0:T(8,128)} %broadcast_in_dim.11), calls=%async_computation.5 | async-start | bytes 262144 | tf_op jit(solution)/shard_map/all_to_all | solution.py:290
  114.7 5.5 %collective-permute-start.6 = (f32[6,8,384]{2,1,0:T(8,128)S(1)}, f32[6,8,384]{2,1,0:T(8,128)S(1)}, u32[]{:S(2)}, u32[]{:S(2)}) collective-permute-start(f32[6,8,384]{2,1,0:T(8,128)S(1)} %get-tuple-element.42), channel_id=1, source_target_pairs={{0,1},{1,2},{2,3},{3,4},{4,5},{5,6},{6,7},{8,9},{9,10},{10,11},{11... | collective-permute-start | bytes 221192 | tf_op jit(solution)/shard_map/ppermute | solution.py:259
  118.2 5.7 %collective-permute-start.7 = (f32[6,8,384]{2,1,0:T(8,128)S(1)}, f32[6,8,384]{2,1,0:T(8,128)S(1)}, u32[]{:S(2)}, u32[]{:S(2)}) collective-permute-start(f32[6,8,384]{2,1,0:T(8,128)S(1)} %get-tuple-element.41), channel_id=1, source_target_pairs={{1,0},{2,1},{3,2},{4,3},{5,4},{6,5},{7,6},{9,8},{10,9},{11,10},{12... | collective-permute-start | bytes 221192 | tf_op jit(solution)/shard_map/ppermute | solution.py:264

commit v2 on v1

v2 whole, which is shorter than its diff:
```python
import math

import jax
import jax.numpy as jnp
import numpy as np
from jax import lax
from jax.experimental import pallas as pl
from jax.experimental.pallas import tpu as pltpu
from jax.sharding import PartitionSpec as P

NBINS = 4096
COURANT = 0.8
OMEGA_RELAX = 0.8
DIAGONAL = 6.1
WEIGHTS = (1.0, 0.5, -0.5, 0.25, 0.75)
NF = 5
X, Y, Z = 8, 8, 384
TILES = NBINS // 128
SW, BN, VE, CSW, CBN, CVE, PLANES = 5, 9, 13, 22, 25, 28, 34
TALL = 24
MEMBERS = 16
F32, BF16 = jnp.float32, jnp.bfloat16


def pieces_of(values):
    upper = values.astype(BF16).astype(F32)
    rest = values - upper
    middle = rest.astype(BF16).astype(F32)
    return upper, middle, rest - middle


def lo_table(lo_row):
    wide = jnp.broadcast_to(lo_row, (16, Z)).astype(BF16)
    row = lax.broadcasted_iota(jnp.int32, (16, Z), 0).astype(F32).astype(BF16)
    one, zero = jnp.ones((16, Z), BF16), jnp.zeros((16, Z), BF16)
    return jnp.concatenate([jnp.where(wide == row + jnp.asarray(16 * k, BF16), one, zero) for k in range(16)], axis=0)


def hi_rows(hi_row, rows16):
    wide = jnp.broadcast_to(hi_row, (16, Z)).astype(BF16)
    zero = jnp.zeros((16, Z), BF16)
    return jnp.concatenate([jnp.where(wide == jnp.asarray(k, BF16), rows16, zero) for k in range(16)], axis=0)


def put_rows(rows, p, values):
    for j in range(3):
        rows[j, pl.ds(p, Y, stride=16), :] = values[:, j * 128 : (j + 1) * 128]


def get_rows(rows, y):
    return jnp.concatenate([rows[j, pl.ds(16 * y, 16), :].astype(BF16) for j in range(3)], axis=1)


def get_field(lifted, x, f):
    return jnp.concatenate([lifted[x, j, pl.ds(f, Y, stride=8), :] for j in range(3)], axis=1)


def add_bins(acc, rows, hi, lo, x):
    left, right = [], []
    for y in range(Y):
        left.append(hi_rows(hi[x, pl.ds(y, 1), :], get_rows(rows, y)))
        right.append(lo_table(lo[x, pl.ds(y, 1), :]))
    acc[...] += lax.dot_general(
        jnp.concatenate(left, 1), jnp.concatenate(right, 1), (((1,), (1,)), ((), ())), preferred_element_type=F32
    )


def put_sums(out, acc, extra):
    for k in range(16):
        s = acc[pl.ds(16 * k, 16), :]
        tile = jnp.concatenate([s[0:5] + s[5:10] + s[10:15], s[15:16], extra], axis=0)
        out[2 * k] = tile[:, :128]
        out[2 * k + 1] = tile[:, 128:]


def split_bins(bins, hi, lo):
    b = bins[...]
    hi[...] = lax.shift_right_logical(b, 8).astype(F32)
    lo[...] = (b & 255).astype(F32)


def sums_kernel(
    state_in, velocity_in, bins_in, to_above, to_below, weighted, shifted, out, hi, lo, rows, acc, state, velocity, bins, sems, more_sems
):
    bins_copy = pltpu.make_async_copy(bins_in, bins, more_sems.at[0])
    bins_copy.start()
    copies = [
        [pltpu.make_async_copy(state_in.at[f, pl.ds(4 * h, 4)], state.at[f, pl.ds(4 * h, 4)], sems.at[h, f]) for f in range(NF)]
        for h in range(2)
    ]
    speed_copies = [pltpu.make_async_copy(velocity_in.at[d], velocity.at[d], more_sems.at[1 + d]) for d in range(3)]
    for copy in copies[0] + speed_copies + copies[1]:
        copy.start()
    acc[...] = jnp.zeros_like(acc)
    put_rows(rows, 15, jnp.ones((Y, Z), F32))
    bins_copy.wait()
    split_bins(bins, hi, lo)

    def step(x, top):
        s = [state[f, x] for f in range(NF)]
        w = WEIGHTS[0] * s[0]
        for f in range(NF):
            for i, piece in enumerate(pieces_of(s[f])):
                put_rows(rows, NF * i + f, piece)
            if f > 0:
                w += WEIGHTS[f] * s[f]
        add_bins(acc, rows, hi, lo, x)
        weighted[x] = w
        b = bins[x].astype(F32) + 1.0
        shifted[x] = b
        v = [velocity[d, x] for d in range(3)]
        for face, near, four, three in ((to_above, Y - 1, Y - 4, Y - 3), (to_below, 0, 0, 0)):
            parts = [c[near : near + 1] for c in s] + [w[four : four + 4], b[four : four + 4]]
            parts += [c[three : three + 3] for c in v] + [jnp.zeros((2, Z), F32)]
            face[x] = jnp.concatenate(parts, axis=0)
        return jnp.maximum(top, jnp.abs(v[0]) + jnp.abs(v[1]) + jnp.abs(v[2]))

    top = jnp.zeros((Y, Z), F32)
    for h in range(2):
        for copy in copies[h] + (speed_copies if h == 0 else []):
            copy.wait()
        top = lax.fori_loop(4 * h, 4 * h + 4, step, top)
    put_sums(out, acc, jnp.full((2, 256), jnp.max(top), F32))


def pack_x_kernel(state, velocity, weighted, shifted, ylo, yhi, to_above, to_below, corners, sems):
    copies = []
    for side, (out, near, four, three) in enumerate(((to_above, X - 1, X - 4, X - 3), (to_below, 0, 0, 0))):
        parts = [(state.at[:, near], 0, NF), (weighted.at[pl.ds(four, 4)], SW, 4), (shifted.at[pl.ds(four, 4)], BN, 4)]
        parts += [(velocity.at[d, pl.ds(three, 3)], VE + 3 * d, 3) for d in range(3)]
        for i, (src, at, n) in enumerate(parts):
            copies.append(pltpu.make_async_copy(src, out.at[pl.ds(at, n)], sems.at[side, i]))
    for copy in copies:
        copy.start()
    gap = jnp.zeros((1, Z), F32)
    for side, (out, three, two) in enumerate(((to_above, X - 3, X - 2), (to_below, 0, 0))):
        for i in range(3):
            x = three + i
            for at, row in ((CSW, SW), (CBN, BN)):
                corners[side, at - CSW + i] = jnp.concatenate([ylo[x, row : row + 4], yhi[x, row : row + 4]], axis=0)
        for i in range(2):
            x = two + i
            for d in range(3):
                row = VE + 3 * d
                corners[side, CVE - CSW + 2 * d + i] = jnp.concatenate(
                    [ylo[x, row : row + 3], gap, yhi[x, row : row + 3], gap], axis=0
                )
        copies.append(pltpu.make_async_copy(corners.at[side], out.at[pl.ds(CSW, PLANES - CSW)], sems.at[side, 6]))
        copies[-1].start()
    for copy in copies:
        copy.wait()


def lift_row(table, hi_row, lo_row):
    found = lax.dot_general(table, lo_table(lo_row), (((1,), (0,)), ((), ())), preferred_element_type=F32)
    wide = jnp.broadcast_to(hi_row, (16, Z))
    acc = jnp.zeros((16, Z), F32)
    for k in range(16):
        acc = jnp.where(wide == float(k), found[16 * k : 16 * k + 16], acc)
    total = acc[0:5] + acc[5:10] + acc[10:15]
    return jnp.concatenate([total, jnp.zeros((3, Z), F32)], axis=0)


def lift_five(first, b):
    index = b.astype(jnp.int32)
    parts = [[] for f in range(NF)]
    for j in range(3):
        cut = index[:, 128 * j : 128 * j + 128]
        tile, lane = lax.shift_right_arithmetic(cut, 7), cut & 127
        found = [jnp.zeros((8, 128), F32)] * NF
        for t in range(TILES):
            here = tile == t
            for f in range(NF):
                row = jnp.broadcast_to(first[t, f : f + 1, :], (8, 128))
                found[f] = jnp.where(here, jnp.take_along_axis(row, lane, axis=1), found[f])
        for f in range(NF):
            parts[f].append(found[f])
    return [jnp.concatenate(part, axis=1) for part in parts]


def step_kernel(
    first, state, velocity, bins, ylo, yhi, xlo, xhi, new_state_out, near_out, out,
    hi, lo, face_bins, face_lift, table, lifted, p, rows, acc, new_state, near_p, sems
):
    for k in range(16):
        pair = jnp.concatenate([first[2 * k], first[2 * k + 1]], axis=1)
        u, m, l = pieces_of(pair)
        block = jnp.concatenate([u[0:5], m[0:5], l[0:5], jnp.zeros((1, 256), F32)], axis=0)
        table[pl.ds(16 * k, 16), :] = block.astype(BF16)
    tab = table[...]
    time_step = COURANT / (1.0 + jnp.max(first[0, 6:7, :]))
    split_bins(bins, hi, lo)
    for x in range(X):
        face_bins[0, x : x + 1, :] = ylo[x, BN + 3 : BN + 4, :] - 1.0
        face_bins[1, x : x + 1, :] = yhi[x, BN : BN + 1, :] - 1.0
    face_bins[2] = xlo[BN + 3] - 1.0
    face_bins[3] = xhi[BN] - 1.0

    def lift_some(i, carry):
        for k in range(2):
            x = 2 * i + k
            for y in range(Y):
                eight = lift_row(tab, hi[x, pl.ds(y, 1), :], lo[x, pl.ds(y, 1), :])
                for j in range(3):
                    lifted[x, j, pl.ds(8 * y, 8), :] = eight[:, 128 * j : 128 * j + 128]
        for f, value in enumerate(lift_five(first, face_bins[i])):
            face_lift[i, f] = value
        for k in range(2):
            x = 2 * i + k
            for f in range(NF):
                p[f, x + 1, pl.ds(8, 8), :] = state[f, x] - get_field(lifted, x, f)
        return carry

    lax.fori_loop(0, 4, lift_some, 0)
    for f in range(NF):
        p[f, 0, pl.ds(8, 8), :] = xlo[f] - face_lift[2, f]
        p[f, X + 1, pl.ds(8, 8), :] = xhi[f] - face_lift[3, f]
        for x in range(X):
            p[f, x + 1, 7:8, :] = ylo[x, f : f + 1, :] - face_lift[0, f, x : x + 1, :]
            p[f, x + 1, 16:17, :] = yhi[x, f : f + 1, :] - face_lift[1, f, x : x + 1, :]

    acc[...] = jnp.zeros_like(acc)
    lane = lax.broadcasted_iota(jnp.int32, (Y, Z), 1)
    put_rows(rows, 15, jnp.zeros((Y, Z), F32))

    def advect(x, carry):
        v = [velocity[d, x] for d in range(3)]
        up = [jnp.maximum(c, 0.0) for c in v]
        down = [jnp.minimum(c, 0.0) for c in v]
        for f in range(NF):
            c = p[f, x + 1, pl.ds(8, 8), :]
            before = jnp.where(lane == 0, 0.0, pltpu.roll(c, 1, 1))
            after = jnp.where(lane == Z - 1, 0.0, pltpu.roll(c, Z - 1, 1))
            change = up[0] * (c - p[f, x, pl.ds(8, 8), :]) + down[0] * (p[f, x + 2, pl.ds(8, 8), :] - c)
            change += up[1] * (c - p[f, x + 1, pl.ds(7, 8), :]) + down[1] * (p[f, x + 1, pl.ds(9, 8), :] - c)
            change += up[2] * (c - before) + down[2] * (after - c)
            moved = c - time_step * change
            new_state[f, x] = get_field(lifted, x, f) + moved
            for i, piece in enumerate(pieces_of(moved)):
                put_rows(rows, NF * i + f, piece)
        state_copy(x).start()
        add_bins(acc, rows, hi, lo, x)
        return carry

    def state_copy(x):
        return pltpu.make_async_copy(new_state.at[:, x], new_state_out.at[:, x], sems.at[x])


    def gather_p(x, carry):
        total = WEIGHTS[0] * p[0, x]
        for f in range(1, NF):
            total += WEIGHTS[f] * p[f, x]
        near_p[x] = total
        return carry

    lax.fori_loop(0, X + 2, gather_p, 0)
    near_copy = pltpu.make_async_copy(near_p, near_out, sems.at[X])
    near_copy.start()
    lax.fori_loop(0, X, advect, 0)
    put_sums(out, acc, jnp.zeros((2, 256), F32))
    for x in range(X):
        state_copy(x).wait()
    near_copy.wait()


def weighted_rows(tiles):
    total = jnp.zeros((TILES, 128), F32)
    for f in range(NF):
        total += WEIGHTS[f] * tiles[:, f, :]
    return total


def row_table(total, pieces):
    return jnp.concatenate(pieces_of(total)[:pieces], axis=0).astype(BF16)


def lift_one(tab, b):
    high = jnp.floor(b * (1.0 / 128.0))
    low = b - 128.0 * high
    row = lax.broadcasted_iota(jnp.int32, (TILES, Z), 0).astype(F32)
    row16 = lax.broadcasted_iota(jnp.int32, (16, Z), 0).astype(F32).astype(BF16)
    one, zero = jnp.ones((16, Z), BF16), jnp.zeros((16, Z), BF16)
    wide = jnp.broadcast_to(low, (16, Z)).astype(BF16)
    t = jnp.concatenate([jnp.where(wide == row16 + jnp.asarray(16 * k, BF16), one, zero) for k in range(8)], axis=0)
    found = lax.dot_general(tab, t, (((1,), (0,)), ((), ())), preferred_element_type=F32)
    total = found[0:TILES]
    for i in range(1, tab.shape[0] // TILES):
        total += found[TILES * i : TILES * i + TILES]
    return jnp.sum(jnp.where(jnp.broadcast_to(high, (TILES, Z)) == row, total, 0.0), axis=0, keepdims=True)


def lift_eight(table, b):
    index = b.astype(jnp.int32)
    parts = []
    for j in range(3):
        cut = index[:, 128 * j : 128 * j + 128]
        tile, lane = lax.shift_right_arithmetic(cut, 7), cut & 127
        found = jnp.zeros((8, 128), F32)
        for t in range(TILES):
            row = jnp.broadcast_to(table[t : t + 1, :], (8, 128))
            found = jnp.where(tile == t, jnp.take_along_axis(row, lane, axis=1), found)
        parts.append(found)
    return jnp.concatenate(parts, axis=1)


def reach_rows(far):
    near = {0: range(7, 17), 1: range(8, 16)}
    return {d: [y for y in range(8 - far + d, 16 + far - d) if y not in near.get(d, ())] for d in range(far + 1)}


def ring_kernel(
    first, near_p, shifted, velocity, ylo, yhi, xlo, xhi, q_out, bins_out, p, q, high, v, faces, flat, sems, v_sems, out_sems
):
    blocks = [
        (near_p, p.at[pl.ds(3, 10)]),
        (xlo.at[pl.ds(SW, 3)], p.at[pl.ds(0, 3), pl.ds(8, 8)]),
        (xhi.at[pl.ds(SW + 1, 3)], p.at[pl.ds(13, 3), pl.ds(8, 8)]),
        (shifted, high.at[pl.ds(4, 8), pl.ds(8, 8)]),
        (xlo.at[pl.ds(BN, 4)], high.at[pl.ds(0, 4), pl.ds(8, 8)]),
        (xhi.at[pl.ds(BN, 4)], high.at[pl.ds(12, 4), pl.ds(8, 8)]),
        (ylo, faces.at[0, pl.ds(0, 8)]),
        (yhi, faces.at[1, pl.ds(0, 8)]),
        (xlo.at[pl.ds(CSW, 12)], faces.at[2, pl.ds(0, 12), pl.ds(0, 8)]),
        (xhi.at[pl.ds(CSW, 12)], faces.at[3, pl.ds(0, 12), pl.ds(0, 8)]),
    ]
    early = [pltpu.make_async_copy(src, dst, sems.at[i]) for i, (src, dst) in enumerate(blocks)]
    late = []
    for d in range(3):
        parts = ((velocity.at[d], 3, 8), (xlo.at[pl.ds(VE + 3 * d, 3)], 0, 3), (xhi.at[pl.ds(VE + 3 * d, 3)], 11, 3))
        for i, (src, at, n) in enumerate(parts):
            late.append(pltpu.make_async_copy(src, v.at[d, pl.ds(at, n), pl.ds(8, 8)], v_sems.at[d, i]))
    for copy in early + late:
        copy.start()
    flat[...] = weighted_rows(first)
    tab = row_table(flat[...], 3)
    for copy in early:
        copy.wait()
    below, above, left, right = (faces.at[i] for i in range(4))
    p[pl.ds(4, 8), 4:7, :] = below[0:8, SW : SW + 3, :]
    p[pl.ds(4, 8), 17:20, :] = above[0:8, SW + 1 : SW + 4, :]
    high[pl.ds(4, 8), 4:8, :] = below[0:8, BN : BN + 4, :]
    high[pl.ds(4, 8), 16:20, :] = above[0:8, BN : BN + 4, :]
    for dst, corner in ((p, 0), (high, CBN - CSW)):
        for ref, at in ((left, 1), (right, 12)):
            dst[pl.ds(at, 3), 4:8, :] = ref[pl.ds(corner, 3), 0:4, :]
            dst[pl.ds(at, 3), 16:20, :] = ref[pl.ds(corner, 3), 4:8, :]
    bins_copy = pltpu.make_async_copy(high, bins_out, out_sems.at[0])
    bins_copy.start()
    rows = reach_rows(4)

    def lift_x(x, rows, block):
        if block:
            p[x, 8:16, :] = p[x, 8:16, :] - lift_eight(flat, high[x, 8:16, :] - 1.0)
        for y in rows:
            p[x, y : y + 1, :] = p[x, y : y + 1, :] - lift_one(tab, high[x, y : y + 1, :] - 1.0)

    def lift_sides(side, carry):
        for d in range(2, 5):
            lift_x((4 - d) + side * (7 + 2 * d), [y for y in rows[d] if not 8 <= y < 16], True)
        lift_x(3 + side * 9, rows[1], False)
        for i in range(4):
            lift_x(4 + 4 * side + i, rows[0], False)
        return carry

    lax.fori_loop(0, 2, lift_sides, 0)
    for copy in late:
        copy.wait()
    for d in range(3):
        row, corner = VE + 3 * d, CVE - CSW + 2 * d
        v[d, pl.ds(3, 8), 5:8, :] = below[0:8, row : row + 3, :]
        v[d, pl.ds(3, 8), 16:19, :] = above[0:8, row : row + 3, :]
        for ref, at in ((left, 1), (right, 11)):
            v[d, pl.ds(at, 2), 5:8, :] = ref[pl.ds(corner, 2), 0:3, :]
            v[d, pl.ds(at, 2), 16:19, :] = ref[pl.ds(corner, 2), 4:7, :]
    time_step = COURANT / (1.0 + jnp.max(first[0, 6:7, :]))
    lane = lax.broadcasted_iota(jnp.int32, (TALL, Z), 1)

    def step(x, carry):
        c = p[x + 1]
        sides = (
            (p[x], p[x + 2]),
            (pltpu.roll(c, 1, 0), pltpu.roll(c, TALL - 1, 0)),
            (jnp.where(lane == 0, 0.0, pltpu.roll(c, 1, 1)), jnp.where(lane == Z - 1, 0.0, pltpu.roll(c, Z - 1, 1))),
        )
        change = jnp.zeros((TALL, Z), F32)
        for d, (before, after) in enumerate(sides):
            change += jnp.maximum(v[d, x], 0.0) * (c - before) + jnp.minimum(v[d, x], 0.0) * (after - c)
        q[x] = c - time_step * change
        return carry

    lax.fori_loop(0, 14, step, 0)
    q_copy = pltpu.make_async_copy(q, q_out, out_sems.at[1])
    q_copy.start()
    q_copy.wait()
    bins_copy.wait()


def relax_kernel(second, first, q_in, bins_in, potential, profile, src, high, pot, flat, sems):
    halves = []
    for h in range(2):
        at = pl.ds(3 + 4 * h, 4)
        bins_at = pl.ds(4 + 4 * h, 4)
        halves.append((q_in.at[at], src.at[at], bins_in.at[bins_at], high.at[bins_at]))
    for at, n in ((0, 3), (11, 3)):
        bins_at = pl.ds(at + 1, n)
        halves.append((q_in.at[pl.ds(at, n)], src.at[pl.ds(at, n)], bins_in.at[bins_at], high.at[bins_at]))
    copies = [
        [pltpu.make_async_copy(parts[2 * i], parts[2 * i + 1], sems.at[h, i]) for i in range(2)] for h, parts in enumerate(halves)
    ]
    for pair in copies:
        for copy in pair:
            copy.start()
    flat[...] = weighted_rows(second)
    tab = row_table(flat[...], 2)
    for t in range(TILES):
        profile[:, 128 * t : 128 * t + 128] = (first[t] + second[t])[0:NF]

    def lift_x(x, rows, block):
        if block:
            src[x, 8:16, :] = src[x, 8:16, :] - lift_eight(flat, high[x + 1, 8:16, :] - 1.0)
        for y in rows:
            src[x, y : y + 1, :] = src[x, y : y + 1, :] - lift_one(tab, high[x + 1, y : y + 1, :] - 1.0)
        scaled = src[x] * (OMEGA_RELAX / DIAGONAL)
        src[x] = scaled
        pot[0, x] = scaled

    def lift_sides(side, carry):
        for d in range(1, 4):
            rows = [y for y in range(5 + d, 19 - d) if d == 3 or not 8 <= y < 16]
            lift_x((3 - d) + side * (7 + 2 * d), rows, d < 3)
        return carry

    for h in range(2):
        for copy in copies[h]:
            copy.wait()
        lax.fori_loop(3 + 4 * h, 7 + 4 * h, lambda x, c: (lift_x(x, (5, 6, 7, 16, 17, 18), True), c)[1], 0)
    for pair in copies[2:]:
        for copy in pair:
            copy.wait()
    lax.fori_loop(0, 2, lift_sides, 0)
    lane = lax.broadcasted_iota(jnp.int32, (TALL, Z), 1)
    for s in range(1, 4):
        now, later = (s + 1) % 2, s % 2

        def sweep(x, carry):
            c = pot[now, x]
            near = pot[now, x - 1] + pot[now, x + 1]
            near += pltpu.roll(c, 1, 0) + pltpu.roll(c, TALL - 1, 0)
            near += jnp.where(lane == 0, 0.0, pltpu.roll(c, 1, 1)) + jnp.where(lane == Z - 1, 0.0, pltpu.roll(c, Z - 1, 1))
            new = (1.0 - OMEGA_RELAX) * c + (src[x] + (OMEGA_RELAX / DIAGONAL) * near)
            if s < 3:
                pot[later, x] = jnp.where(high[x + 1] < 0.5, 0.0, new)
            else:
                potential[x - 3] = new[8:16]
            return carry

        lax.fori_loop(s, 14 - s, sweep, 0)


def f32_like(*shape):
    return jax.ShapeDtypeStruct(shape, F32)


def call(kernel, plan, *args):
    micros, out_shape, scratch, more = plan
    more = dict(more)
    limit = more.pop("megabytes") * 1024 * 1024
    return pl.pallas_call(
        kernel,
        out_shape=out_shape,
        cost_estimate=pl.CostEstimate(flops=micros * 1_000_000_000, bytes_accessed=0, transcendentals=0),
        scratch_shapes=[pltpu.VMEM(*part) if isinstance(part, tuple) else part for part in scratch],
        compiler_params=pltpu.CompilerParams(vmem_limit_bytes=limit),
        **more,
    )(*args)


def from_below(face, axis):
    count = lax.axis_size(axis)
    return lax.ppermute(face, axis, [(i, i + 1) for i in range(count - 1)])


def from_above(face, axis):
    count = lax.axis_size(axis)
    return lax.ppermute(face, axis, [(i + 1, i) for i in range(count - 1)])


def added(tiles):
    total, top = tiles[0], tiles[0]
    for i in range(1, MEMBERS):
        total, top = total + tiles[i], jnp.maximum(top, tiles[i])
    return jnp.where(lax.broadcasted_iota(jnp.int32, total.shape, 1) == 6, top, total)


def merge_kernel(tiles, share, copies):
    total = added(tiles)
    share[...] = total
    for i in range(MEMBERS):
        copies[i] = total


def divide_kernel(tiles, counts, share, copies):
    total = added(tiles)
    cells = total if counts is None else counts
    row = lax.broadcasted_iota(jnp.int32, total.shape, 1)
    mean = jnp.where(row < NF, total / jnp.maximum(cells[:, 5:6, :], 1.0), total)
    share[...] = total
    for i in range(MEMBERS):
        copies[i] = mean


def divide_own_kernel(tiles, share, copies):
    divide_kernel(tiles, None, share, copies)


def groups_of(varied):
    sizes = (4, 8, 4, 2)
    fixed = [d for d in range(4) if d not in varied]
    places = np.arange(256).reshape(sizes).transpose(fixed + list(varied))
    return places.reshape(-1, math.prod(sizes[d] for d in varied)).tolist()


SHARE_GROUPS = groups_of((0, 2))
OTHER_GROUPS = groups_of((1, 3))
def swap(parts, groups):
    return lax.all_to_all(parts, ("box", "depth"), 0, 0, axis_index_groups=groups, tiled=True)


def in_members(tiles):
    return tiles.reshape(MEMBERS, TILES // MEMBERS, 8, 128)


VISIBLE = pl.BlockSpec(memory_space=pltpu.VMEM)
REMOTE = pl.BlockSpec(memory_space=pl.ANY)
SUMS = (
    7,
    (f32_like(X, TALL, Z), f32_like(X, TALL, Z), f32_like(X, Y, Z), f32_like(X, Y, Z), f32_like(TILES, 8, 128)),
    [
        ((X, Y, Z), F32), ((X, Y, Z), F32), ((3, Y * 16, 128), F32), ((256, 256), F32),
        ((NF, X, Y, Z), F32), ((3, X, Y, Z), F32), ((X, Y, Z), jnp.int32),
        pltpu.SemaphoreType.DMA((2, NF)), pltpu.SemaphoreType.DMA((4,)),
    ],
    dict(in_specs=[REMOTE] * 3, megabytes=58),
)
PACK_X = (
    2,
    (f32_like(PLANES, Y, Z), f32_like(PLANES, Y, Z)),
    [((2, PLANES - CSW, Y, Z), F32), pltpu.SemaphoreType.DMA((2, 7))],
    dict(in_specs=[REMOTE] * 4 + [VISIBLE] * 2, out_specs=(REMOTE, REMOTE), megabytes=20),
)
STEP = (
    14,
    (f32_like(NF, X, Y, Z), f32_like(X + 2, TALL, Z), f32_like(TILES, 8, 128)),
    [
        ((X, Y, Z), F32), ((X, Y, Z), F32), ((4, Y, Z), F32), ((4, NF, Y, Z), F32), ((256, 256), BF16),
        ((X, 3, 64, 128), F32), ((NF, X + 2, TALL, Z), F32), ((3, Y * 16, 128), F32), ((256, 256), F32),
        ((NF, X, Y, Z), F32), ((X + 2, TALL, Z), F32), pltpu.SemaphoreType.DMA((X + 1,)),
    ],
    dict(out_specs=(REMOTE, REMOTE, VISIBLE), megabytes=24),
)
RING = (
    8,
    (f32_like(14, TALL, Z), f32_like(16, TALL, Z)),
    [
        ((16, TALL, Z), F32), ((14, TALL, Z), F32), ((16, TALL, Z), F32), ((3, 14, TALL, Z), F32), ((4, 12, TALL, Z), F32), ((TILES, 128), F32),
        pltpu.SemaphoreType.DMA((10,)), pltpu.SemaphoreType.DMA((3, 3)), pltpu.SemaphoreType.DMA((2,)),
    ],
    dict(in_specs=[VISIBLE] + [REMOTE] * 7, out_specs=(REMOTE, REMOTE), megabytes=58),
)
RELAX = (
    9,
    (f32_like(X, Y, Z), f32_like(NF, NBINS)),
    [((14, TALL, Z), F32), ((16, TALL, Z), F32), ((2, 14, TALL, Z), F32), ((TILES, 128), F32), pltpu.SemaphoreType.DMA((4, 2))],
    dict(in_specs=[VISIBLE] * 2 + [REMOTE] * 2, megabytes=58),
)


MERGE = (1, (f32_like(2, 8, 128), f32_like(MEMBERS, 2, 8, 128)), [], dict(megabytes=20))


def per_device(state, velocity, bins):
    to_above, to_below, weighted, shifted, tiles = call(sums_kernel, SUMS, state, velocity, bins)
    ylo = from_below(to_above, "box")
    yhi = from_above(to_below, "box")
    to_above, to_below = call(pack_x_kernel, PACK_X, state, velocity, weighted, shifted, ylo, yhi)
    xlo = from_below(to_above, "depth")
    xhi = from_above(to_below, "depth")
    share, copies = call(merge_kernel, MERGE, swap(in_members(tiles), SHARE_GROUPS))
    share, copies = call(divide_own_kernel, MERGE, swap(copies, OTHER_GROUPS))
    first = swap(copies, SHARE_GROUPS).reshape(TILES, 8, 128)
    new_state, near_p, tiles = call(step_kernel, STEP, first, state, velocity, bins, ylo, yhi, xlo, xhi)
    q, wide_bins = call(ring_kernel, RING, first, near_p, shifted, velocity, ylo, yhi, xlo, xhi)
    part, copies = call(merge_kernel, MERGE, swap(in_members(tiles), SHARE_GROUPS))
    copies, q, wide_bins = lax.optimization_barrier((copies, q, wide_bins))
    part, copies = call(divide_kernel, MERGE, swap(copies, OTHER_GROUPS), share)
    second = swap(copies, SHARE_GROUPS).reshape(TILES, 8, 128)
    potential, profile = call(relax_kernel, RELAX, second, first, q, wide_bins)
    return (new_state, potential, profile)


def solution(mesh):
    return jax.shard_map(
        per_device,
        mesh=mesh,
        in_specs=(
            P(None, "depth", "box", None),
            P(None, "depth", "box", None),
            P("depth", "box", None),
        ),
        out_specs=(P(None, "depth", "box", None), P("depth", "box", None), P()),
        check_vma=False,
    )
```

time: 134 us -> 123 us (0.918)
  blocking collectives: 8.51 us -> 57.4 us
  starting transfers between devices: 61.2 us -> 21.9 us
  waiting for transfers between devices: 26.5 us -> 3.56 us
  Pallas kernels: 29.4 us -> 38 us
  local copies, waits for them, and re-layouts: 6.19 us -> 0.77 us
    all_to_all x1 -> x4, blocking collectives: 8.51 us -> 57.4 us  [swap(): lax.all_to_all(parts, ('box', 'depth'), 0, 0, axis_index_groups=groups, t...]
    all_to_all x5 -> x2, starting transfers between devices: 40 us -> 11.9 us  [swap(): lax.all_to_all(parts, ('box', 'depth'), 0, 0, axis_index_groups=groups, t...]
    all_to_all x5 -> x2, waiting for transfers between devices: 15.1 us -> 3.55 us  [swap(): lax.all_to_all(parts, ('box', 'depth'), 0, 0, axis_index_groups=groups, t...]
    ppermute x4 -> x2, waiting for transfers between devices: 11.4 us -> 0.01 us  [from_above(): return lax.ppermute(face, axis, [(i + 1, i) for i in range(count - 1)])]
    pallas_call x3 -> x9, Pallas kernels: 29.4 us -> 38 us  [call(): pl.pallas_call(kernel, out_shape=out_shape, cost_estimate=pl.CostEstimate...]
    ppermute x4 -> x2, starting transfers between devices: 14.7 us -> 6.57 us  [from_below(): return lax.ppermute(face, axis, [(i, i + 1) for i in range(count - 1)])]
    broadcast_in_dim x4 -> x0, local copies, waits for them, and re-layouts: 3.08 us -> none  [the longest x2 1.74 us: own_share(): copies = jnp.broadcast_to(share[None], (box,) + share.shape)]
    ppermute x4 -> x2, starting transfers between devices: 6.43 us -> 3.46 us  [from_above(): return lax.ppermute(face, axis, [(i + 1, i) for i in range(count - 1)])]
  transfers between devices with their start and end apart: 13 -> 6, of which waited for: 6 -> 1; matrix products, arithmetic and copies ran while one was open for 2% -> 0% of each run, Pallas kernels for 0% -> 7%
where the time goes in v2:
time: 123 us; the launch traced here: 122 us
  blocking collectives  57.4 us (47%)
  Pallas kernels  38 us (31%)
  starting transfers between devices  21.9 us (18%)
  waiting for transfers between devices  3.56 us (3%)
    all_to_all x4, blocking collectives, swap(): lax.all_to_all(parts, ('box', 'depth'), 0, 0, axis_index_groups=groups, t...  57.4 us
    pallas_call x9, Pallas kernels, call(): pl.pallas_call(kernel, out_shape=out_shape, cost_estimate=pl.CostEstimate...  38 us
    all_to_all x2, starting transfers between devices, swap(): lax.all_to_all(parts, ('box', 'depth'), 0, 0, axis_index_groups=groups, t...  11.9 us
    ppermute x2, starting transfers between devices, from_below(): return lax.ppermute(face, axis, [(i, i + 1) for i in range(count - 1)])  6.57 us
    all_to_all x2, waiting for transfers between devices, swap(): lax.all_to_all(parts, ('box', 'depth'), 0, 0, axis_index_groups=groups, t...  3.55 us
    ppermute x2, starting transfers between devices, from_above(): return lax.ppermute(face, axis, [(i + 1, i) for i in range(count - 1)])  3.46 us
  transfers between devices with their start and end apart: 6, of which 1 were waited for; matrix products, arithmetic and copies ran while one was open for 0% of the time, Pallas kernels for 7%

profile of v2, /device:TPU:1, one launch (start us, length us, event | category | flops | bytes accessed | tf_op | source)
XLA Modules:
  0.0 122.5 jit_solution(13251995282176039474)
XLA Ops:
  0.6 7.3 %shard_map.58 = (f32[8,24,384]{2,1,0:T(8,128)}, f32[8,24,384]{2,1,0:T(8,128)}, f32[8,8,384]{2,1,0:T(8,128)}, f32[8,8,384]{2,1,0:T(8,128)}, f32[32,8,128]{2,1,0:T(8,128)}) custom-call(f32[5,8,8,384]{3,2,1,0:T(8,128)} %state.3, f32[3,8,8,384]{3,2,1,0:T(8,128)} %velocity.5, s32[8,8,384]{2,1,0:T(8,128)} %bins.1), custom_call_target="tpu_custom_call" | custom-call | flops 7000000000 | tf_op jit(solution)/shard_map/pallas_call | solution.py:468
  7.9 4.4 %collective-permute-start = (f32[8,24,384]{2,1,0:T(8,128)}, f32[8,24,384]{2,1,0:T(8,128)S(1)}, u32[]{:S(2)}, u32[]{:S(2)}) collective-permute-start(f32[8,24,384]{2,1,0:T(8,128)} %get-tuple-element.28), channel_id=1, source_target_pairs={{0,8},{8,16},{16,24},{24,32},{32,40},{40,48},{48,56},{56,64},{64,7... | collective-permute-start | bytes 884744 | tf_op jit(solution)/shard_map/ppermute | solution.py:480
  12.3 1.3 %collective-permute-start.1 = (f32[8,24,384]{2,1,0:T(8,128)}, f32[8,24,384]{2,1,0:T(8,128)S(1)}, u32[]{:S(2)}, u32[]{:S(2)}) collective-permute-start(f32[8,24,384]{2,1,0:T(8,128)} %get-tuple-element.29), channel_id=1, source_target_pairs={{8,0},{16,8},{24,16},{32,24},{40,32},{48,40},{56,48},{64,56},{72,6... | collective-permute-start | bytes 884744 | tf_op jit(solution)/shard_map/ppermute | solution.py:485
  13.6 18.2 %all_to_all.30.tiles = f32[16,2,8,128]{3,2,1,0:T(8,128)S(1)} all-to-all(f32[16,2,8,128]{3,2,1,0:T(8,128)} %bitcast.7), channel_id=1, replica_groups={{0,2,4,6,64,66,68,70,128,130,132,134,192,194,196,198},{1,3,5,7,65,67,69..., dimensions={0} | all-to-all | bytes 262144 | tf_op jit(solution)/shard_map/all_to_all | solution.py:526
  31.8 0.7 shard_map.59
  32.5 8.4 %all-to-all-start.1 = ((f32[16,2,8,128]{3,2,1,0:T(8,128)}), f32[16,2,8,128]{3,2,1,0:T(8,128)S(1)}, u32[]{:S(2)}, u32[]{:S(2)}) async-start(f32[16,2,8,128]{3,2,1,0:T(8,128)} %get-tuple-element.26), calls=%async_computation.1 | async-start | bytes 262144 | tf_op jit(solution)/shard_map/all_to_all | solution.py:526
  40.8 0.0 collective-permute-done.ylo
  40.8 0.0 collective-permute-done.1.yhi
  40.9 1.2 shard_map.61
  42.1 2.2 %collective-permute-start.2 = (f32[34,8,384]{2,1,0:T(8,128)S(1)}, f32[34,8,384]{2,1,0:T(8,128)S(1)}, u32[]{:S(2)}, u32[]{:S(2)}) collective-permute-start(f32[34,8,384]{2,1,0:T(8,128)S(1)} %get-tuple-element.32), channel_id=1, source_target_pairs={{0,1},{1,2},{2,3},{3,4},{4,5},{5,6},{6,7},{8,9},{9,10},{10,11},{11... | collective-permute-start | bytes 1253384 | tf_op jit(solution)/shard_map/ppermute | solution.py:480
  44.3 2.2 %collective-permute-start.3 = (f32[34,8,384]{2,1,0:T(8,128)S(1)}, f32[34,8,384]{2,1,0:T(8,128)S(1)}, u32[]{:S(2)}, u32[]{:S(2)}) collective-permute-start(f32[34,8,384]{2,1,0:T(8,128)S(1)} %get-tuple-element.33), channel_id=1, source_target_pairs={{1,0},{2,1},{3,2},{4,3},{5,4},{6,5},{7,6},{9,8},{10,9},{11,10},{12... | collective-permute-start | bytes 1253384 | tf_op jit(solution)/shard_map/ppermute | solution.py:485
  46.4 3.6 %all-to-all-done.1.tiles = f32[16,2,8,128]{3,2,1,0:T(8,128)S(1)} async-done(((f32[16,2,8,128]{3,2,1,0:T(8,128)}), f32[16,2,8,128]{3,2,1,0:T(8,128)S(1)}, u32[]{:S(2)}, u32[]{:S(2)}) %all-to-all-start.1) | async-done | bytes 131104 | tf_op jit(solution)/shard_map/all_to_all | solution.py:526
  50.0 0.0 copy-start.7
  50.0 10.3 %all_to_all.31 = f32[16,2,8,128]{3,2,1,0:T(8,128)S(1)} all-to-all(f32[16,2,8,128]{3,2,1,0:T(8,128)S(1)} %get-tuple-element.27), channel_id=1, replica_groups={{0,2,4,6,64,66,68,70,128,130,132,134,192,194,196,198},{1,3,5,7,65,67,69..., dimensions={0} | all-to-all | bytes 262144 | tf_op jit(solution)/shard_map/all_to_all | solution.py:526
  60.4 0.0 collective-permute-done.3.xhi
  60.4 12.1 %shard_map.62 = (f32[5,8,8,384]{3,2,1,0:T(8,128)}, f32[10,24,384]{2,1,0:T(8,128)S(1)}, f32[32,8,128]{2,1,0:T(8,128)}) custom-call(f32[32,8,128]{2,1,0:T(8,128)S(1)} %bitcast.4, f32[5,8,8,384]{3,2,1,0:T(8,128)S(1)} %copy-done.1, f32[3,8,8,384]{3,2,1,0:T(8,128)S(1)} %copy-done.4, s32[8,8,384]{2,1,0:T(8,128)S(1)} %copy-done.7, ...), custom_call_target="tpu_custom_call" | custom-call | flops 14000000000 | tf_op jit(solution)/shard_map/pallas_call | solution.py:468
  72.5 0.7 copy-done.10
  73.3 3.5 %all-to-all-start.3 = ((f32[16,2,8,128]{3,2,1,0:T(8,128)}), f32[16,2,8,128]{3,2,1,0:T(8,128)S(1)}, u32[]{:S(2)}, u32[]{:S(2)}) async-start(f32[16,2,8,128]{3,2,1,0:T(8,128)} %bitcast.2), calls=%async_computation.3 | async-start | bytes 262144 | tf_op jit(solution)/shard_map/all_to_all | solution.py:526
  76.8 7.1 %shard_map.64 = (f32[14,24,384]{2,1,0:T(8,128)}, f32[16,24,384]{2,1,0:T(8,128)}) custom-call(f32[32,8,128]{2,1,0:T(8,128)} %bitcast.5, f32[10,24,384]{2,1,0:T(8,128)} %copy-done.10, f32[8,8,384]{2,1,0:T(8,128)} %get-tuple-element.31.shifted, f32[3,8,8,384]{3,2,1,0:T(8,128)} %velocity.5, f32[8,24,384]{2,1,0:T(8,128)} %copy-done.5, f32[8,24,384]{2,1,0:T(8,128)} %copy-done.6, ...), custom_call_target="tpu_custom_call" | custom-call | flops 8000000000 | tf_op jit(solution)/shard_map/pallas_call | solution.py:468
  83.9 0.6 shard_map.63
  84.5 15.6 %all_to_all.32.tiles = f32[16,2,8,128]{3,2,1,0:T(8,128)S(1)} all-to-all(f32[16,2,8,128]{3,2,1,0:T(8,128)S(1)} %get-tuple-element.40), channel_id=1, replica_groups={{0,1,8,9,16,17,24,25,32,33,40,41,48,49,56,57},{2,3,10,11,18,19,26,27,34..., dimensions={0} | all-to-all | bytes 262144 | tf_op jit(solution)/shard_map/all_to_all | solution.py:526
  100.1 0.6 shard_map.65
  100.7 13.3 %all_to_all.33 = f32[16,2,8,128]{3,2,1,0:T(8,128)} all-to-all(f32[16,2,8,128]{3,2,1,0:T(8,128)S(1)} %get-tuple-element.42), channel_id=1, replica_groups={{0,2,4,6,64,66,68,70,128,130,132,134,192,194,196,198},{1,3,5,7,65,67,69..., dimensions={0} | all-to-all | bytes 262144 | tf_op jit(solution)/shard_map/all_to_all | solution.py:526
  114.0 8.5 %shard_map.66 = (f32[8,8,384]{2,1,0:T(8,128)}, f32[5,4096]{1,0:T(8,128)}) custom-call(f32[32,8,128]{2,1,0:T(8,128)} %bitcast.8, f32[32,8,128]{2,1,0:T(8,128)} %bitcast.6, f32[14,24,384]{2,1,0:T(8,128)} %get-tuple-element.43.q_in, f32[16,24,384]{2,1,0:T(8,128)} %get-tuple-element.44.bins_in), custom_call_target="tpu_custom_call" | custom-call | flops 8999999488 | tf_op jit(solution)/shard_map/pallas_call | solution.py:468
  (23 shorter events, 0.1 us)
Async XLA Ops:
  7.9 32.9 %collective-permute-start = (f32[8,24,384]{2,1,0:T(8,128)}, f32[8,24,384]{2,1,0:T(8,128)S(1)}, u32[]{:S(2)}, u32[]{:S(2)}) collective-permute-start(f32[8,24,384]{2,1,0:T(8,128)} %get-tuple-element.28), channel_id=1, source_target_pairs={{0,8},{8,16},{16,24},{24,32},{32,40},{40,48},{48,56},{56,64},{64,7... | collective-permute-start | bytes 884744 | tf_op jit(solution)/shard_map/ppermute | solution.py:480
  12.3 28.5 %collective-permute-start.1 = (f32[8,24,384]{2,1,0:T(8,128)}, f32[8,24,384]{2,1,0:T(8,128)S(1)}, u32[]{:S(2)}, u32[]{:S(2)}) collective-permute-start(f32[8,24,384]{2,1,0:T(8,128)} %get-tuple-element.29), channel_id=1, source_target_pairs={{8,0},{16,8},{24,16},{32,24},{40,32},{48,40},{56,48},{64,56},{72,6... | collective-permute-start | bytes 884744 | tf_op jit(solution)/shard_map/ppermute | solution.py:485
  31.8 9.1 %copy-start.1 = (f32[5,8,8,384]{3,2,1,0:T(8,128)S(1)}, f32[5,8,8,384]{3,2,1,0:T(8,128)}, u32[]{:S(2)}) copy-start(f32[5,8,8,384]{3,2,1,0:T(8,128)} %state.3) | copy-start | bytes 1474564
  31.8 9.1 %copy-start.4 = (f32[3,8,8,384]{3,2,1,0:T(8,128)S(1)}, f32[3,8,8,384]{3,2,1,0:T(8,128)}, u32[]{:S(2)}) copy-start(f32[3,8,8,384]{3,2,1,0:T(8,128)} %velocity.5) | copy-start | bytes 884740
  32.5 8.4 %copy-start.8 = (f32[8,8,384]{2,1,0:T(8,128)S(1)}, f32[8,8,384]{2,1,0:T(8,128)}, u32[]{:S(2)}) copy-start(f32[8,8,384]{2,1,0:T(8,128)} %get-tuple-element.31.shifted) | copy-start | bytes 294916
  32.5 8.4 %copy-start.9 = (f32[8,8,384]{2,1,0:T(8,128)S(1)}, f32[8,8,384]{2,1,0:T(8,128)}, u32[]{:S(2)}) copy-start(f32[8,8,384]{2,1,0:T(8,128)} %get-tuple-element.30.weighted) | copy-start | bytes 294916
  32.5 17.5 %all-to-all-start.1 = ((f32[16,2,8,128]{3,2,1,0:T(8,128)}), f32[16,2,8,128]{3,2,1,0:T(8,128)S(1)}, u32[]{:S(2)}, u32[]{:S(2)}) async-start(f32[16,2,8,128]{3,2,1,0:T(8,128)} %get-tuple-element.26), calls=%async_computation.1 | async-start | bytes 262144 | tf_op jit(solution)/shard_map/all_to_all | solution.py:526
  40.8 19.6 %copy-start.5 = (f32[8,24,384]{2,1,0:T(8,128)}, f32[8,24,384]{2,1,0:T(8,128)S(1)}, u32[]{:S(2)}) copy-start(f32[8,24,384]{2,1,0:T(8,128)S(1)} %collective-permute-done.ylo) | copy-start | bytes 884740
  40.8 19.5 %copy-start.6 = (f32[8,24,384]{2,1,0:T(8,128)}, f32[8,24,384]{2,1,0:T(8,128)S(1)}, u32[]{:S(2)}) copy-start(f32[8,24,384]{2,1,0:T(8,128)S(1)} %collective-permute-done.1.yhi) | copy-start | bytes 884740
  42.1 18.3 %collective-permute-start.2 = (f32[34,8,384]{2,1,0:T(8,128)S(1)}, f32[34,8,384]{2,1,0:T(8,128)S(1)}, u32[]{:S(2)}, u32[]{:S(2)}) collective-permute-start(f32[34,8,384]{2,1,0:T(8,128)S(1)} %get-tuple-element.32), channel_id=1, source_target_pairs={{0,1},{1,2},{2,3},{3,4},{4,5},{5,6},{6,7},{8,9},{9,10},{10,11},{11... | collective-permute-start | bytes 1253384 | tf_op jit(solution)/shard_map/ppermute | solution.py:480
  44.3 16.1 %collective-permute-start.3 = (f32[34,8,384]{2,1,0:T(8,128)S(1)}, f32[34,8,384]{2,1,0:T(8,128)S(1)}, u32[]{:S(2)}, u32[]{:S(2)}) collective-permute-start(f32[34,8,384]{2,1,0:T(8,128)S(1)} %get-tuple-element.33), channel_id=1, source_target_pairs={{1,0},{2,1},{3,2},{4,3},{5,4},{6,5},{7,6},{9,8},{10,9},{11,10},{12... | collective-permute-start | bytes 1253384 | tf_op jit(solution)/shard_map/ppermute | solution.py:485
  50.0 10.4 %copy-start.7 = (s32[8,8,384]{2,1,0:T(8,128)S(1)}, s32[8,8,384]{2,1,0:T(8,128)}, u32[]{:S(2)}) copy-start(s32[8,8,384]{2,1,0:T(8,128)} %bins.1) | copy-start | bytes 294916
  60.4 12.2 %copy-start = (f32[16,2,8,128]{3,2,1,0:T(8,128)}, f32[16,2,8,128]{3,2,1,0:T(8,128)S(1)}, u32[]{:S(2)}) copy-start(f32[16,2,8,128]{3,2,1,0:T(8,128)S(1)} %all_to_all.31) | copy-start | bytes 393220
  60.4 12.2 %copy-start.2 = (f32[34,8,384]{2,1,0:T(8,128)}, f32[34,8,384]{2,1,0:T(8,128)S(1)}, u32[]{:S(2)}) copy-start(f32[34,8,384]{2,1,0:T(8,128)S(1)} %collective-permute-done.2.xlo) | copy-start | bytes 1253380
  60.4 12.2 %copy-start.3 = (f32[34,8,384]{2,1,0:T(8,128)}, f32[34,8,384]{2,1,0:T(8,128)S(1)}, u32[]{:S(2)}) copy-start(f32[34,8,384]{2,1,0:T(8,128)S(1)} %collective-permute-done.3.xhi) | copy-start | bytes 1253380
  72.5 0.7 copy-start.10
  73.3 10.6 %all-to-all-start.3 = ((f32[16,2,8,128]{3,2,1,0:T(8,128)}), f32[16,2,8,128]{3,2,1,0:T(8,128)S(1)}, u32[]{:S(2)}, u32[]{:S(2)}) async-start(f32[16,2,8,128]{3,2,1,0:T(8,128)} %bitcast.2), calls=%async_computation.3 | async-start | bytes 262144 | tf_op jit(solution)/shard_map/all_to_all | solution.py:526

commit v3 on v2

--- a/solution.py
+++ b/solution.py
@@ -1,3 +1,4 @@
+import functools
 import math
 
 import jax
@@ -79,22 +80,49 @@
     lo[...] = (b & 255).astype(F32)
 
 
+def is_odd(axis):
+    return lax.rem(lax.axis_index(axis), 2) == 1
+
+
+def start_by(odd, make, even_place, odd_place):
+    @pl.when(jnp.logical_not(odd))
+    def _():
+        for copy in make(even_place, odd_place):
+            copy.start()
+
+    @pl.when(odd)
+    def _():
+        for copy in make(odd_place, even_place):
+            copy.start()
+
+
 def sums_kernel(
-    state_in, velocity_in, bins_in, to_above, to_below, weighted, shifted, out, hi, lo, rows, acc, state, velocity, bins, sems, more_sems
+    state_in, velocity_in, bins_in, mate_out, next_out, weighted_out, shifted_out, out,
+    hi, lo, rows, acc, state, velocity, bins, to_above, to_below, weighted, shifted, sems, out_sems
 ):
-    bins_copy = pltpu.make_async_copy(bins_in, bins, more_sems.at[0])
+    bins_copy = pltpu.make_async_copy(bins_in, bins, sems.at[4, 0])
     bins_copy.start()
-    copies = [
-        [pltpu.make_async_copy(state_in.at[f, pl.ds(4 * h, 4)], state.at[f, pl.ds(4 * h, 4)], sems.at[h, f]) for f in range(NF)]
-        for h in range(2)
-    ]
-    speed_copies = [pltpu.make_async_copy(velocity_in.at[d], velocity.at[d], more_sems.at[1 + d]) for d in range(3)]
-    for copy in copies[0] + speed_copies + copies[1]:
-        copy.start()
+
+    def arrive(h):
+        at = pl.ds(2 * h, 2)
+        return [
+            pltpu.make_async_copy(state_in.at[:, at], state.at[:, at], sems.at[h, 0]),
+            pltpu.make_async_copy(velocity_in.at[:, at], velocity.at[:, at], sems.at[h, 1]),
+        ]
+
+    def leave(h, above_out, below_out):
+        at = pl.ds(4 * h, 4)
+        pairs = ((to_above, above_out), (to_below, below_out), (weighted, weighted_out), (shifted, shifted_out))
+        return [pltpu.make_async_copy(src.at[at], dst.at[at], out_sems.at[h, i]) for i, (src, dst) in enumerate(pairs)]
+
+    for h in range(4):
+        for copy in arrive(h):
+            copy.start()
     acc[...] = jnp.zeros_like(acc)
     put_rows(rows, 15, jnp.ones((Y, Z), F32))
     bins_copy.wait()
     split_bins(bins, hi, lo)
+    shifted[...] = bins[...].astype(F32) + 1.0
 
     def step(x, top):
         s = [state[f, x] for f in range(NF)]
@@ -106,8 +134,7 @@
                 w += WEIGHTS[f] * s[f]
         add_bins(acc, rows, hi, lo, x)
         weighted[x] = w
-        b = bins[x].astype(F32) + 1.0
-        shifted[x] = b
+        b = shifted[x]
         v = [velocity[d, x] for d in range(3)]
         for face, near, four, three in ((to_above, Y - 1, Y - 4, Y - 3), (to_below, 0, 0, 0)):
             parts = [c[near : near + 1] for c in s] + [w[four : four + 4], b[four : four + 4]]
@@ -116,38 +143,50 @@
         return jnp.maximum(top, jnp.abs(v[0]) + jnp.abs(v[1]) + jnp.abs(v[2]))
 
     top = jnp.zeros((Y, Z), F32)
+    for h in range(4):
+        for copy in arrive(h):
+            copy.wait()
+        top = lax.fori_loop(2 * h, 2 * h + 2, step, top)
+        if h % 2 == 1:
+            start_by(is_odd("box"), functools.partial(leave, h // 2), mate_out, next_out)
+    put_sums(out, acc, jnp.full((2, 256), jnp.max(top), F32))
     for h in range(2):
-        for copy in copies[h] + (speed_copies if h == 0 else []):
+        for copy in leave(h, mate_out, next_out):
             copy.wait()
-        top = lax.fori_loop(4 * h, 4 * h + 4, step, top)
-    put_sums(out, acc, jnp.full((2, 256), jnp.max(top), F32))
-
-
-def pack_x_kernel(state, velocity, weighted, shifted, ylo, yhi, to_above, to_below, corners, sems):
-    copies = []
-    for side, (out, near, four, three) in enumerate(((to_above, X - 1, X - 4, X - 3), (to_below, 0, 0, 0))):
-        parts = [(state.at[:, near], 0, NF), (weighted.at[pl.ds(four, 4)], SW, 4), (shifted.at[pl.ds(four, 4)], BN, 4)]
-        parts += [(velocity.at[d, pl.ds(three, 3)], VE + 3 * d, 3) for d in range(3)]
-        for i, (src, at, n) in enumerate(parts):
-            copies.append(pltpu.make_async_copy(src, out.at[pl.ds(at, n)], sems.at[side, i]))
-    for copy in copies:
-        copy.start()
+
+
+def pack_x_kernel(state, velocity, weighted, shifted, ymate, ynext, mate_out, next_out, corners, sems):
+    def fill(to_above, to_below):
+        copies = []
+        for side, (out, near, four, three) in enumerate(((to_above, X - 1, X - 4, X - 3), (to_below, 0, 0, 0))):
+            parts = [(state.at[:, near], 0, NF), (weighted.at[pl.ds(four, 4)], SW, 4), (shifted.at[pl.ds(four, 4)], BN, 4)]
+            parts += [(velocity.at[d, pl.ds(three, 3)], VE + 3 * d, 3) for d in range(3)]
+            for i, (src, at, n) in enumerate(parts):
+                copies.append(pltpu.make_async_copy(src, out.at[pl.ds(at, n)], sems.at[side, i]))
+        return copies
+
+    def fill_corners(to_above, to_below):
+        return [
+            pltpu.make_async_copy(corners.at[side], out.at[pl.ds(CSW, PLANES - CSW)], sems.at[side, 6])
+            for side, out in enumerate((to_above, to_below))
+        ]
+
+    start_by(is_odd("depth"), fill, mate_out, next_out)
+    odd = is_odd("box")
     gap = jnp.zeros((1, Z), F32)
-    for side, (out, three, two) in enumerate(((to_above, X - 3, X - 2), (to_below, 0, 0))):
-        for i in range(3):
-            x = three + i
+    for side, (three, two) in enumerate(((X - 3, X - 2), (0, 0))):
+        for x in range(three, three + 3):
+            ylo, yhi = jnp.where(odd, ymate[x], ynext[x]), jnp.where(odd, ynext[x], ymate[x])
             for at, row in ((CSW, SW), (CBN, BN)):
-                corners[side, at - CSW + i] = jnp.concatenate([ylo[x, row : row + 4], yhi[x, row : row + 4]], axis=0)
-        for i in range(2):
-            x = two + i
-            for d in range(3):
-                row = VE + 3 * d
-                corners[side, CVE - CSW + 2 * d + i] = jnp.concatenate(
-                    [ylo[x, row : row + 3], gap, yhi[x, row : row + 3], gap], axis=0
-                )
-        copies.append(pltpu.make_async_copy(corners.at[side], out.at[pl.ds(CSW, PLANES - CSW)], sems.at[side, 6]))
-        copies[-1].start()
-    for copy in copies:
+                corners[side, at - CSW + x - three] = jnp.concatenate([ylo[row : row + 4], yhi[row : row + 4]], axis=0)
+            if 0 <= x - two < 2:
+                for d in range(3):
+                    row = VE + 3 * d
+                    corners[side, CVE - CSW + 2 * d + x - two] = jnp.concatenate(
+                        [ylo[row : row + 3], gap, yhi[row : row + 3], gap], axis=0
+                    )
+    start_by(is_odd("depth"), fill_corners, mate_out, next_out)
+    for copy in fill(mate_out, next_out) + fill_corners(mate_out, next_out):
         copy.wait()
 
 
@@ -179,7 +218,7 @@
 
 
 def step_kernel(
-    first, state, velocity, bins, ylo, yhi, xlo, xhi, new_state_out, near_out, out,
+    first, state, velocity, bins, ymate, ynext, xmate, xnext, new_state_out, near_out, out,
     hi, lo, face_bins, face_lift, table, lifted, p, rows, acc, new_state, near_p, sems
 ):
     for k in range(16):
@@ -190,11 +229,19 @@
     tab = table[...]
     time_step = COURANT / (1.0 + jnp.max(first[0, 6:7, :]))
     split_bins(bins, hi, lo)
+    odd_y, odd_x = is_odd("box"), is_odd("depth")
+
+    def lower(odd, mate, other):
+        return jnp.where(odd, mate, other)
+
+    def upper(odd, mate, other):
+        return jnp.where(odd, other, mate)
+
     for x in range(X):
-        face_bins[0, x : x + 1, :] = ylo[x, BN + 3 : BN + 4, :] - 1.0
-        face_bins[1, x : x + 1, :] = yhi[x, BN : BN + 1, :] - 1.0
-    face_bins[2] = xlo[BN + 3] - 1.0
-    face_bins[3] = xhi[BN] - 1.0
+        face_bins[0, x : x + 1, :] = lower(odd_y, ymate[x, BN + 3 : BN + 4, :], ynext[x, BN + 3 : BN + 4, :]) - 1.0
+        face_bins[1, x : x + 1, :] = upper(odd_y, ymate[x, BN : BN + 1, :], ynext[x, BN : BN + 1, :]) - 1.0
+    face_bins[2] = lower(odd_x, xmate[BN + 3], xnext[BN + 3]) - 1.0
+    face_bins[3] = upper(odd_x, xmate[BN], xnext[BN]) - 1.0
 
     def lift_some(i, carry):
         for k in range(2):
@@ -213,11 +260,12 @@
 
     lax.fori_loop(0, 4, lift_some, 0)
     for f in range(NF):
-        p[f, 0, pl.ds(8, 8), :] = xlo[f] - face_lift[2, f]
-        p[f, X + 1, pl.ds(8, 8), :] = xhi[f] - face_lift[3, f]
+        p[f, 0, pl.ds(8, 8), :] = lower(odd_x, xmate[f], xnext[f]) - face_lift[2, f]
+        p[f, X + 1, pl.ds(8, 8), :] = upper(odd_x, xmate[f], xnext[f]) - face_lift[3, f]
         for x in range(X):
-            p[f, x + 1, 7:8, :] = ylo[x, f : f + 1, :] - face_lift[0, f, x : x + 1, :]
-            p[f, x + 1, 16:17, :] = yhi[x, f : f + 1, :] - face_lift[1, f, x : x + 1, :]
+            mate, other = ymate[x, f : f + 1, :], ynext[x, f : f + 1, :]
+            p[f, x + 1, 7:8, :] = lower(odd_y, mate, other) - face_lift[0, f, x : x + 1, :]
+            p[f, x + 1, 16:17, :] = upper(odd_y, mate, other) - face_lift[1, f, x : x + 1, :]
 
     acc[...] = jnp.zeros_like(acc)
     lane = lax.broadcasted_iota(jnp.int32, (Y, Z), 1)
@@ -309,28 +357,51 @@
 
 
 def ring_kernel(
-    first, near_p, shifted, velocity, ylo, yhi, xlo, xhi, q_out, bins_out, p, q, high, v, faces, flat, sems, v_sems, out_sems
+    first, near_p, shifted, velocity, ymate, ynext, xmate, xnext, q_out, bins_out, p, q, high, v, faces, flat, sems, v_sems, out_sems
 ):
-    blocks = [
-        (near_p, p.at[pl.ds(3, 10)]),
-        (xlo.at[pl.ds(SW, 3)], p.at[pl.ds(0, 3), pl.ds(8, 8)]),
-        (xhi.at[pl.ds(SW + 1, 3)], p.at[pl.ds(13, 3), pl.ds(8, 8)]),
-        (shifted, high.at[pl.ds(4, 8), pl.ds(8, 8)]),
-        (xlo.at[pl.ds(BN, 4)], high.at[pl.ds(0, 4), pl.ds(8, 8)]),
-        (xhi.at[pl.ds(BN, 4)], high.at[pl.ds(12, 4), pl.ds(8, 8)]),
-        (ylo, faces.at[0, pl.ds(0, 8)]),
-        (yhi, faces.at[1, pl.ds(0, 8)]),
-        (xlo.at[pl.ds(CSW, 12)], faces.at[2, pl.ds(0, 12), pl.ds(0, 8)]),
-        (xhi.at[pl.ds(CSW, 12)], faces.at[3, pl.ds(0, 12), pl.ds(0, 8)]),
-    ]
-    early = [pltpu.make_async_copy(src, dst, sems.at[i]) for i, (src, dst) in enumerate(blocks)]
-    late = []
-    for d in range(3):
-        parts = ((velocity.at[d], 3, 8), (xlo.at[pl.ds(VE + 3 * d, 3)], 0, 3), (xhi.at[pl.ds(VE + 3 * d, 3)], 11, 3))
-        for i, (src, at, n) in enumerate(parts):
-            late.append(pltpu.make_async_copy(src, v.at[d, pl.ds(at, n), pl.ds(8, 8)], v_sems.at[d, i]))
-    for copy in early + late:
+    def own():
+        return [
+            pltpu.make_async_copy(near_p, p.at[pl.ds(3, 10)], sems.at[0]),
+            pltpu.make_async_copy(shifted, high.at[pl.ds(4, 8), pl.ds(8, 8)], sems.at[1]),
+        ]
+
+    def along_y(yhi, ylo):
+        return [
+            pltpu.make_async_copy(ylo, faces.at[0, pl.ds(0, 8)], sems.at[2]),
+            pltpu.make_async_copy(yhi, faces.at[1, pl.ds(0, 8)], sems.at[3]),
+        ]
+
+    def along_x(xhi, xlo):
+        blocks = [
+            (xlo.at[pl.ds(SW, 3)], p.at[pl.ds(0, 3), pl.ds(8, 8)]),
+            (xhi.at[pl.ds(SW + 1, 3)], p.at[pl.ds(13, 3), pl.ds(8, 8)]),
+            (xlo.at[pl.ds(BN, 4)], high.at[pl.ds(0, 4), pl.ds(8, 8)]),
+            (xhi.at[pl.ds(BN, 4)], high.at[pl.ds(12, 4), pl.ds(8, 8)]),
+            (xlo.at[pl.ds(CSW, 12)], faces.at[2, pl.ds(0, 12), pl.ds(0, 8)]),
+            (xhi.at[pl.ds(CSW, 12)], faces.at[3, pl.ds(0, 12), pl.ds(0, 8)]),
+        ]
+        return [pltpu.make_async_copy(src, dst, sems.at[4 + i]) for i, (src, dst) in enumerate(blocks)]
+
+    def own_speed():
+        return [pltpu.make_async_copy(velocity.at[d], v.at[d, pl.ds(3, 8), pl.ds(8, 8)], v_sems.at[d, 0]) for d in range(3)]
+
+    def speed_x(xhi, xlo):
+        copies = []
+        for d in range(3):
+            for i, (src, at) in enumerate(((xlo, 0), (xhi, 11))):
+                src = src.at[pl.ds(VE + 3 * d, 3)]
+                copies.append(pltpu.make_async_copy(src, v.at[d, pl.ds(at, 3), pl.ds(8, 8)], v_sems.at[d, 1 + i]))
+        return copies
+
+    for copy in own():
         copy.start()
+    start_by(is_odd("box"), along_y, ymate, ynext)
+    start_by(is_odd("depth"), along_x, xmate, xnext)
+    for copy in own_speed():
+        copy.start()
+    start_by(is_odd("depth"), speed_x, xmate, xnext)
+    early = own() + along_y(ymate, ynext) + along_x(xmate, xnext)
+    late = own_speed() + speed_x(xmate, xnext)
     flat[...] = weighted_rows(first)
     tab = row_table(flat[...], 3)
     for copy in early:
@@ -375,7 +446,7 @@
     time_step = COURANT / (1.0 + jnp.max(first[0, 6:7, :]))
     lane = lax.broadcasted_iota(jnp.int32, (TALL, Z), 1)
 
-    def step(x, carry):
+    for x in range(14):
         c = p[x + 1]
         sides = (
             (p[x], p[x + 2]),
@@ -386,34 +457,39 @@
         for d, (before, after) in enumerate(sides):
             change += jnp.maximum(v[d, x], 0.0) * (c - before) + jnp.minimum(v[d, x], 0.0) * (after - c)
         q[x] = c - time_step * change
-        return carry
-
-    lax.fori_loop(0, 14, step, 0)
     q_copy = pltpu.make_async_copy(q, q_out, out_sems.at[1])
     q_copy.start()
     q_copy.wait()
     bins_copy.wait()
 
 
-def relax_kernel(second, first, q_in, bins_in, potential, profile, src, high, pot, flat, sems):
-    halves = []
-    for h in range(2):
-        at = pl.ds(3 + 4 * h, 4)
-        bins_at = pl.ds(4 + 4 * h, 4)
-        halves.append((q_in.at[at], src.at[at], bins_in.at[bins_at], high.at[bins_at]))
-    for at, n in ((0, 3), (11, 3)):
+def relax_kernel(
+    second_in, first_in, q_in, bins_in, potential_out, profile_out, src, high, pot, flat, second, first, potential, profile, sems, out_sems
+):
+    tables = [
+        pltpu.make_async_copy(second_in, second, sems.at[4, 0]),
+        pltpu.make_async_copy(first_in, first, sems.at[4, 1]),
+    ]
+    blocks = []
+    for at, n in ((3, 4), (7, 4), (0, 3), (11, 3)):
         bins_at = pl.ds(at + 1, n)
-        halves.append((q_in.at[pl.ds(at, n)], src.at[pl.ds(at, n)], bins_in.at[bins_at], high.at[bins_at]))
-    copies = [
-        [pltpu.make_async_copy(parts[2 * i], parts[2 * i + 1], sems.at[h, i]) for i in range(2)] for h, parts in enumerate(halves)
-    ]
-    for pair in copies:
+        at = pl.ds(at, n)
+        i = len(blocks)
+        blocks.append([
+            pltpu.make_async_copy(q_in.at[at], src.at[at], sems.at[i, 0]),
+            pltpu.make_async_copy(bins_in.at[bins_at], high.at[bins_at], sems.at[i, 1]),
+        ])
+    for pair in [tables] + blocks:
         for copy in pair:
             copy.start()
+    for copy in tables:
+        copy.wait()
     flat[...] = weighted_rows(second)
     tab = row_table(flat[...], 2)
     for t in range(TILES):
         profile[:, 128 * t : 128 * t + 128] = (first[t] + second[t])[0:NF]
+    profile_copy = pltpu.make_async_copy(profile, profile_out, out_sems.at[0])
+    profile_copy.start()
 
     def lift_x(x, rows, block):
         if block:
@@ -431,18 +507,17 @@
         return carry
 
     for h in range(2):
-        for copy in copies[h]:
+        for copy in blocks[h]:
             copy.wait()
         lax.fori_loop(3 + 4 * h, 7 + 4 * h, lambda x, c: (lift_x(x, (5, 6, 7, 16, 17, 18), True), c)[1], 0)
-    for pair in copies[2:]:
+    for pair in blocks[2:]:
         for copy in pair:
             copy.wait()
     lax.fori_loop(0, 2, lift_sides, 0)
     lane = lax.broadcasted_iota(jnp.int32, (TALL, Z), 1)
     for s in range(1, 4):
         now, later = (s + 1) % 2, s % 2
-
-        def sweep(x, carry):
+        for x in range(s, 14 - s):
             c = pot[now, x]
             near = pot[now, x - 1] + pot[now, x + 1]
             near += pltpu.roll(c, 1, 0) + pltpu.roll(c, TALL - 1, 0)
@@ -452,9 +527,10 @@
                 pot[later, x] = jnp.where(high[x + 1] < 0.5, 0.0, new)
             else:
                 potential[x - 3] = new[8:16]
-            return carry
-
-        lax.fori_loop(s, 14 - s, sweep, 0)
+    potential_copy = pltpu.make_async_copy(potential, potential_out, out_sems.at[1])
+    potential_copy.start()
+    potential_copy.wait()
+    profile_copy.wait()
 
 
 def f32_like(*shape):
@@ -475,14 +551,11 @@
     )(*args)
 
 
-def from_below(face, axis):
+def exchange(to_mate, to_next, axis):
     count = lax.axis_size(axis)
-    return lax.ppermute(face, axis, [(i, i + 1) for i in range(count - 1)])
-
-
-def from_above(face, axis):
-    count = lax.axis_size(axis)
-    return lax.ppermute(face, axis, [(i + 1, i) for i in range(count - 1)])
+    mates = [(i, i ^ 1) for i in range(count)]
+    others = [pair for i in range(1, count - 1, 2) for pair in ((i, i + 1), (i + 1, i))]
+    return lax.ppermute(to_mate, axis, mates), lax.ppermute(to_next, axis, others)
 
 
 def added(tiles):
@@ -534,13 +607,14 @@
 REMOTE = pl.BlockSpec(memory_space=pl.ANY)
 SUMS = (
     7,
-    (f32_like(X, TALL, Z), f32_like(X, TALL, Z), f32_like(X, Y, Z), f32_like(X, Y, Z), f32_like(TILES, 8, 128)),
+    tuple(pltpu.HBM(shape, F32) for shape in ((X, TALL, Z), (X, TALL, Z), (X, Y, Z), (X, Y, Z))) + (f32_like(TILES, 8, 128),),
     [
         ((X, Y, Z), F32), ((X, Y, Z), F32), ((3, Y * 16, 128), F32), ((256, 256), F32),
         ((NF, X, Y, Z), F32), ((3, X, Y, Z), F32), ((X, Y, Z), jnp.int32),
-        pltpu.SemaphoreType.DMA((2, NF)), pltpu.SemaphoreType.DMA((4,)),
+        ((X, TALL, Z), F32), ((X, TALL, Z), F32), ((X, Y, Z), F32), ((X, Y, Z), F32),
+        pltpu.SemaphoreType.DMA((5, 2)), pltpu.SemaphoreType.DMA((2, 4)),
     ],
-    dict(in_specs=[REMOTE] * 3, megabytes=58),
+    dict(in_specs=[REMOTE] * 3, out_specs=(REMOTE,) * 4 + (VISIBLE,), megabytes=58),
 )
 PACK_X = (
     2,
@@ -550,7 +624,7 @@
 )
 STEP = (
     14,
-    (f32_like(NF, X, Y, Z), f32_like(X + 2, TALL, Z), f32_like(TILES, 8, 128)),
+    (f32_like(NF, X, Y, Z), pltpu.HBM((X + 2, TALL, Z), F32), f32_like(TILES, 8, 128)),
     [
         ((X, Y, Z), F32), ((X, Y, Z), F32), ((4, Y, Z), F32), ((4, NF, Y, Z), F32), ((256, 256), BF16),
         ((X, 3, 64, 128), F32), ((NF, X + 2, TALL, Z), F32), ((3, Y * 16, 128), F32), ((256, 256), F32),
@@ -569,27 +643,29 @@
 )
 RELAX = (
     9,
-    (f32_like(X, Y, Z), f32_like(NF, NBINS)),
-    [((14, TALL, Z), F32), ((16, TALL, Z), F32), ((2, 14, TALL, Z), F32), ((TILES, 128), F32), pltpu.SemaphoreType.DMA((4, 2))],
-    dict(in_specs=[VISIBLE] * 2 + [REMOTE] * 2, megabytes=58),
+    (pltpu.HBM((X, Y, Z), F32), pltpu.HBM((NF, NBINS), F32)),
+    [
+        ((14, TALL, Z), F32), ((16, TALL, Z), F32), ((2, 14, TALL, Z), F32), ((TILES, 128), F32),
+        ((TILES, 8, 128), F32), ((TILES, 8, 128), F32), ((X, Y, Z), F32), ((NF, NBINS), F32),
+        pltpu.SemaphoreType.DMA((5, 2)), pltpu.SemaphoreType.DMA((2,)),
+    ],
+    dict(in_specs=[REMOTE] * 4, out_specs=(REMOTE, REMOTE), megabytes=58),
 )
 
 
-MERGE = (1, (f32_like(2, 8, 128), f32_like(MEMBERS, 2, 8, 128)), [], dict(megabytes=20))
+MERGE = (0, (f32_like(2, 8, 128), f32_like(MEMBERS, 2, 8, 128)), [], dict(megabytes=20))
 
 
 def per_device(state, velocity, bins):
-    to_above, to_below, weighted, shifted, tiles = call(sums_kernel, SUMS, state, velocity, bins)
-    ylo = from_below(to_above, "box")
-    yhi = from_above(to_below, "box")
-    to_above, to_below = call(pack_x_kernel, PACK_X, state, velocity, weighted, shifted, ylo, yhi)
-    xlo = from_below(to_above, "depth")
-    xhi = from_above(to_below, "depth")
+    to_mate, to_next, weighted, shifted, tiles = call(sums_kernel, SUMS, state, velocity, bins)
+    ymate, ynext = exchange(to_mate, to_next, "box")
+    to_mate, to_next = call(pack_x_kernel, PACK_X, state, velocity, weighted, shifted, ymate, ynext)
+    xmate, xnext = exchange(to_mate, to_next, "depth")
     share, copies = call(merge_kernel, MERGE, swap(in_members(tiles), SHARE_GROUPS))
     share, copies = call(divide_own_kernel, MERGE, swap(copies, OTHER_GROUPS))
     first = swap(copies, SHARE_GROUPS).reshape(TILES, 8, 128)
-    new_state, near_p, tiles = call(step_kernel, STEP, first, state, velocity, bins, ylo, yhi, xlo, xhi)
-    q, wide_bins = call(ring_kernel, RING, first, near_p, shifted, velocity, ylo, yhi, xlo, xhi)
+    new_state, near_p, tiles = call(step_kernel, STEP, first, state, velocity, bins, ymate, ynext, xmate, xnext)
+    q, wide_bins = call(ring_kernel, RING, first, near_p, shifted, velocity, ymate, ynext, xmate, xnext)
     part, copies = call(merge_kernel, MERGE, swap(in_members(tiles), SHARE_GROUPS))
     copies, q, wide_bins = lax.optimization_barrier((copies, q, wide_bins))
     part, copies = call(divide_kernel, MERGE, swap(copies, OTHER_GROUPS), share)

time: 123 us -> 115 us (0.935)
  blocking collectives: 57.4 us -> 53.5 us
  Pallas kernels: 38 us -> 34.5 us
  starting transfers between devices: 21.9 us -> 24.6 us
  waiting for transfers between devices: 3.56 us -> 1.15 us
    all_to_all x2, starting transfers between devices: 11.9 us -> 16.3 us  [swap(): lax.all_to_all(parts, ('box', 'depth'), 0, 0, axis_index_groups=groups, t...]
    all_to_all x4, blocking collectives: 57.4 us -> 53.5 us  [swap(): lax.all_to_all(parts, ('box', 'depth'), 0, 0, axis_index_groups=groups, t...]
    pallas_call x9, Pallas kernels: 38 us -> 34.5 us  [call(): pl.pallas_call(kernel, out_shape=out_shape, cost_estimate=pl.CostEstimate...]
    all_to_all x2, waiting for transfers between devices: 3.55 us -> 1.14 us  [swap(): lax.all_to_all(parts, ('box', 'depth'), 0, 0, axis_index_groups=groups, t...]
    ppermute x4, starting transfers between devices: 10 us -> 8.27 us  [the longest x2 4.16 us: exchange(): lax.ppermute(to_mate, axis, mates)]
  transfers between devices with their start and end apart: 6 -> 6, of which waited for: 1 -> 2; matrix products, arithmetic and copies ran while one was open for 0% -> 0% of each run, Pallas kernels for 7% -> 7%
where the time goes in v3:
time: 115 us
  blocking collectives  53.5 us (47%)
  Pallas kernels  34.5 us (30%)
  starting transfers between devices  24.6 us (21%)
    all_to_all x4, blocking collectives, swap(): lax.all_to_all(parts, ('box', 'depth'), 0, 0, axis_index_groups=groups, t...  53.5 us
    pallas_call x9, Pallas kernels, call(): pl.pallas_call(kernel, out_shape=out_shape, cost_estimate=pl.CostEstimate...  34.5 us
    all_to_all x2, starting transfers between devices, swap(): lax.all_to_all(parts, ('box', 'depth'), 0, 0, axis_index_groups=groups, t...  16.3 us
    ppermute x2, starting transfers between devices, exchange(): lax.ppermute(to_mate, axis, mates)  4.16 us
    ppermute x2, starting transfers between devices, exchange(): lax.ppermute(to_next, axis, others)  4.12 us
  transfers between devices with their start and end apart: 6, of which 2 were waited for; matrix products, arithmetic and copies ran while one was open for 0% of the time, Pallas kernels for 7%

profile of v3, /device:TPU:1, one launch (start us, length us, event | category | flops | bytes accessed | tf_op | source)
XLA Modules:
  0.0 114.7 jit_solution(9310448713306114031)
XLA Ops:
  0.6 0.0 copy-start.4
  0.7 7.8 %shard_map.58 = (f32[8,24,384]{2,1,0:T(8,128)}, f32[8,24,384]{2,1,0:T(8,128)}, f32[8,8,384]{2,1,0:T(8,128)}, f32[8,8,384]{2,1,0:T(8,128)}, f32[32,8,128]{2,1,0:T(8,128)}) custom-call(f32[5,8,8,384]{3,2,1,0:T(8,128)} %state.3, f32[3,8,8,384]{3,2,1,0:T(8,128)} %velocity.5, s32[8,8,384]{2,1,0:T(8,128)} %bins.1), custom_call_target="tpu_custom_call" | custom-call | flops 7000000000 | tf_op jit(solution)/shard_map/pallas_call | solution.py:544
  8.5 2.5 %collective-permute-start = (f32[8,24,384]{2,1,0:T(8,128)}, f32[8,24,384]{2,1,0:T(8,128)S(1)}, u32[]{:S(2)}, u32[]{:S(2)}) collective-permute-start(f32[8,24,384]{2,1,0:T(8,128)} %get-tuple-element.28), channel_id=1, source_target_pairs={{0,8},{8,0},{16,24},{24,16},{32,40},{40,32},{48,56},{56,48},{64,72... | collective-permute-start | bytes 884744 | tf_op jit(solution)/shard_map/ppermute | solution.py:558
  11.0 0.7 collective-permute-start.1
  11.7 0.0 copy-start.9
  11.7 12.8 %all-to-all-start = ((f32[16,2,8,128]{3,2,1,0:T(8,128)}), f32[16,2,8,128]{3,2,1,0:T(8,128)S(1)}, u32[]{:S(2)}, u32[]{:S(2)}) async-start(f32[16,2,8,128]{3,2,1,0:T(8,128)} %bitcast.7), calls=%async_computation | async-start | bytes 262144 | tf_op jit(solution)/shard_map/all_to_all | solution.py:599
  24.5 0.0 collective-permute-done.ymate
  24.6 1.2 %shard_map.61 = (f32[34,8,384]{2,1,0:T(8,128)S(1)}, f32[34,8,384]{2,1,0:T(8,128)S(1)}) custom-call(f32[5,8,8,384]{3,2,1,0:T(8,128)S(1)} %copy-done.1, f32[3,8,8,384]{3,2,1,0:T(8,128)S(1)} %copy-done.4, f32[8,8,384]{2,1,0:T(8,128)S(1)} %copy-done.9, f32[8,8,384]{2,1,0:T(8,128)S(1)} %copy-done.8, f32[8,24,384]{2,1,0:T(8,128)S(1)} %collective-permute-done.ymate, ...), custom_call_target="tpu_custom_call" | custom-call | flops 2000000000 | tf_op jit(solution)/shard_map/pallas_call | solution.py:544
  25.8 1.6 %collective-permute-start.2 = (f32[34,8,384]{2,1,0:T(8,128)S(1)}, f32[34,8,384]{2,1,0:T(8,128)S(1)}, u32[]{:S(2)}, u32[]{:S(2)}) collective-permute-start(f32[34,8,384]{2,1,0:T(8,128)S(1)} %get-tuple-element.32), channel_id=1, source_target_pairs={{0,1},{1,0},{2,3},{3,2},{4,5},{5,4},{6,7},{7,6},{8,9},{9,8},{10,11... | collective-permute-start | bytes 1253384 | tf_op jit(solution)/shard_map/ppermute | solution.py:558
  27.4 3.4 %collective-permute-start.3 = (f32[34,8,384]{2,1,0:T(8,128)S(1)}, f32[34,8,384]{2,1,0:T(8,128)S(1)}, u32[]{:S(2)}, u32[]{:S(2)}) collective-permute-start(f32[34,8,384]{2,1,0:T(8,128)S(1)} %get-tuple-element.33), channel_id=1, source_target_pairs={{1,2},{2,1},{3,4},{4,3},{5,6},{6,5},{9,10},{10,9},{11,12},{12,11},... | collective-permute-start | bytes 1253384 | tf_op jit(solution)/shard_map/ppermute | solution.py:558
  30.9 0.5 all-to-all-done.tiles
  31.4 0.6 shard_map.59
  32.0 14.8 %all_to_all.30.tiles = f32[16,2,8,128]{3,2,1,0:T(8,128)S(1)} all-to-all(f32[16,2,8,128]{3,2,1,0:T(8,128)S(1)} %get-tuple-element.26), channel_id=1, replica_groups={{0,1,8,9,16,17,24,25,32,33,40,41,48,49,56,57},{2,3,10,11,18,19,26,27,34..., dimensions={0} | all-to-all | bytes 262144 | tf_op jit(solution)/shard_map/all_to_all | solution.py:599
  46.8 0.0 copy-start.7
  46.9 12.7 %all_to_all.31 = f32[16,2,8,128]{3,2,1,0:T(8,128)S(1)} all-to-all(f32[16,2,8,128]{3,2,1,0:T(8,128)S(1)} %get-tuple-element.27), channel_id=1, replica_groups={{0,2,4,6,64,66,68,70,128,130,132,134,192,194,196,198},{1,3,5,7,65,67,69..., dimensions={0} | all-to-all | bytes 262144 | tf_op jit(solution)/shard_map/all_to_all | solution.py:599
  59.6 11.9 %shard_map.62 = (f32[5,8,8,384]{3,2,1,0:T(8,128)}, f32[10,24,384]{2,1,0:T(8,128)}, f32[32,8,128]{2,1,0:T(8,128)}) custom-call(f32[32,8,128]{2,1,0:T(8,128)S(1)} %bitcast.4, f32[5,8,8,384]{3,2,1,0:T(8,128)S(1)} %copy-done.1, f32[3,8,8,384]{3,2,1,0:T(8,128)S(1)} %copy-done.4, s32[8,8,384]{2,1,0:T(8,128)S(1)} %copy-done.7, ...), custom_call_target="tpu_custom_call" | custom-call | flops 14000000000 | tf_op jit(solution)/shard_map/pallas_call | solution.py:544
  71.6 3.5 %all-to-all-start.3 = ((f32[16,2,8,128]{3,2,1,0:T(8,128)}), f32[16,2,8,128]{3,2,1,0:T(8,128)S(1)}, u32[]{:S(2)}, u32[]{:S(2)}) async-start(f32[16,2,8,128]{3,2,1,0:T(8,128)} %bitcast.2), calls=%async_computation.3 | async-start | bytes 262144 | tf_op jit(solution)/shard_map/all_to_all | solution.py:599
  75.1 6.1 %shard_map.64 = (f32[14,24,384]{2,1,0:T(8,128)}, f32[16,24,384]{2,1,0:T(8,128)}) custom-call(f32[32,8,128]{2,1,0:T(8,128)} %bitcast.5, f32[10,24,384]{2,1,0:T(8,128)} %get-tuple-element.37.near_p, f32[8,8,384]{2,1,0:T(8,128)} %get-tuple-element.31.shifted, f32[3,8,8,384]{3,2,1,0:T(8,128)} %velocity.5, f32[8,24,384]{2,1,0:T(8,128)} %copy-done.5, ...), custom_call_target="tpu_custom_call" | custom-call | flops 8000000000 | tf_op jit(solution)/shard_map/pallas_call | solution.py:544
  81.3 0.6 all-to-all-done.3.tiles
  81.9 0.6 shard_map.63
  82.5 13.6 %all_to_all.32.tiles = f32[16,2,8,128]{3,2,1,0:T(8,128)S(1)} all-to-all(f32[16,2,8,128]{3,2,1,0:T(8,128)S(1)} %get-tuple-element.40), channel_id=1, replica_groups={{0,1,8,9,16,17,24,25,32,33,40,41,48,49,56,57},{2,3,10,11,18,19,26,27,34..., dimensions={0} | all-to-all | bytes 262144 | tf_op jit(solution)/shard_map/all_to_all | solution.py:599
  96.2 0.6 shard_map.65
  96.8 12.4 %all_to_all.33 = f32[16,2,8,128]{3,2,1,0:T(8,128)} all-to-all(f32[16,2,8,128]{3,2,1,0:T(8,128)S(1)} %get-tuple-element.42), channel_id=1, replica_groups={{0,2,4,6,64,66,68,70,128,130,132,134,192,194,196,198},{1,3,5,7,65,67,69..., dimensions={0} | all-to-all | bytes 262144 | tf_op jit(solution)/shard_map/all_to_all | solution.py:599
  109.1 5.5 %shard_map.66 = (f32[8,8,384]{2,1,0:T(8,128)}, f32[5,4096]{1,0:T(8,128)}) custom-call(f32[32,8,128]{2,1,0:T(8,128)} %bitcast.8, f32[32,8,128]{2,1,0:T(8,128)} %bitcast.6, f32[14,24,384]{2,1,0:T(8,128)} %get-tuple-element.43.q_in, f32[16,24,384]{2,1,0:T(8,128)} %get-tuple-element.44.bins_in), custom_call_target="tpu_custom_call" | custom-call | flops 8999999488 | tf_op jit(solution)/shard_map/pallas_call | solution.py:544
  (21 shorter events, 0.1 us)
Async XLA Ops:
  0.6 23.9 %copy-start.4 = (f32[3,8,8,384]{3,2,1,0:T(8,128)S(1)}, f32[3,8,8,384]{3,2,1,0:T(8,128)}, u32[]{:S(2)}) copy-start(f32[3,8,8,384]{3,2,1,0:T(8,128)} %velocity.5) | copy-start | bytes 884740
  0.6 23.9 %copy-start.1 = (f32[5,8,8,384]{3,2,1,0:T(8,128)S(1)}, f32[5,8,8,384]{3,2,1,0:T(8,128)}, u32[]{:S(2)}) copy-start(f32[5,8,8,384]{3,2,1,0:T(8,128)} %state.3) | copy-start | bytes 1474564
  8.5 16.0 %collective-permute-start = (f32[8,24,384]{2,1,0:T(8,128)}, f32[8,24,384]{2,1,0:T(8,128)S(1)}, u32[]{:S(2)}, u32[]{:S(2)}) collective-permute-start(f32[8,24,384]{2,1,0:T(8,128)} %get-tuple-element.28), channel_id=1, source_target_pairs={{0,8},{8,0},{16,24},{24,16},{32,40},{40,32},{48,56},{56,48},{64,72... | collective-permute-start | bytes 884744 | tf_op jit(solution)/shard_map/ppermute | solution.py:558
  11.0 13.5 %collective-permute-start.1 = (f32[8,24,384]{2,1,0:T(8,128)}, f32[8,24,384]{2,1,0:T(8,128)S(1)}, u32[]{:S(2)}, u32[]{:S(2)}) collective-permute-start(f32[8,24,384]{2,1,0:T(8,128)} %get-tuple-element.29), channel_id=1, source_target_pairs={{8,16},{16,8},{24,32},{32,24},{40,48},{48,40},{56,64},{64,56},{72,... | collective-permute-start | bytes 884744 | tf_op jit(solution)/shard_map/ppermute | solution.py:558
  11.7 12.9 %copy-start.8 = (f32[8,8,384]{2,1,0:T(8,128)S(1)}, f32[8,8,384]{2,1,0:T(8,128)}, u32[]{:S(2)}) copy-start(f32[8,8,384]{2,1,0:T(8,128)} %get-tuple-element.31.shifted) | copy-start | bytes 294916
  11.7 12.9 %copy-start.9 = (f32[8,8,384]{2,1,0:T(8,128)S(1)}, f32[8,8,384]{2,1,0:T(8,128)}, u32[]{:S(2)}) copy-start(f32[8,8,384]{2,1,0:T(8,128)} %get-tuple-element.30.weighted) | copy-start | bytes 294916
  11.7 19.6 %all-to-all-start = ((f32[16,2,8,128]{3,2,1,0:T(8,128)}), f32[16,2,8,128]{3,2,1,0:T(8,128)S(1)}, u32[]{:S(2)}, u32[]{:S(2)}) async-start(f32[16,2,8,128]{3,2,1,0:T(8,128)} %bitcast.7), calls=%async_computation | async-start | bytes 262144 | tf_op jit(solution)/shard_map/all_to_all | solution.py:599
  24.5 35.0 %copy-start.5 = (f32[8,24,384]{2,1,0:T(8,128)}, f32[8,24,384]{2,1,0:T(8,128)S(1)}, u32[]{:S(2)}) copy-start(f32[8,24,384]{2,1,0:T(8,128)S(1)} %collective-permute-done.ymate) | copy-start | bytes 884740
  24.5 35.0 %copy-start.6 = (f32[8,24,384]{2,1,0:T(8,128)}, f32[8,24,384]{2,1,0:T(8,128)S(1)}, u32[]{:S(2)}) copy-start(f32[8,24,384]{2,1,0:T(8,128)S(1)} %collective-permute-done.1.ynext) | copy-start | bytes 884740
  25.8 33.8 %collective-permute-start.2 = (f32[34,8,384]{2,1,0:T(8,128)S(1)}, f32[34,8,384]{2,1,0:T(8,128)S(1)}, u32[]{:S(2)}, u32[]{:S(2)}) collective-permute-start(f32[34,8,384]{2,1,0:T(8,128)S(1)} %get-tuple-element.32), channel_id=1, source_target_pairs={{0,1},{1,0},{2,3},{3,2},{4,5},{5,4},{6,7},{7,6},{8,9},{9,8},{10,11... | collective-permute-start | bytes 1253384 | tf_op jit(solution)/shard_map/ppermute | solution.py:558
  27.4 32.2 %collective-permute-start.3 = (f32[34,8,384]{2,1,0:T(8,128)S(1)}, f32[34,8,384]{2,1,0:T(8,128)S(1)}, u32[]{:S(2)}, u32[]{:S(2)}) collective-permute-start(f32[34,8,384]{2,1,0:T(8,128)S(1)} %get-tuple-element.33), channel_id=1, source_target_pairs={{1,2},{2,1},{3,4},{4,3},{5,6},{6,5},{9,10},{10,9},{11,12},{12,11},... | collective-permute-start | bytes 1253384 | tf_op jit(solution)/shard_map/ppermute | solution.py:558
  46.8 12.7 %copy-start.7 = (s32[8,8,384]{2,1,0:T(8,128)S(1)}, s32[8,8,384]{2,1,0:T(8,128)}, u32[]{:S(2)}) copy-start(s32[8,8,384]{2,1,0:T(8,128)} %bins.1) | copy-start | bytes 294916
  59.5 12.0 %copy-start = (f32[16,2,8,128]{3,2,1,0:T(8,128)}, f32[16,2,8,128]{3,2,1,0:T(8,128)S(1)}, u32[]{:S(2)}) copy-start(f32[16,2,8,128]{3,2,1,0:T(8,128)S(1)} %all_to_all.31) | copy-start | bytes 393220
  59.5 12.0 %copy-start.2 = (f32[34,8,384]{2,1,0:T(8,128)}, f32[34,8,384]{2,1,0:T(8,128)S(1)}, u32[]{:S(2)}) copy-start(f32[34,8,384]{2,1,0:T(8,128)S(1)} %collective-permute-done.2.xmate) | copy-start | bytes 1253380
  59.6 12.0 %copy-start.3 = (f32[34,8,384]{2,1,0:T(8,128)}, f32[34,8,384]{2,1,0:T(8,128)S(1)}, u32[]{:S(2)}) copy-start(f32[34,8,384]{2,1,0:T(8,128)S(1)} %collective-permute-done.3.xnext) | copy-start | bytes 1253380
  71.6 10.3 %all-to-all-start.3 = ((f32[16,2,8,128]{3,2,1,0:T(8,128)}), f32[16,2,8,128]{3,2,1,0:T(8,128)S(1)}, u32[]{:S(2)}, u32[]{:S(2)}) async-start(f32[16,2,8,128]{3,2,1,0:T(8,128)} %bitcast.2), calls=%async_computation.3 | async-start | bytes 262144 | tf_op jit(solution)/shard_map/all_to_all | solution.py:599

commit v4 on v3

--- a/solution.py
+++ b/solution.py
@@ -97,8 +97,8 @@
 
 
 def sums_kernel(
-    state_in, velocity_in, bins_in, mate_out, next_out, weighted_out, shifted_out, out,
-    hi, lo, rows, acc, state, velocity, bins, to_above, to_below, weighted, shifted, sems, out_sems
+    state_in, velocity_in, bins_in, mate_out, next_out, weighted_out, shifted_out, tiles_out,
+    hi, lo, rows, acc, state, velocity, bins, to_above, to_below, weighted, shifted, out, sems, out_sems
 ):
     bins_copy = pltpu.make_async_copy(bins_in, bins, sems.at[4, 0])
     bins_copy.start()
@@ -111,7 +111,7 @@
         ]
 
     def leave(h, above_out, below_out):
-        at = pl.ds(4 * h, 4)
+        at = pl.ds(2 * h, 2)
         pairs = ((to_above, above_out), (to_below, below_out), (weighted, weighted_out), (shifted, shifted_out))
         return [pltpu.make_async_copy(src.at[at], dst.at[at], out_sems.at[h, i]) for i, (src, dst) in enumerate(pairs)]
 
@@ -143,14 +143,19 @@
         return jnp.maximum(top, jnp.abs(v[0]) + jnp.abs(v[1]) + jnp.abs(v[2]))
 
     top = jnp.zeros((Y, Z), F32)
-    for h in range(4):
+    def two(h, top):
         for copy in arrive(h):
             copy.wait()
-        top = lax.fori_loop(2 * h, 2 * h + 2, step, top)
-        if h % 2 == 1:
-            start_by(is_odd("box"), functools.partial(leave, h // 2), mate_out, next_out)
+        top = step(2 * h + 1, step(2 * h, top))
+        start_by(is_odd("box"), functools.partial(leave, h), mate_out, next_out)
+        return top
+
+    top = lax.fori_loop(0, 4, two, top)
     put_sums(out, acc, jnp.full((2, 256), jnp.max(top), F32))
-    for h in range(2):
+    tiles_copy = pltpu.make_async_copy(out, tiles_out, sems.at[4, 1])
+    tiles_copy.start()
+    tiles_copy.wait()
+    for h in range(4):
         for copy in leave(h, mate_out, next_out):
             copy.wait()
 
@@ -258,7 +263,8 @@
                 p[f, x + 1, pl.ds(8, 8), :] = state[f, x] - get_field(lifted, x, f)
         return carry
 
-    lax.fori_loop(0, 4, lift_some, 0)
+    for i in range(4):
+        lift_some(i, 0)
     for f in range(NF):
         p[f, 0, pl.ds(8, 8), :] = lower(odd_x, xmate[f], xnext[f]) - face_lift[2, f]
         p[f, X + 1, pl.ds(8, 8), :] = upper(odd_x, xmate[f], xnext[f]) - face_lift[3, f]
@@ -294,17 +300,14 @@
         return pltpu.make_async_copy(new_state.at[:, x], new_state_out.at[:, x], sems.at[x])
 
 
-    def gather_p(x, carry):
+    for x in range(X + 2):
         total = WEIGHTS[0] * p[0, x]
         for f in range(1, NF):
             total += WEIGHTS[f] * p[f, x]
         near_p[x] = total
-        return carry
-
-    lax.fori_loop(0, X + 2, gather_p, 0)
     near_copy = pltpu.make_async_copy(near_p, near_out, sems.at[X])
     near_copy.start()
-    lax.fori_loop(0, X, advect, 0)
+    lax.fori_loop(0, X // 2, lambda i, c: advect(2 * i + 1, advect(2 * i, c)), 0)
     put_sums(out, acc, jnp.zeros((2, 256), F32))
     for x in range(X):
         state_copy(x).wait()
@@ -433,7 +436,8 @@
             lift_x(4 + 4 * side + i, rows[0], False)
         return carry
 
-    lax.fori_loop(0, 2, lift_sides, 0)
+    for side in range(2):
+        lift_sides(side, 0)
     for copy in late:
         copy.wait()
     for d in range(3):
@@ -509,11 +513,13 @@
     for h in range(2):
         for copy in blocks[h]:
             copy.wait()
-        lax.fori_loop(3 + 4 * h, 7 + 4 * h, lambda x, c: (lift_x(x, (5, 6, 7, 16, 17, 18), True), c)[1], 0)
+        for x in range(3 + 4 * h, 7 + 4 * h):
+            lift_x(x, (5, 6, 7, 16, 17, 18), True)
     for pair in blocks[2:]:
         for copy in pair:
             copy.wait()
-    lax.fori_loop(0, 2, lift_sides, 0)
+    for side in range(2):
+        lift_sides(side, 0)
     lane = lax.broadcasted_iota(jnp.int32, (TALL, Z), 1)
     for s in range(1, 4):
         now, later = (s + 1) % 2, s % 2
@@ -607,14 +613,14 @@
 REMOTE = pl.BlockSpec(memory_space=pl.ANY)
 SUMS = (
     7,
-    tuple(pltpu.HBM(shape, F32) for shape in ((X, TALL, Z), (X, TALL, Z), (X, Y, Z), (X, Y, Z))) + (f32_like(TILES, 8, 128),),
+    tuple(pltpu.HBM(shape, F32) for shape in ((X, TALL, Z), (X, TALL, Z), (X, Y, Z), (X, Y, Z), (TILES, 8, 128))),
     [
         ((X, Y, Z), F32), ((X, Y, Z), F32), ((3, Y * 16, 128), F32), ((256, 256), F32),
         ((NF, X, Y, Z), F32), ((3, X, Y, Z), F32), ((X, Y, Z), jnp.int32),
-        ((X, TALL, Z), F32), ((X, TALL, Z), F32), ((X, Y, Z), F32), ((X, Y, Z), F32),
-        pltpu.SemaphoreType.DMA((5, 2)), pltpu.SemaphoreType.DMA((2, 4)),
+        ((X, TALL, Z), F32), ((X, TALL, Z), F32), ((X, Y, Z), F32), ((X, Y, Z), F32), ((TILES, 8, 128), F32),
+        pltpu.SemaphoreType.DMA((5, 2)), pltpu.SemaphoreType.DMA((4, 4)),
     ],
-    dict(in_specs=[REMOTE] * 3, out_specs=(REMOTE,) * 4 + (VISIBLE,), megabytes=58),
+    dict(in_specs=[REMOTE] * 3, out_specs=(REMOTE,) * 5, megabytes=58),
 )
 PACK_X = (
     2,

time: 115 us -> 111 us (0.965)
  Pallas kernels: 34.5 us -> 30 us
    pallas_call x9, Pallas kernels: 34.5 us -> 30 us  [call(): pl.pallas_call(kernel, out_shape=out_shape, cost_estimate=pl.CostEstimate...]
where the time goes in v4:
time: 111 us; the launch traced here: 110 us
  blocking collectives  53.2 us (48%)
  Pallas kernels  30 us (27%)
  starting transfers between devices  24.8 us (22%)
  waiting for transfers between devices  1.25 us (1%)
    all_to_all x4, blocking collectives, swap(): lax.all_to_all(parts, ('box', 'depth'), 0, 0, axis_index_groups=groups, t...  53.2 us
    pallas_call x9, Pallas kernels, call(): pl.pallas_call(kernel, out_shape=out_shape, cost_estimate=pl.CostEstimate...  30 us
    all_to_all x2, starting transfers between devices, swap(): lax.all_to_all(parts, ('box', 'depth'), 0, 0, axis_index_groups=groups, t...  16.5 us
    ppermute x2, starting transfers between devices, exchange(): lax.ppermute(to_mate, axis, mates)  4.16 us
    ppermute x2, starting transfers between devices, exchange(): lax.ppermute(to_next, axis, others)  4.12 us
  transfers between devices with their start and end apart: 6, of which 2 were waited for; matrix products, arithmetic and copies ran while one was open for 0% of the time, Pallas kernels for 7%

profile of v4, /device:TPU:1, one launch (start us, length us, event | category | flops | bytes accessed | tf_op | source)
XLA Modules:
  0.0 110.3 jit_solution(7976462282602499747)
XLA Ops:
  0.6 0.0 copy-start.4
  0.7 6.4 %shard_map.58 = (f32[8,24,384]{2,1,0:T(8,128)}, f32[8,24,384]{2,1,0:T(8,128)}, f32[8,8,384]{2,1,0:T(8,128)}, f32[8,8,384]{2,1,0:T(8,128)}, f32[32,8,128]{2,1,0:T(8,128)}) custom-call(f32[5,8,8,384]{3,2,1,0:T(8,128)} %state.3, f32[3,8,8,384]{3,2,1,0:T(8,128)} %velocity.5, s32[8,8,384]{2,1,0:T(8,128)} %bins.1), custom_call_target="tpu_custom_call" | custom-call | flops 7000000000 | tf_op jit(solution)/shard_map/pallas_call | solution.py:550
  7.0 2.6 %collective-permute-start = (f32[8,24,384]{2,1,0:T(8,128)}, f32[8,24,384]{2,1,0:T(8,128)S(1)}, u32[]{:S(2)}, u32[]{:S(2)}) collective-permute-start(f32[8,24,384]{2,1,0:T(8,128)} %get-tuple-element.28), channel_id=1, source_target_pairs={{0,8},{8,0},{16,24},{24,16},{32,40},{40,32},{48,56},{56,48},{64,72... | collective-permute-start | bytes 884744 | tf_op jit(solution)/shard_map/ppermute | solution.py:564
  9.6 0.7 collective-permute-start.1
  10.3 0.0 copy-start.9
  10.3 12.8 %all-to-all-start = ((f32[16,2,8,128]{3,2,1,0:T(8,128)}), f32[16,2,8,128]{3,2,1,0:T(8,128)S(1)}, u32[]{:S(2)}, u32[]{:S(2)}) async-start(f32[16,2,8,128]{3,2,1,0:T(8,128)} %bitcast.7), calls=%async_computation | async-start | bytes 262144 | tf_op jit(solution)/shard_map/all_to_all | solution.py:605
  23.1 0.0 collective-permute-done.1.ynext
  23.2 1.2 %shard_map.61 = (f32[34,8,384]{2,1,0:T(8,128)S(1)}, f32[34,8,384]{2,1,0:T(8,128)S(1)}) custom-call(f32[5,8,8,384]{3,2,1,0:T(8,128)S(1)} %copy-done.1, f32[3,8,8,384]{3,2,1,0:T(8,128)S(1)} %copy-done.4, f32[8,8,384]{2,1,0:T(8,128)S(1)} %copy-done.9, f32[8,8,384]{2,1,0:T(8,128)S(1)} %copy-done.8, f32[8,24,384]{2,1,0:T(8,128)S(1)} %collective-permute-done.ymate, ...), custom_call_target="tpu_custom_call" | custom-call | flops 2000000000 | tf_op jit(solution)/shard_map/pallas_call | solution.py:550
  24.4 1.6 %collective-permute-start.2 = (f32[34,8,384]{2,1,0:T(8,128)S(1)}, f32[34,8,384]{2,1,0:T(8,128)S(1)}, u32[]{:S(2)}, u32[]{:S(2)}) collective-permute-start(f32[34,8,384]{2,1,0:T(8,128)S(1)} %get-tuple-element.32), channel_id=1, source_target_pairs={{0,1},{1,0},{2,3},{3,2},{4,5},{5,4},{6,7},{7,6},{8,9},{9,8},{10,11... | collective-permute-start | bytes 1253384 | tf_op jit(solution)/shard_map/ppermute | solution.py:564
  26.0 3.4 %collective-permute-start.3 = (f32[34,8,384]{2,1,0:T(8,128)S(1)}, f32[34,8,384]{2,1,0:T(8,128)S(1)}, u32[]{:S(2)}, u32[]{:S(2)}) collective-permute-start(f32[34,8,384]{2,1,0:T(8,128)S(1)} %get-tuple-element.33), channel_id=1, source_target_pairs={{1,2},{2,1},{3,4},{4,3},{5,6},{6,5},{9,10},{10,9},{11,12},{12,11},... | collective-permute-start | bytes 1253384 | tf_op jit(solution)/shard_map/ppermute | solution.py:564
  29.4 0.5 all-to-all-done.tiles
  29.9 0.6 shard_map.59
  30.5 14.8 %all_to_all.30.tiles = f32[16,2,8,128]{3,2,1,0:T(8,128)S(1)} all-to-all(f32[16,2,8,128]{3,2,1,0:T(8,128)S(1)} %get-tuple-element.26), channel_id=1, replica_groups={{0,1,8,9,16,17,24,25,32,33,40,41,48,49,56,57},{2,3,10,11,18,19,26,27,34..., dimensions={0} | all-to-all | bytes 262144 | tf_op jit(solution)/shard_map/all_to_all | solution.py:605
  45.4 0.0 copy-start.7
  45.4 12.7 %all_to_all.31 = f32[16,2,8,128]{3,2,1,0:T(8,128)S(1)} all-to-all(f32[16,2,8,128]{3,2,1,0:T(8,128)S(1)} %get-tuple-element.27), channel_id=1, replica_groups={{0,2,4,6,64,66,68,70,128,130,132,134,192,194,196,198},{1,3,5,7,65,67,69..., dimensions={0} | all-to-all | bytes 262144 | tf_op jit(solution)/shard_map/all_to_all | solution.py:605
  58.2 10.4 %shard_map.62 = (f32[5,8,8,384]{3,2,1,0:T(8,128)}, f32[10,24,384]{2,1,0:T(8,128)}, f32[32,8,128]{2,1,0:T(8,128)}) custom-call(f32[32,8,128]{2,1,0:T(8,128)S(1)} %bitcast.4, f32[5,8,8,384]{3,2,1,0:T(8,128)S(1)} %copy-done.1, f32[3,8,8,384]{3,2,1,0:T(8,128)S(1)} %copy-done.4, s32[8,8,384]{2,1,0:T(8,128)S(1)} %copy-done.7, ...), custom_call_target="tpu_custom_call" | custom-call | flops 14000000000 | tf_op jit(solution)/shard_map/pallas_call | solution.py:550
  68.6 3.7 %all-to-all-start.3 = ((f32[16,2,8,128]{3,2,1,0:T(8,128)}), f32[16,2,8,128]{3,2,1,0:T(8,128)S(1)}, u32[]{:S(2)}, u32[]{:S(2)}) async-start(f32[16,2,8,128]{3,2,1,0:T(8,128)} %bitcast.2), calls=%async_computation.3 | async-start | bytes 262144 | tf_op jit(solution)/shard_map/all_to_all | solution.py:605
  72.3 5.9 %shard_map.64 = (f32[14,24,384]{2,1,0:T(8,128)}, f32[16,24,384]{2,1,0:T(8,128)}) custom-call(f32[32,8,128]{2,1,0:T(8,128)} %bitcast.5, f32[10,24,384]{2,1,0:T(8,128)} %get-tuple-element.37.near_p, f32[8,8,384]{2,1,0:T(8,128)} %get-tuple-element.31.shifted, f32[3,8,8,384]{3,2,1,0:T(8,128)} %velocity.5, f32[8,24,384]{2,1,0:T(8,128)} %copy-done.5, ...), custom_call_target="tpu_custom_call" | custom-call | flops 8000000000 | tf_op jit(solution)/shard_map/pallas_call | solution.py:550
  78.2 0.7 all-to-all-done.3.tiles
  78.9 0.6 shard_map.63
  79.5 13.6 %all_to_all.32.tiles = f32[16,2,8,128]{3,2,1,0:T(8,128)S(1)} all-to-all(f32[16,2,8,128]{3,2,1,0:T(8,128)S(1)} %get-tuple-element.40), channel_id=1, replica_groups={{0,1,8,9,16,17,24,25,32,33,40,41,48,49,56,57},{2,3,10,11,18,19,26,27,34..., dimensions={0} | all-to-all | bytes 262144 | tf_op jit(solution)/shard_map/all_to_all | solution.py:605
  93.1 0.6 shard_map.65
  93.8 12.1 %all_to_all.33 = f32[16,2,8,128]{3,2,1,0:T(8,128)} all-to-all(f32[16,2,8,128]{3,2,1,0:T(8,128)S(1)} %get-tuple-element.42), channel_id=1, replica_groups={{0,2,4,6,64,66,68,70,128,130,132,134,192,194,196,198},{1,3,5,7,65,67,69..., dimensions={0} | all-to-all | bytes 262144 | tf_op jit(solution)/shard_map/all_to_all | solution.py:605
  105.9 4.3 %shard_map.66 = (f32[8,8,384]{2,1,0:T(8,128)}, f32[5,4096]{1,0:T(8,128)}) custom-call(f32[32,8,128]{2,1,0:T(8,128)} %bitcast.8, f32[32,8,128]{2,1,0:T(8,128)} %bitcast.6, f32[14,24,384]{2,1,0:T(8,128)} %get-tuple-element.43.q_in, f32[16,24,384]{2,1,0:T(8,128)} %get-tuple-element.44.bins_in), custom_call_target="tpu_custom_call" | custom-call | flops 8999999488 | tf_op jit(solution)/shard_map/pallas_call | solution.py:550
  (21 shorter events, 0.1 us)
Async XLA Ops:
  0.6 22.5 %copy-start.4 = (f32[3,8,8,384]{3,2,1,0:T(8,128)S(1)}, f32[3,8,8,384]{3,2,1,0:T(8,128)}, u32[]{:S(2)}) copy-start(f32[3,8,8,384]{3,2,1,0:T(8,128)} %velocity.5) | copy-start | bytes 884740
  0.6 22.5 %copy-start.1 = (f32[5,8,8,384]{3,2,1,0:T(8,128)S(1)}, f32[5,8,8,384]{3,2,1,0:T(8,128)}, u32[]{:S(2)}) copy-start(f32[5,8,8,384]{3,2,1,0:T(8,128)} %state.3) | copy-start | bytes 1474564
  7.0 16.1 %collective-permute-start = (f32[8,24,384]{2,1,0:T(8,128)}, f32[8,24,384]{2,1,0:T(8,128)S(1)}, u32[]{:S(2)}, u32[]{:S(2)}) collective-permute-start(f32[8,24,384]{2,1,0:T(8,128)} %get-tuple-element.28), channel_id=1, source_target_pairs={{0,8},{8,0},{16,24},{24,16},{32,40},{40,32},{48,56},{56,48},{64,72... | collective-permute-start | bytes 884744 | tf_op jit(solution)/shard_map/ppermute | solution.py:564
  9.6 13.5 %collective-permute-start.1 = (f32[8,24,384]{2,1,0:T(8,128)}, f32[8,24,384]{2,1,0:T(8,128)S(1)}, u32[]{:S(2)}, u32[]{:S(2)}) collective-permute-start(f32[8,24,384]{2,1,0:T(8,128)} %get-tuple-element.29), channel_id=1, source_target_pairs={{8,16},{16,8},{24,32},{32,24},{40,48},{48,40},{56,64},{64,56},{72,... | collective-permute-start | bytes 884744 | tf_op jit(solution)/shard_map/ppermute | solution.py:564
  10.3 12.9 %copy-start.8 = (f32[8,8,384]{2,1,0:T(8,128)S(1)}, f32[8,8,384]{2,1,0:T(8,128)}, u32[]{:S(2)}) copy-start(f32[8,8,384]{2,1,0:T(8,128)} %get-tuple-element.31.shifted) | copy-start | bytes 294916
  10.3 12.9 %copy-start.9 = (f32[8,8,384]{2,1,0:T(8,128)S(1)}, f32[8,8,384]{2,1,0:T(8,128)}, u32[]{:S(2)}) copy-start(f32[8,8,384]{2,1,0:T(8,128)} %get-tuple-element.30.weighted) | copy-start | bytes 294916
  10.3 19.6 %all-to-all-start = ((f32[16,2,8,128]{3,2,1,0:T(8,128)}), f32[16,2,8,128]{3,2,1,0:T(8,128)S(1)}, u32[]{:S(2)}, u32[]{:S(2)}) async-start(f32[16,2,8,128]{3,2,1,0:T(8,128)} %bitcast.7), calls=%async_computation | async-start | bytes 262144 | tf_op jit(solution)/shard_map/all_to_all | solution.py:605
  23.1 35.0 %copy-start.5 = (f32[8,24,384]{2,1,0:T(8,128)}, f32[8,24,384]{2,1,0:T(8,128)S(1)}, u32[]{:S(2)}) copy-start(f32[8,24,384]{2,1,0:T(8,128)S(1)} %collective-permute-done.ymate) | copy-start | bytes 884740
  23.1 35.0 %copy-start.6 = (f32[8,24,384]{2,1,0:T(8,128)}, f32[8,24,384]{2,1,0:T(8,128)S(1)}, u32[]{:S(2)}) copy-start(f32[8,24,384]{2,1,0:T(8,128)S(1)} %collective-permute-done.1.ynext) | copy-start | bytes 884740
  24.4 33.8 %collective-permute-start.2 = (f32[34,8,384]{2,1,0:T(8,128)S(1)}, f32[34,8,384]{2,1,0:T(8,128)S(1)}, u32[]{:S(2)}, u32[]{:S(2)}) collective-permute-start(f32[34,8,384]{2,1,0:T(8,128)S(1)} %get-tuple-element.32), channel_id=1, source_target_pairs={{0,1},{1,0},{2,3},{3,2},{4,5},{5,4},{6,7},{7,6},{8,9},{9,8},{10,11... | collective-permute-start | bytes 1253384 | tf_op jit(solution)/shard_map/ppermute | solution.py:564
  26.0 32.2 %collective-permute-start.3 = (f32[34,8,384]{2,1,0:T(8,128)S(1)}, f32[34,8,384]{2,1,0:T(8,128)S(1)}, u32[]{:S(2)}, u32[]{:S(2)}) collective-permute-start(f32[34,8,384]{2,1,0:T(8,128)S(1)} %get-tuple-element.33), channel_id=1, source_target_pairs={{1,2},{2,1},{3,4},{4,3},{5,6},{6,5},{9,10},{10,9},{11,12},{12,11},... | collective-permute-start | bytes 1253384 | tf_op jit(solution)/shard_map/ppermute | solution.py:564
  45.4 12.8 %copy-start.7 = (s32[8,8,384]{2,1,0:T(8,128)S(1)}, s32[8,8,384]{2,1,0:T(8,128)}, u32[]{:S(2)}) copy-start(s32[8,8,384]{2,1,0:T(8,128)} %bins.1) | copy-start | bytes 294916
  58.1 10.4 %copy-start = (f32[16,2,8,128]{3,2,1,0:T(8,128)}, f32[16,2,8,128]{3,2,1,0:T(8,128)S(1)}, u32[]{:S(2)}) copy-start(f32[16,2,8,128]{3,2,1,0:T(8,128)S(1)} %all_to_all.31) | copy-start | bytes 393220
  58.1 10.4 %copy-start.2 = (f32[34,8,384]{2,1,0:T(8,128)}, f32[34,8,384]{2,1,0:T(8,128)S(1)}, u32[]{:S(2)}) copy-start(f32[34,8,384]{2,1,0:T(8,128)S(1)} %collective-permute-done.2.xmate) | copy-start | bytes 1253380
  58.1 10.4 %copy-start.3 = (f32[34,8,384]{2,1,0:T(8,128)}, f32[34,8,384]{2,1,0:T(8,128)S(1)}, u32[]{:S(2)}) copy-start(f32[34,8,384]{2,1,0:T(8,128)S(1)} %collective-permute-done.3.xnext) | copy-start | bytes 1253380
  68.6 10.3 %all-to-all-start.3 = ((f32[16,2,8,128]{3,2,1,0:T(8,128)}), f32[16,2,8,128]{3,2,1,0:T(8,128)S(1)}, u32[]{:S(2)}, u32[]{:S(2)}) async-start(f32[16,2,8,128]{3,2,1,0:T(8,128)} %bitcast.2), calls=%async_computation.3 | async-start | bytes 262144 | tf_op jit(solution)/shard_map/all_to_all | solution.py:605

commit v5 on v4

--- a/solution.py
+++ b/solution.py
@@ -488,6 +488,8 @@
             copy.start()
     for copy in tables:
         copy.wait()
+    for t in range(TILES):
+        second[t] = second[t] / jnp.maximum(first[t, 5:6, :], 1.0)
     flat[...] = weighted_rows(second)
     tab = row_table(flat[...], 2)
     for t in range(TILES):
@@ -566,30 +568,23 @@
 
 def added(tiles):
     total, top = tiles[0], tiles[0]
-    for i in range(1, MEMBERS):
+    for i in range(1, tiles.shape[0]):
         total, top = total + tiles[i], jnp.maximum(top, tiles[i])
-    return jnp.where(lax.broadcasted_iota(jnp.int32, total.shape, 1) == 6, top, total)
-
-
-def merge_kernel(tiles, share, copies):
+    return jnp.where(lax.broadcasted_iota(jnp.int32, total.shape, total.ndim - 2) == 6, top, total)
+
+
+def merge_kernel(tiles, copies):
     total = added(tiles)
-    share[...] = total
-    for i in range(MEMBERS):
+    for i in range(copies.shape[0]):
         copies[i] = total
 
 
-def divide_kernel(tiles, counts, share, copies):
+def divide_kernel(tiles, copies):
     total = added(tiles)
-    cells = total if counts is None else counts
     row = lax.broadcasted_iota(jnp.int32, total.shape, 1)
-    mean = jnp.where(row < NF, total / jnp.maximum(cells[:, 5:6, :], 1.0), total)
-    share[...] = total
+    mean = jnp.where(row < NF, total / jnp.maximum(total[:, 5:6, :], 1.0), total)
     for i in range(MEMBERS):
         copies[i] = mean
-
-
-def divide_own_kernel(tiles, share, copies):
-    divide_kernel(tiles, None, share, copies)
 
 
 def groups_of(varied):
@@ -601,6 +596,8 @@
 
 SHARE_GROUPS = groups_of((0, 2))
 OTHER_GROUPS = groups_of((1, 3))
+LAYER_GROUPS = groups_of((0, 2, 3))
+COLUMN_GROUPS = groups_of((1,))
 def swap(parts, groups):
     return lax.all_to_all(parts, ("box", "depth"), 0, 0, axis_index_groups=groups, tiled=True)
 
@@ -659,7 +656,9 @@
 )
 
 
-MERGE = (0, (f32_like(2, 8, 128), f32_like(MEMBERS, 2, 8, 128)), [], dict(megabytes=20))
+MERGE = (0, f32_like(MEMBERS, 2, 8, 128), [], dict(megabytes=20))
+COLUMN = (0, f32_like(8, 8, 128), [], dict(megabytes=20))
+LAYER = (0, f32_like(TILES, 8, 128), [], dict(megabytes=20))
 
 
 def per_device(state, velocity, bins):
@@ -667,15 +666,15 @@
     ymate, ynext = exchange(to_mate, to_next, "box")
     to_mate, to_next = call(pack_x_kernel, PACK_X, state, velocity, weighted, shifted, ymate, ynext)
     xmate, xnext = exchange(to_mate, to_next, "depth")
-    share, copies = call(merge_kernel, MERGE, swap(in_members(tiles), SHARE_GROUPS))
-    share, copies = call(divide_own_kernel, MERGE, swap(copies, OTHER_GROUPS))
+    copies = call(merge_kernel, MERGE, swap(in_members(tiles), SHARE_GROUPS))
+    copies = call(divide_kernel, MERGE, swap(copies, OTHER_GROUPS))
     first = swap(copies, SHARE_GROUPS).reshape(TILES, 8, 128)
     new_state, near_p, tiles = call(step_kernel, STEP, first, state, velocity, bins, ymate, ynext, xmate, xnext)
     q, wide_bins = call(ring_kernel, RING, first, near_p, shifted, velocity, ymate, ynext, xmate, xnext)
-    part, copies = call(merge_kernel, MERGE, swap(in_members(tiles), SHARE_GROUPS))
+    copies = call(merge_kernel, COLUMN, swap(tiles, LAYER_GROUPS))
     copies, q, wide_bins = lax.optimization_barrier((copies, q, wide_bins))
-    part, copies = call(divide_kernel, MERGE, swap(copies, OTHER_GROUPS), share)
-    second = swap(copies, SHARE_GROUPS).reshape(TILES, 8, 128)
+    copies = call(merge_kernel, LAYER, swap(copies, COLUMN_GROUPS))
+    second = swap(copies, LAYER_GROUPS)
     potential, profile = call(relax_kernel, RELAX, second, first, q, wide_bins)
     return (new_state, potential, profile)
 

time: 111 us -> 109 us (0.982)
  blocking collectives: 53.2 us -> 51.2 us
  Pallas kernels: 30 us -> 28.2 us
    all_to_all x4, blocking collectives: 53.2 us -> 51.2 us  [swap(): lax.all_to_all(parts, ('box', 'depth'), 0, 0, axis_index_groups=groups, t...]
    pallas_call x9, Pallas kernels: 30 us -> 28.2 us  [call(): pl.pallas_call(kernel, out_shape=out_shape, cost_estimate=pl.CostEstimate...]
    all_to_all x2, waiting for transfers between devices: 1.24 us -> 2.35 us  [swap(): lax.all_to_all(parts, ('box', 'depth'), 0, 0, axis_index_groups=groups, t...]
where the time goes in v5:
time: 109 us; the launch traced here: 108 us
  blocking collectives  51.2 us (47%)
  Pallas kernels  28.2 us (26%)
  starting transfers between devices  25.4 us (23%)
  waiting for transfers between devices  2.36 us (2%)
    all_to_all x4, blocking collectives, swap(): lax.all_to_all(parts, ('box', 'depth'), 0, 0, axis_index_groups=groups, t...  51.2 us
    pallas_call x9, Pallas kernels, call(): pl.pallas_call(kernel, out_shape=out_shape, cost_estimate=pl.CostEstimate...  28.2 us
    all_to_all x2, starting transfers between devices, swap(): lax.all_to_all(parts, ('box', 'depth'), 0, 0, axis_index_groups=groups, t...  17.2 us
    ppermute x2, starting transfers between devices, exchange(): lax.ppermute(to_mate, axis, mates)  4.16 us
    ppermute x2, starting transfers between devices, exchange(): lax.ppermute(to_next, axis, others)  4.12 us
    all_to_all x2, waiting for transfers between devices, swap(): lax.all_to_all(parts, ('box', 'depth'), 0, 0, axis_index_groups=groups, t...  2.35 us
  transfers between devices with their start and end apart: 6, of which 2 were waited for; matrix products, arithmetic and copies ran while one was open for 0% of the time, Pallas kernels for 7%

profile of v5, /device:TPU:1, one launch (start us, length us, event | category | flops | bytes accessed | tf_op | source)
XLA Modules:
  0.0 108.3 jit_solution(3151029116057647817)
XLA Ops:
  0.6 0.0 copy-start.4
  0.7 6.4 %shard_map.58 = (f32[8,24,384]{2,1,0:T(8,128)}, f32[8,24,384]{2,1,0:T(8,128)}, f32[8,8,384]{2,1,0:T(8,128)}, f32[8,8,384]{2,1,0:T(8,128)}, f32[32,8,128]{2,1,0:T(8,128)}) custom-call(f32[5,8,8,384]{3,2,1,0:T(8,128)} %state.3, f32[3,8,8,384]{3,2,1,0:T(8,128)} %velocity.5, s32[8,8,384]{2,1,0:T(8,128)} %bins.1), custom_call_target="tpu_custom_call" | custom-call | flops 7000000000 | tf_op jit(solution)/shard_map/pallas_call | solution.py:552
  7.0 2.6 %collective-permute-start = (f32[8,24,384]{2,1,0:T(8,128)}, f32[8,24,384]{2,1,0:T(8,128)S(1)}, u32[]{:S(2)}, u32[]{:S(2)}) collective-permute-start(f32[8,24,384]{2,1,0:T(8,128)} %get-tuple-element.21), channel_id=1, source_target_pairs={{0,8},{8,0},{16,24},{24,16},{32,40},{40,32},{48,56},{56,48},{64,72... | collective-permute-start | bytes 884744 | tf_op jit(solution)/shard_map/ppermute | solution.py:566
  9.6 0.7 collective-permute-start.1
  10.3 0.0 copy-start.9
  10.3 12.8 %all-to-all-start = ((f32[16,2,8,128]{3,2,1,0:T(8,128)}), f32[16,2,8,128]{3,2,1,0:T(8,128)S(1)}, u32[]{:S(2)}, u32[]{:S(2)}) async-start(f32[16,2,8,128]{3,2,1,0:T(8,128)} %bitcast.5), calls=%async_computation | async-start | bytes 262144 | tf_op jit(solution)/shard_map/all_to_all | solution.py:602
  23.1 0.0 collective-permute-done.ymate
  23.1 0.0 collective-permute-done.1.ynext
  23.2 1.2 %shard_map.61 = (f32[34,8,384]{2,1,0:T(8,128)S(1)}, f32[34,8,384]{2,1,0:T(8,128)S(1)}) custom-call(f32[5,8,8,384]{3,2,1,0:T(8,128)S(1)} %copy-done.1, f32[3,8,8,384]{3,2,1,0:T(8,128)S(1)} %copy-done.4, f32[8,8,384]{2,1,0:T(8,128)S(1)} %copy-done.9, f32[8,8,384]{2,1,0:T(8,128)S(1)} %copy-done.8, f32[8,24,384]{2,1,0:T(8,128)S(1)} %collective-permute-done.ymate, ...), custom_call_target="tpu_custom_call" | custom-call | flops 2000000000 | tf_op jit(solution)/shard_map/pallas_call | solution.py:552
  24.4 1.6 %collective-permute-start.2 = (f32[34,8,384]{2,1,0:T(8,128)S(1)}, f32[34,8,384]{2,1,0:T(8,128)S(1)}, u32[]{:S(2)}, u32[]{:S(2)}) collective-permute-start(f32[34,8,384]{2,1,0:T(8,128)S(1)} %get-tuple-element.25), channel_id=1, source_target_pairs={{0,1},{1,0},{2,3},{3,2},{4,5},{5,4},{6,7},{7,6},{8,9},{9,8},{10,11... | collective-permute-start | bytes 1253384 | tf_op jit(solution)/shard_map/ppermute | solution.py:566
  26.0 3.4 %collective-permute-start.3 = (f32[34,8,384]{2,1,0:T(8,128)S(1)}, f32[34,8,384]{2,1,0:T(8,128)S(1)}, u32[]{:S(2)}, u32[]{:S(2)}) collective-permute-start(f32[34,8,384]{2,1,0:T(8,128)S(1)} %get-tuple-element.26), channel_id=1, source_target_pairs={{1,2},{2,1},{3,4},{4,3},{5,6},{6,5},{9,10},{10,9},{11,12},{12,11},... | collective-permute-start | bytes 1253384 | tf_op jit(solution)/shard_map/ppermute | solution.py:566
  29.4 0.5 all-to-all-done.tiles
  29.9 14.8 %all_to_all.30.tiles = f32[16,2,8,128]{3,2,1,0:T(8,128)S(1)} all-to-all(f32[16,2,8,128]{3,2,1,0:T(8,128)S(1)} %shard_map.59), channel_id=1, replica_groups={{0,1,8,9,16,17,24,25,32,33,40,41,48,49,56,57},{2,3,10,11,18,19,26,27,34..., dimensions={0} | all-to-all | bytes 262144 | tf_op jit(solution)/shard_map/all_to_all | solution.py:602
  44.8 0.0 copy-start.7
  44.8 12.7 %all_to_all.31 = f32[16,2,8,128]{3,2,1,0:T(8,128)S(1)} all-to-all(f32[16,2,8,128]{3,2,1,0:T(8,128)S(1)} %shard_map.60), channel_id=1, replica_groups={{0,2,4,6,64,66,68,70,128,130,132,134,192,194,196,198},{1,3,5,7,65,67,69..., dimensions={0} | all-to-all | bytes 262144 | tf_op jit(solution)/shard_map/all_to_all | solution.py:602
  57.5 0.0 collective-permute-done.2.xmate
  57.5 0.0 collective-permute-done.3.xnext
  57.6 10.4 %shard_map.62 = (f32[5,8,8,384]{3,2,1,0:T(8,128)}, f32[10,24,384]{2,1,0:T(8,128)}, f32[32,8,128]{2,1,0:T(8,128)}) custom-call(f32[32,8,128]{2,1,0:T(8,128)S(1)} %bitcast.2, f32[5,8,8,384]{3,2,1,0:T(8,128)S(1)} %copy-done.1, f32[3,8,8,384]{3,2,1,0:T(8,128)S(1)} %copy-done.4, s32[8,8,384]{2,1,0:T(8,128)S(1)} %copy-done.7, ...), custom_call_target="tpu_custom_call" | custom-call | flops 14000000000 | tf_op jit(solution)/shard_map/pallas_call | solution.py:552
  68.0 4.4 %all-to-all-start.3 = ((f32[32,8,128]{2,1,0:T(8,128)}), f32[32,8,128]{2,1,0:T(8,128)S(1)}, u32[]{:S(2)}, u32[]{:S(2)}) async-start(f32[32,8,128]{2,1,0:T(8,128)} %get-tuple-element.28), calls=%async_computation.3 | async-start | bytes 262144 | tf_op jit(solution)/shard_map/all_to_all | solution.py:602
  72.4 5.9 %shard_map.64 = (f32[14,24,384]{2,1,0:T(8,128)}, f32[16,24,384]{2,1,0:T(8,128)}) custom-call(f32[32,8,128]{2,1,0:T(8,128)} %bitcast.3, f32[10,24,384]{2,1,0:T(8,128)} %get-tuple-element.29.near_p, f32[8,8,384]{2,1,0:T(8,128)} %get-tuple-element.24.shifted, f32[3,8,8,384]{3,2,1,0:T(8,128)} %velocity.5, f32[8,24,384]{2,1,0:T(8,128)} %copy-done.5, ...), custom_call_target="tpu_custom_call" | custom-call | flops 8000000000 | tf_op jit(solution)/shard_map/pallas_call | solution.py:552
  78.3 1.9 %all-to-all-done.3.tiles = f32[32,8,128]{2,1,0:T(8,128)S(1)} async-done(((f32[32,8,128]{2,1,0:T(8,128)}), f32[32,8,128]{2,1,0:T(8,128)S(1)}, u32[]{:S(2)}, u32[]{:S(2)}) %all-to-all-start.3) | async-done | bytes 131104 | tf_op jit(solution)/shard_map/all_to_all | solution.py:602
  80.1 9.2 %all_to_all.32.tiles = f32[8,8,128]{2,1,0:T(8,128)S(1)} all-to-all(f32[8,8,128]{2,1,0:T(8,128)S(1)} %shard_map.63), channel_id=1, replica_groups={{0,8,16,24,32,40,48,56},{1,9,17,25,33,41,49,57},{2,10,18,26,34,42,50,58..., dimensions={0} | all-to-all | bytes 65536 | tf_op jit(solution)/shard_map/all_to_all | solution.py:602
  89.4 14.4 %all_to_all.33.second_in = f32[32,8,128]{2,1,0:T(8,128)} all-to-all(f32[32,8,128]{2,1,0:T(8,128)S(1)} %shard_map.65), channel_id=1, replica_groups={{0,1,2,3,4,5,6,7,64,65,66,67,68,69,70,71,128,129,130,131,132,133,134,13..., dimensions={0} | all-to-all | bytes 262144 | tf_op jit(solution)/shard_map/all_to_all | solution.py:602
  103.8 4.3 %shard_map.66 = (f32[8,8,384]{2,1,0:T(8,128)}, f32[5,4096]{1,0:T(8,128)}) custom-call(f32[32,8,128]{2,1,0:T(8,128)} %all_to_all.33.second_in, f32[32,8,128]{2,1,0:T(8,128)} %bitcast.4, f32[14,24,384]{2,1,0:T(8,128)} %get-tuple-element.33.q_in, f32[16,24,384]{2,1,0:T(8,128)} %get-tuple-element.34.bins_in), custom_call_target="tpu_custom_call" | custom-call | flops 8999999488 | tf_op jit(solution)/shard_map/pallas_call | solution.py:552
  (21 shorter events, 0.1 us)
Async XLA Ops:
  0.6 22.5 %copy-start.1 = (f32[5,8,8,384]{3,2,1,0:T(8,128)S(1)}, f32[5,8,8,384]{3,2,1,0:T(8,128)}, u32[]{:S(2)}) copy-start(f32[5,8,8,384]{3,2,1,0:T(8,128)} %state.3) | copy-start | bytes 1474564
  0.6 22.5 %copy-start.4 = (f32[3,8,8,384]{3,2,1,0:T(8,128)S(1)}, f32[3,8,8,384]{3,2,1,0:T(8,128)}, u32[]{:S(2)}) copy-start(f32[3,8,8,384]{3,2,1,0:T(8,128)} %velocity.5) | copy-start | bytes 884740
  7.0 16.1 %collective-permute-start = (f32[8,24,384]{2,1,0:T(8,128)}, f32[8,24,384]{2,1,0:T(8,128)S(1)}, u32[]{:S(2)}, u32[]{:S(2)}) collective-permute-start(f32[8,24,384]{2,1,0:T(8,128)} %get-tuple-element.21), channel_id=1, source_target_pairs={{0,8},{8,0},{16,24},{24,16},{32,40},{40,32},{48,56},{56,48},{64,72... | collective-permute-start | bytes 884744 | tf_op jit(solution)/shard_map/ppermute | solution.py:566
  9.6 13.5 %collective-permute-start.1 = (f32[8,24,384]{2,1,0:T(8,128)}, f32[8,24,384]{2,1,0:T(8,128)S(1)}, u32[]{:S(2)}, u32[]{:S(2)}) collective-permute-start(f32[8,24,384]{2,1,0:T(8,128)} %get-tuple-element.22), channel_id=1, source_target_pairs={{8,16},{16,8},{24,32},{32,24},{40,48},{48,40},{56,64},{64,56},{72,... | collective-permute-start | bytes 884744 | tf_op jit(solution)/shard_map/ppermute | solution.py:566
  10.3 12.9 %copy-start.8 = (f32[8,8,384]{2,1,0:T(8,128)S(1)}, f32[8,8,384]{2,1,0:T(8,128)}, u32[]{:S(2)}) copy-start(f32[8,8,384]{2,1,0:T(8,128)} %get-tuple-element.24.shifted) | copy-start | bytes 294916
  10.3 12.9 %copy-start.9 = (f32[8,8,384]{2,1,0:T(8,128)S(1)}, f32[8,8,384]{2,1,0:T(8,128)}, u32[]{:S(2)}) copy-start(f32[8,8,384]{2,1,0:T(8,128)} %get-tuple-element.23.weighted) | copy-start | bytes 294916
  10.3 19.6 %all-to-all-start = ((f32[16,2,8,128]{3,2,1,0:T(8,128)}), f32[16,2,8,128]{3,2,1,0:T(8,128)S(1)}, u32[]{:S(2)}, u32[]{:S(2)}) async-start(f32[16,2,8,128]{3,2,1,0:T(8,128)} %bitcast.5), calls=%async_computation | async-start | bytes 262144 | tf_op jit(solution)/shard_map/all_to_all | solution.py:602
  23.1 34.5 %copy-start.5 = (f32[8,24,384]{2,1,0:T(8,128)}, f32[8,24,384]{2,1,0:T(8,128)S(1)}, u32[]{:S(2)}) copy-start(f32[8,24,384]{2,1,0:T(8,128)S(1)} %collective-permute-done.ymate) | copy-start | bytes 884740
  23.1 34.5 %copy-start.6 = (f32[8,24,384]{2,1,0:T(8,128)}, f32[8,24,384]{2,1,0:T(8,128)S(1)}, u32[]{:S(2)}) copy-start(f32[8,24,384]{2,1,0:T(8,128)S(1)} %collective-permute-done.1.ynext) | copy-start | bytes 884740
  24.4 33.2 %collective-permute-start.2 = (f32[34,8,384]{2,1,0:T(8,128)S(1)}, f32[34,8,384]{2,1,0:T(8,128)S(1)}, u32[]{:S(2)}, u32[]{:S(2)}) collective-permute-start(f32[34,8,384]{2,1,0:T(8,128)S(1)} %get-tuple-element.25), channel_id=1, source_target_pairs={{0,1},{1,0},{2,3},{3,2},{4,5},{5,4},{6,7},{7,6},{8,9},{9,8},{10,11... | collective-permute-start | bytes 1253384 | tf_op jit(solution)/shard_map/ppermute | solution.py:566
  26.0 31.6 %collective-permute-start.3 = (f32[34,8,384]{2,1,0:T(8,128)S(1)}, f32[34,8,384]{2,1,0:T(8,128)S(1)}, u32[]{:S(2)}, u32[]{:S(2)}) collective-permute-start(f32[34,8,384]{2,1,0:T(8,128)S(1)} %get-tuple-element.26), channel_id=1, source_target_pairs={{1,2},{2,1},{3,4},{4,3},{5,6},{6,5},{9,10},{10,9},{11,12},{12,11},... | collective-permute-start | bytes 1253384 | tf_op jit(solution)/shard_map/ppermute | solution.py:566
  44.8 12.8 %copy-start.7 = (s32[8,8,384]{2,1,0:T(8,128)S(1)}, s32[8,8,384]{2,1,0:T(8,128)}, u32[]{:S(2)}) copy-start(s32[8,8,384]{2,1,0:T(8,128)} %bins.1) | copy-start | bytes 294916
  57.5 10.4 %copy-start = (f32[16,2,8,128]{3,2,1,0:T(8,128)}, f32[16,2,8,128]{3,2,1,0:T(8,128)S(1)}, u32[]{:S(2)}) copy-start(f32[16,2,8,128]{3,2,1,0:T(8,128)S(1)} %all_to_all.31) | copy-start | bytes 393220
  57.5 10.4 %copy-start.2 = (f32[34,8,384]{2,1,0:T(8,128)}, f32[34,8,384]{2,1,0:T(8,128)S(1)}, u32[]{:S(2)}) copy-start(f32[34,8,384]{2,1,0:T(8,128)S(1)} %collective-permute-done.2.xmate) | copy-start | bytes 1253380
  57.5 10.4 %copy-start.3 = (f32[34,8,384]{2,1,0:T(8,128)}, f32[34,8,384]{2,1,0:T(8,128)S(1)}, u32[]{:S(2)}) copy-start(f32[34,8,384]{2,1,0:T(8,128)S(1)} %collective-permute-done.3.xnext) | copy-start | bytes 1253380
  68.0 12.1 %all-to-all-start.3 = ((f32[32,8,128]{2,1,0:T(8,128)}), f32[32,8,128]{2,1,0:T(8,128)S(1)}, u32[]{:S(2)}, u32[]{:S(2)}) async-start(f32[32,8,128]{2,1,0:T(8,128)} %get-tuple-element.28), calls=%async_computation.3 | async-start | bytes 262144 | tf_op jit(solution)/shard_map/all_to_all | solution.py:602

commit v6 on v5

--- a/solution.py
+++ b/solution.py
@@ -205,21 +205,15 @@
     return jnp.concatenate([total, jnp.zeros((3, Z), F32)], axis=0)
 
 
-def lift_five(first, b):
-    index = b.astype(jnp.int32)
-    parts = [[] for f in range(NF)]
-    for j in range(3):
-        cut = index[:, 128 * j : 128 * j + 128]
-        tile, lane = lax.shift_right_arithmetic(cut, 7), cut & 127
-        found = [jnp.zeros((8, 128), F32)] * NF
-        for t in range(TILES):
-            here = tile == t
-            for f in range(NF):
-                row = jnp.broadcast_to(first[t, f : f + 1, :], (8, 128))
-                found[f] = jnp.where(here, jnp.take_along_axis(row, lane, axis=1), found[f])
+def lift_five(first, index):
+    tile, lane = lax.shift_right_arithmetic(index, 7), index & 127
+    found = [jnp.zeros((8, 128), F32)] * NF
+    for t in range(TILES):
+        here = tile == t
         for f in range(NF):
-            parts[f].append(found[f])
-    return [jnp.concatenate(part, axis=1) for part in parts]
+            row = jnp.broadcast_to(first[t, f : f + 1, :], (8, 128))
+            found[f] = jnp.where(here, jnp.take_along_axis(row, lane, axis=1), found[f])
+    return found
 
 
 def step_kernel(
@@ -249,16 +243,22 @@
     face_bins[3] = upper(odd_x, xmate[BN], xnext[BN]) - 1.0
 
     def lift_some(i, carry):
-        for k in range(2):
-            x = 2 * i + k
+        planes = [x for x in (2 * i, 2 * i + 1) if x < X - 1]
+        for x in planes:
             for y in range(Y):
                 eight = lift_row(tab, hi[x, pl.ds(y, 1), :], lo[x, pl.ds(y, 1), :])
                 for j in range(3):
                     lifted[x, j, pl.ds(8 * y, 8), :] = eight[:, 128 * j : 128 * j + 128]
-        for f, value in enumerate(lift_five(first, face_bins[i])):
-            face_lift[i, f] = value
-        for k in range(2):
-            x = 2 * i + k
+        for j in range(3):
+            at = slice(128 * j, 128 * j + 128)
+            for f, value in enumerate(lift_five(first, face_bins[i, :, at].astype(jnp.int32))):
+                face_lift[i, f, :, at] = value
+        if i < 3:
+            for f, value in enumerate(lift_five(first, bins[X - 1, :, 128 * i : 128 * i + 128])):
+                lifted[X - 1, i, pl.ds(f, Y, stride=8), :] = value
+        else:
+            planes.append(X - 1)
+        for x in planes:
             for f in range(NF):
                 p[f, x + 1, pl.ds(8, 8), :] = state[f, x] - get_field(lifted, x, f)
         return carry
@@ -450,6 +450,9 @@
     time_step = COURANT / (1.0 + jnp.max(first[0, 6:7, :]))
     lane = lax.broadcasted_iota(jnp.int32, (TALL, Z), 1)
 
+    q_copies = [
+        pltpu.make_async_copy(q.at[pl.ds(7 * i, 7)], q_out.at[pl.ds(7 * i, 7)], out_sems.at[1 + i]) for i in range(2)
+    ]
     for x in range(14):
         c = p[x + 1]
         sides = (
@@ -461,9 +464,10 @@
         for d, (before, after) in enumerate(sides):
             change += jnp.maximum(v[d, x], 0.0) * (c - before) + jnp.minimum(v[d, x], 0.0) * (after - c)
         q[x] = c - time_step * change
-    q_copy = pltpu.make_async_copy(q, q_out, out_sems.at[1])
-    q_copy.start()
-    q_copy.wait()
+        if x % 7 == 6:
+            q_copies[x // 7].start()
+    for copy in q_copies:
+        copy.wait()
     bins_copy.wait()
 
 
@@ -640,7 +644,7 @@
     (f32_like(14, TALL, Z), f32_like(16, TALL, Z)),
     [
         ((16, TALL, Z), F32), ((14, TALL, Z), F32), ((16, TALL, Z), F32), ((3, 14, TALL, Z), F32), ((4, 12, TALL, Z), F32), ((TILES, 128), F32),
-        pltpu.SemaphoreType.DMA((10,)), pltpu.SemaphoreType.DMA((3, 3)), pltpu.SemaphoreType.DMA((2,)),
+        pltpu.SemaphoreType.DMA((10,)), pltpu.SemaphoreType.DMA((3, 3)), pltpu.SemaphoreType.DMA((3,)),
     ],
     dict(in_specs=[VISIBLE] + [REMOTE] * 7, out_specs=(REMOTE, REMOTE), megabytes=58),
 )

time: 109 us -> 108 us (level)
  no operation moved by 1% of the time
where the time goes in v6:
time: 108 us
  blocking collectives  51.1 us (47%)
  Pallas kernels  27.6 us (26%)
  starting transfers between devices  25.4 us (24%)
  waiting for transfers between devices  2.45 us (2%)
    all_to_all x4, blocking collectives, swap(): lax.all_to_all(parts, ('box', 'depth'), 0, 0, axis_index_groups=groups, t...  51.1 us
    pallas_call x9, Pallas kernels, call(): pl.pallas_call(kernel, out_shape=out_shape, cost_estimate=pl.CostEstimate...  27.6 us
    all_to_all x2, starting transfers between devices, swap(): lax.all_to_all(parts, ('box', 'depth'), 0, 0, axis_index_groups=groups, t...  17.2 us
    ppermute x2, starting transfers between devices, exchange(): lax.ppermute(to_mate, axis, mates)  4.16 us
    ppermute x2, starting transfers between devices, exchange(): lax.ppermute(to_next, axis, others)  4.12 us
    all_to_all x2, waiting for transfers between devices, swap(): lax.all_to_all(parts, ('box', 'depth'), 0, 0, axis_index_groups=groups, t...  2.44 us
  transfers between devices with their start and end apart: 6, of which 2 were waited for; matrix products, arithmetic and copies ran while one was open for 0% of the time, Pallas kernels for 7%

profile of v6, /device:TPU:1, one launch (start us, length us, event | category | flops | bytes accessed | tf_op | source)
XLA Modules:
  0.0 107.7 jit_solution(4075604662577332434)
XLA Ops:
  0.6 0.0 copy-start.4
  0.7 6.4 %shard_map.58 = (f32[8,24,384]{2,1,0:T(8,128)}, f32[8,24,384]{2,1,0:T(8,128)}, f32[8,8,384]{2,1,0:T(8,128)}, f32[8,8,384]{2,1,0:T(8,128)}, f32[32,8,128]{2,1,0:T(8,128)}) custom-call(f32[5,8,8,384]{3,2,1,0:T(8,128)} %state.3, f32[3,8,8,384]{3,2,1,0:T(8,128)} %velocity.5, s32[8,8,384]{2,1,0:T(8,128)} %bins.1), custom_call_target="tpu_custom_call" | custom-call | flops 7000000000 | tf_op jit(solution)/shard_map/pallas_call | solution.py:556
  7.0 2.6 %collective-permute-start = (f32[8,24,384]{2,1,0:T(8,128)}, f32[8,24,384]{2,1,0:T(8,128)S(1)}, u32[]{:S(2)}, u32[]{:S(2)}) collective-permute-start(f32[8,24,384]{2,1,0:T(8,128)} %get-tuple-element.21), channel_id=1, source_target_pairs={{0,8},{8,0},{16,24},{24,16},{32,40},{40,32},{48,56},{56,48},{64,72... | collective-permute-start | bytes 884744 | tf_op jit(solution)/shard_map/ppermute | solution.py:570
  9.6 0.7 collective-permute-start.1
  10.3 0.0 copy-start.9
  10.3 12.8 %all-to-all-start = ((f32[16,2,8,128]{3,2,1,0:T(8,128)}), f32[16,2,8,128]{3,2,1,0:T(8,128)S(1)}, u32[]{:S(2)}, u32[]{:S(2)}) async-start(f32[16,2,8,128]{3,2,1,0:T(8,128)} %bitcast.5), calls=%async_computation | async-start | bytes 262144 | tf_op jit(solution)/shard_map/all_to_all | solution.py:606
  23.1 0.0 collective-permute-done.ymate
  23.1 0.0 collective-permute-done.1.ynext
  23.2 1.2 %shard_map.61 = (f32[34,8,384]{2,1,0:T(8,128)S(1)}, f32[34,8,384]{2,1,0:T(8,128)S(1)}) custom-call(f32[5,8,8,384]{3,2,1,0:T(8,128)S(1)} %copy-done.1, f32[3,8,8,384]{3,2,1,0:T(8,128)S(1)} %copy-done.4, f32[8,8,384]{2,1,0:T(8,128)S(1)} %copy-done.9, f32[8,8,384]{2,1,0:T(8,128)S(1)} %copy-done.8, f32[8,24,384]{2,1,0:T(8,128)S(1)} %collective-permute-done.ymate, ...), custom_call_target="tpu_custom_call" | custom-call | flops 2000000000 | tf_op jit(solution)/shard_map/pallas_call | solution.py:556
  24.4 1.6 %collective-permute-start.2 = (f32[34,8,384]{2,1,0:T(8,128)S(1)}, f32[34,8,384]{2,1,0:T(8,128)S(1)}, u32[]{:S(2)}, u32[]{:S(2)}) collective-permute-start(f32[34,8,384]{2,1,0:T(8,128)S(1)} %get-tuple-element.25), channel_id=1, source_target_pairs={{0,1},{1,0},{2,3},{3,2},{4,5},{5,4},{6,7},{7,6},{8,9},{9,8},{10,11... | collective-permute-start | bytes 1253384 | tf_op jit(solution)/shard_map/ppermute | solution.py:570
  26.0 3.4 %collective-permute-start.3 = (f32[34,8,384]{2,1,0:T(8,128)S(1)}, f32[34,8,384]{2,1,0:T(8,128)S(1)}, u32[]{:S(2)}, u32[]{:S(2)}) collective-permute-start(f32[34,8,384]{2,1,0:T(8,128)S(1)} %get-tuple-element.26), channel_id=1, source_target_pairs={{1,2},{2,1},{3,4},{4,3},{5,6},{6,5},{9,10},{10,9},{11,12},{12,11},... | collective-permute-start | bytes 1253384 | tf_op jit(solution)/shard_map/ppermute | solution.py:570
  29.4 0.5 all-to-all-done.tiles
  29.9 14.8 %all_to_all.30.tiles = f32[16,2,8,128]{3,2,1,0:T(8,128)S(1)} all-to-all(f32[16,2,8,128]{3,2,1,0:T(8,128)S(1)} %shard_map.59), channel_id=1, replica_groups={{0,1,8,9,16,17,24,25,32,33,40,41,48,49,56,57},{2,3,10,11,18,19,26,27,34..., dimensions={0} | all-to-all | bytes 262144 | tf_op jit(solution)/shard_map/all_to_all | solution.py:606
  44.8 0.0 copy-start.7
  44.8 12.7 %all_to_all.31 = f32[16,2,8,128]{3,2,1,0:T(8,128)S(1)} all-to-all(f32[16,2,8,128]{3,2,1,0:T(8,128)S(1)} %shard_map.60), channel_id=1, replica_groups={{0,2,4,6,64,66,68,70,128,130,132,134,192,194,196,198},{1,3,5,7,65,67,69..., dimensions={0} | all-to-all | bytes 262144 | tf_op jit(solution)/shard_map/all_to_all | solution.py:606
  57.5 0.0 collective-permute-done.2.xmate
  57.5 0.0 collective-permute-done.3.xnext
  57.6 9.9 %shard_map.62 = (f32[5,8,8,384]{3,2,1,0:T(8,128)}, f32[10,24,384]{2,1,0:T(8,128)}, f32[32,8,128]{2,1,0:T(8,128)}) custom-call(f32[32,8,128]{2,1,0:T(8,128)S(1)} %bitcast.2, f32[5,8,8,384]{3,2,1,0:T(8,128)S(1)} %copy-done.1, f32[3,8,8,384]{3,2,1,0:T(8,128)S(1)} %copy-done.4, s32[8,8,384]{2,1,0:T(8,128)S(1)} %copy-done.7, ...), custom_call_target="tpu_custom_call" | custom-call | flops 14000000000 | tf_op jit(solution)/shard_map/pallas_call | solution.py:556
  67.5 4.4 %all-to-all-start.3 = ((f32[32,8,128]{2,1,0:T(8,128)}), f32[32,8,128]{2,1,0:T(8,128)S(1)}, u32[]{:S(2)}, u32[]{:S(2)}) async-start(f32[32,8,128]{2,1,0:T(8,128)} %get-tuple-element.28), calls=%async_computation.3 | async-start | bytes 262144 | tf_op jit(solution)/shard_map/all_to_all | solution.py:606
  71.9 5.8 %shard_map.64 = (f32[14,24,384]{2,1,0:T(8,128)}, f32[16,24,384]{2,1,0:T(8,128)}) custom-call(f32[32,8,128]{2,1,0:T(8,128)} %bitcast.3, f32[10,24,384]{2,1,0:T(8,128)} %get-tuple-element.29.near_p, f32[8,8,384]{2,1,0:T(8,128)} %get-tuple-element.24.shifted, f32[3,8,8,384]{3,2,1,0:T(8,128)} %velocity.5, f32[8,24,384]{2,1,0:T(8,128)} %copy-done.5, ...), custom_call_target="tpu_custom_call" | custom-call | flops 8000000000 | tf_op jit(solution)/shard_map/pallas_call | solution.py:556
  77.7 1.9 %all-to-all-done.3.tiles = f32[32,8,128]{2,1,0:T(8,128)S(1)} async-done(((f32[32,8,128]{2,1,0:T(8,128)}), f32[32,8,128]{2,1,0:T(8,128)S(1)}, u32[]{:S(2)}, u32[]{:S(2)}) %all-to-all-start.3) | async-done | bytes 131104 | tf_op jit(solution)/shard_map/all_to_all | solution.py:606
  79.6 9.2 %all_to_all.32.tiles = f32[8,8,128]{2,1,0:T(8,128)S(1)} all-to-all(f32[8,8,128]{2,1,0:T(8,128)S(1)} %shard_map.63), channel_id=1, replica_groups={{0,8,16,24,32,40,48,56},{1,9,17,25,33,41,49,57},{2,10,18,26,34,42,50,58..., dimensions={0} | all-to-all | bytes 65536 | tf_op jit(solution)/shard_map/all_to_all | solution.py:606
  88.9 14.4 %all_to_all.33.second_in = f32[32,8,128]{2,1,0:T(8,128)} all-to-all(f32[32,8,128]{2,1,0:T(8,128)S(1)} %shard_map.65), channel_id=1, replica_groups={{0,1,2,3,4,5,6,7,64,65,66,67,68,69,70,71,128,129,130,131,132,133,134,13..., dimensions={0} | all-to-all | bytes 262144 | tf_op jit(solution)/shard_map/all_to_all | solution.py:606
  103.3 4.3 %shard_map.66 = (f32[8,8,384]{2,1,0:T(8,128)}, f32[5,4096]{1,0:T(8,128)}) custom-call(f32[32,8,128]{2,1,0:T(8,128)} %all_to_all.33.second_in, f32[32,8,128]{2,1,0:T(8,128)} %bitcast.4, f32[14,24,384]{2,1,0:T(8,128)} %get-tuple-element.33.q_in, f32[16,24,384]{2,1,0:T(8,128)} %get-tuple-element.34.bins_in), custom_call_target="tpu_custom_call" | custom-call | flops 8999999488 | tf_op jit(solution)/shard_map/pallas_call | solution.py:556
  (21 shorter events, 0.1 us)
Async XLA Ops:
  0.6 22.5 %copy-start.1 = (f32[5,8,8,384]{3,2,1,0:T(8,128)S(1)}, f32[5,8,8,384]{3,2,1,0:T(8,128)}, u32[]{:S(2)}) copy-start(f32[5,8,8,384]{3,2,1,0:T(8,128)} %state.3) | copy-start | bytes 1474564
  0.6 22.5 %copy-start.4 = (f32[3,8,8,384]{3,2,1,0:T(8,128)S(1)}, f32[3,8,8,384]{3,2,1,0:T(8,128)}, u32[]{:S(2)}) copy-start(f32[3,8,8,384]{3,2,1,0:T(8,128)} %velocity.5) | copy-start | bytes 884740
  7.0 16.1 %collective-permute-start = (f32[8,24,384]{2,1,0:T(8,128)}, f32[8,24,384]{2,1,0:T(8,128)S(1)}, u32[]{:S(2)}, u32[]{:S(2)}) collective-permute-start(f32[8,24,384]{2,1,0:T(8,128)} %get-tuple-element.21), channel_id=1, source_target_pairs={{0,8},{8,0},{16,24},{24,16},{32,40},{40,32},{48,56},{56,48},{64,72... | collective-permute-start | bytes 884744 | tf_op jit(solution)/shard_map/ppermute | solution.py:570
  9.6 13.5 %collective-permute-start.1 = (f32[8,24,384]{2,1,0:T(8,128)}, f32[8,24,384]{2,1,0:T(8,128)S(1)}, u32[]{:S(2)}, u32[]{:S(2)}) collective-permute-start(f32[8,24,384]{2,1,0:T(8,128)} %get-tuple-element.22), channel_id=1, source_target_pairs={{8,16},{16,8},{24,32},{32,24},{40,48},{48,40},{56,64},{64,56},{72,... | collective-permute-start | bytes 884744 | tf_op jit(solution)/shard_map/ppermute | solution.py:570
  10.3 12.9 %copy-start.8 = (f32[8,8,384]{2,1,0:T(8,128)S(1)}, f32[8,8,384]{2,1,0:T(8,128)}, u32[]{:S(2)}) copy-start(f32[8,8,384]{2,1,0:T(8,128)} %get-tuple-element.24.shifted) | copy-start | bytes 294916
  10.3 12.9 %copy-start.9 = (f32[8,8,384]{2,1,0:T(8,128)S(1)}, f32[8,8,384]{2,1,0:T(8,128)}, u32[]{:S(2)}) copy-start(f32[8,8,384]{2,1,0:T(8,128)} %get-tuple-element.23.weighted) | copy-start | bytes 294916
  10.3 19.6 %all-to-all-start = ((f32[16,2,8,128]{3,2,1,0:T(8,128)}), f32[16,2,8,128]{3,2,1,0:T(8,128)S(1)}, u32[]{:S(2)}, u32[]{:S(2)}) async-start(f32[16,2,8,128]{3,2,1,0:T(8,128)} %bitcast.5), calls=%async_computation | async-start | bytes 262144 | tf_op jit(solution)/shard_map/all_to_all | solution.py:606
  23.1 34.5 %copy-start.5 = (f32[8,24,384]{2,1,0:T(8,128)}, f32[8,24,384]{2,1,0:T(8,128)S(1)}, u32[]{:S(2)}) copy-start(f32[8,24,384]{2,1,0:T(8,128)S(1)} %collective-permute-done.ymate) | copy-start | bytes 884740
  23.1 34.5 %copy-start.6 = (f32[8,24,384]{2,1,0:T(8,128)}, f32[8,24,384]{2,1,0:T(8,128)S(1)}, u32[]{:S(2)}) copy-start(f32[8,24,384]{2,1,0:T(8,128)S(1)} %collective-permute-done.1.ynext) | copy-start | bytes 884740
  24.4 33.2 %collective-permute-start.2 = (f32[34,8,384]{2,1,0:T(8,128)S(1)}, f32[34,8,384]{2,1,0:T(8,128)S(1)}, u32[]{:S(2)}, u32[]{:S(2)}) collective-permute-start(f32[34,8,384]{2,1,0:T(8,128)S(1)} %get-tuple-element.25), channel_id=1, source_target_pairs={{0,1},{1,0},{2,3},{3,2},{4,5},{5,4},{6,7},{7,6},{8,9},{9,8},{10,11... | collective-permute-start | bytes 1253384 | tf_op jit(solution)/shard_map/ppermute | solution.py:570
  26.0 31.6 %collective-permute-start.3 = (f32[34,8,384]{2,1,0:T(8,128)S(1)}, f32[34,8,384]{2,1,0:T(8,128)S(1)}, u32[]{:S(2)}, u32[]{:S(2)}) collective-permute-start(f32[34,8,384]{2,1,0:T(8,128)S(1)} %get-tuple-element.26), channel_id=1, source_target_pairs={{1,2},{2,1},{3,4},{4,3},{5,6},{6,5},{9,10},{10,9},{11,12},{12,11},... | collective-permute-start | bytes 1253384 | tf_op jit(solution)/shard_map/ppermute | solution.py:570
  44.8 12.8 %copy-start.7 = (s32[8,8,384]{2,1,0:T(8,128)S(1)}, s32[8,8,384]{2,1,0:T(8,128)}, u32[]{:S(2)}) copy-start(s32[8,8,384]{2,1,0:T(8,128)} %bins.1) | copy-start | bytes 294916
  57.5 9.9 %copy-start = (f32[16,2,8,128]{3,2,1,0:T(8,128)}, f32[16,2,8,128]{3,2,1,0:T(8,128)S(1)}, u32[]{:S(2)}) copy-start(f32[16,2,8,128]{3,2,1,0:T(8,128)S(1)} %all_to_all.31) | copy-start | bytes 393220
  57.5 9.9 %copy-start.2 = (f32[34,8,384]{2,1,0:T(8,128)}, f32[34,8,384]{2,1,0:T(8,128)S(1)}, u32[]{:S(2)}) copy-start(f32[34,8,384]{2,1,0:T(8,128)S(1)} %collective-permute-done.2.xmate) | copy-start | bytes 1253380
  57.5 9.9 %copy-start.3 = (f32[34,8,384]{2,1,0:T(8,128)}, f32[34,8,384]{2,1,0:T(8,128)S(1)}, u32[]{:S(2)}) copy-start(f32[34,8,384]{2,1,0:T(8,128)S(1)} %collective-permute-done.3.xnext) | copy-start | bytes 1253380
  67.5 12.1 %all-to-all-start.3 = ((f32[32,8,128]{2,1,0:T(8,128)}), f32[32,8,128]{2,1,0:T(8,128)S(1)}, u32[]{:S(2)}, u32[]{:S(2)}) async-start(f32[32,8,128]{2,1,0:T(8,128)} %get-tuple-element.28), calls=%async_computation.3 | async-start | bytes 262144 | tf_op jit(solution)/shard_map/all_to_all | solution.py:606
